TPU v7x, 32 devices: a whole 2x2x4 slice. The times are simulated.
32 devices in a mesh: dp: 4 (over y, x), seq: 8 (over z, core).
Axes of the slice: x: 2, y: 2, z: 4, core: 2. Of those that a mesh axis runs over, the one named last changes fastest.
Arguments:
- frames: bfloat16 [8, 1024, 1024], P('dp', 'seq'), may hold values from -6 to 6
- segments: int32 [8, 1024], P('dp', 'seq'), may hold values from 0 to 16, as said below
- cotangent: bfloat16 [8, 1024, 1024], P('dp', 'seq'), may hold values from -6 to 6
- norm_gains: bfloat16 [6, 1024], P(None, 'seq'), may hold values from 0.5 to 1.5
- norm_biases: bfloat16 [6, 1024], P(None, 'seq'), may hold values from -3 to 3
- front_up: bfloat16 [1024, 4096], P('seq'), may hold values from -0.1875 to 0.1875
- front_down: bfloat16 [4096, 1024], P('seq'), may hold values from -0.09375 to 0.09375
- attend_in: bfloat16 [1024, 3072], P('seq'), may hold values from -0.1875 to 0.1875
- attend_out: bfloat16 [1024, 1024], P('seq'), may hold values from -0.75 to 0.75
- slopes: float32 [16], replicated, may hold values from 0.05 to 0.6
- point_in: bfloat16 [1024, 2048], P('seq'), may hold values from -0.1875 to 0.1875
- depthwise: bfloat16 [31, 1024], P(None, 'seq'), may hold values from -1 to 1
- point_out: bfloat16 [1024, 1024], P('seq'), may hold values from -0.1875 to 0.1875
- rear_up: bfloat16 [1024, 4096], P('seq'), may hold values from -0.1875 to 0.1875
- rear_down: bfloat16 [4096, 1024], P('seq'), may hold values from -0.09375 to 0.09375
Outputs:
- result: bfloat16 [8, 1024, 1024], P('dp', 'seq')
- frames_grad: bfloat16 [8, 1024, 1024], P('dp', 'seq')
- gains_grad: float32 [6, 1024], P(None, 'seq')
- biases_grad: float32 [6, 1024], P(None, 'seq')
- front_up_grad: float32 [1024, 4096], P('seq')
- front_down_grad: float32 [4096, 1024], P('seq')
- attend_in_grad: float32 [1024, 3072], P('seq')
- attend_out_grad: float32 [1024, 1024], P('seq')
- slopes_grad: float32 [16], replicated
- point_in_grad: float32 [1024, 2048], P('seq')
- depthwise_grad: float32 [31, 1024], P(None, 'seq')
- point_out_grad: float32 [1024, 1024], P('seq')
- rear_up_grad: float32 [1024, 4096], P('seq')
- rear_down_grad: float32 [4096, 1024], P('seq')
Inputs may be any that keep to these rules, and one draw needn't show every extreme that they name: `segments`: each row's numbers start at 0 and rise by 0 or 1 from one frame to the next, so an utterance is a run of frames. In each group of 2 rows of one index of dp, one row drawn from the seed holds exactly three utterances, the middle one starting within the first 128 frames and ending within the last 128; every other row ends at the number 2 * 8.
All inputs are finite; a program needn't handle non-finite values.
Results may differ from a plain program's by a relative error of at most 0.03.
Values may be sent and summed in bfloat16 or wider, within the bound.
A program may use at most 320 MiB of HBM per device.

v0:
```python
import jax
import jax.numpy as jnp
from jax import lax
from jax.sharding import PartitionSpec as P


def padded(value, sides, width):
    for axis, dim in sides:
        peers, length = (lax.axis_size(axis), value.shape[dim])
        up = [(i, (i + 1) % peers) for i in range(peers - 1)]
        down = [(j, i) for i, j in up]
        last = lax.slice_in_dim(value, length - width, length, axis=dim)
        leading = lax.slice_in_dim(value, 0, width, axis=dim)
        before = lax.ppermute(last, axis, up)
        after = lax.ppermute(leading, axis, down)
        value = jnp.concatenate([before, value, after], axis=dim)
    return value


def shifted(block, axis, distance):
    devices = range(lax.axis_size(axis))
    route = [((i - distance) % len(devices), i) for i in devices]
    return lax.ppermute(block, axis, route)


def layer_norm(stream, norm_gain, norm_bias):
    average = jnp.mean(stream, axis=-1, keepdims=True)
    centred = stream - average
    spread = jnp.mean(centred * centred, axis=-1, keepdims=True)
    return centred * lax.rsqrt(spread + 1e-05) * norm_gain + norm_bias


def feed_forward(stream, norm_gain, norm_bias, weight_up, weight_down):
    normed, norm_pull = jax.vjp(layer_norm, stream, norm_gain, norm_bias)
    normed_low = normed.astype(jnp.bfloat16)
    inner_act = jnp.dot(normed_low, weight_up, preferred_element_type=jnp.float32)
    hidden, act_pull = jax.vjp(jax.nn.silu, inner_act)
    hidden_low = hidden.astype(jnp.bfloat16)
    branch = jnp.dot(hidden_low, weight_down, preferred_element_type=jnp.float32)
    return (stream + 0.5 * branch, (norm_pull, normed_low, act_pull, hidden_low))


def feed_backward(grad_in, saved_state, weight_up, weight_down):
    norm_pull, normed_low, act_pull, hidden_low = saved_state
    branch_low = (0.5 * grad_in).astype(jnp.bfloat16)
    down_grad = jnp.einsum("tf,td->fd", hidden_low, branch_low, preferred_element_type=jnp.float32)
    hidden_grad = jnp.einsum(
        "td,fd->tf", branch_low, weight_down, preferred_element_type=jnp.float32
    )
    inner_grad = act_pull(hidden_grad)[0].astype(jnp.bfloat16)
    up_grad = jnp.einsum("td,tf->df", normed_low, inner_grad, preferred_element_type=jnp.float32)
    normed_grad = jnp.einsum("tf,df->td", inner_grad, weight_up, preferred_element_type=jnp.float32)
    stream_grad, gain_grad, bias_grad = norm_pull(normed_grad)
    return (grad_in + stream_grad, gain_grad, bias_grad, up_grad, down_grad)


def score_block(query_heads, key_piece, query_start, key_start, query_seg, key_seg, slopes):
    row_count, key_count, feature_count = key_piece.shape
    head_count = query_heads.shape[2]
    head_size = query_heads.shape[3]
    key_heads = key_piece.reshape(row_count, key_count, head_count, head_size)
    raw_score = jnp.einsum(
        "rqhd,rkhd->rqhk", query_heads, key_heads, preferred_element_type=jnp.float32
    ) * head_size ** (-0.5)
    query_place = query_start + jnp.arange(query_heads.shape[1], dtype=jnp.int32)
    key_place = key_start + jnp.arange(key_count, dtype=jnp.int32)
    log_distance = jnp.log1p(jnp.abs(query_place[:, None] - key_place[None, :]).astype(jnp.float32))
    is_live = (query_seg[:, :, None] == key_seg[:, None, :])[:, :, None, :]
    logits = jnp.where(
        is_live, raw_score - slopes[None, None, :, None] * log_distance[None, :, None, :], -1e30
    )
    return (logits, is_live, log_distance, key_heads)


def prob_grads(
    query_heads,
    grad_heads,
    log_sum,
    row_delta,
    query_start,
    query_seg,
    key_piece,
    value_piece,
    key_start,
    key_seg,
    slopes,
):
    logits, is_live, log_distance, key_heads = score_block(
        query_heads, key_piece, query_start, key_start, query_seg, key_seg, slopes
    )
    row_prob = jnp.where(is_live, jnp.exp(logits - log_sum[..., None]), 0.0)
    value_heads = value_piece.reshape(key_heads.shape)
    prob_grad = jnp.einsum(
        "rqhd,rkhd->rqhk", grad_heads, value_heads, preferred_element_type=jnp.float32
    )
    score_grad = row_prob * (prob_grad - row_delta[..., None])
    return (row_prob, score_grad, score_grad.astype(jnp.bfloat16), log_distance, key_heads)


def body(
    frames,
    segments,
    cotangent,
    norm_gains,
    norm_biases,
    front_up,
    front_down,
    attend_in,
    attend_out,
    slopes,
    point_in,
    depthwise,
    point_out,
    rear_up,
    rear_down,
):
    row_count, frame_count, feature_count = frames.shape
    head_count = slopes.shape[0]
    head_size = feature_count // head_count
    token_count = row_count * frame_count
    seq_size = lax.axis_size("seq")
    seq_index = lax.axis_index("seq")
    query_start = seq_index * frame_count
    score_scale = head_size ** (-0.5)
    (
        gains_w,
        biases_w,
        front_up_w,
        front_down_w,
        attend_in_w,
        attend_out_w,
        point_in_w,
        depth_w,
        point_out_w,
        rear_up_w,
        rear_down_w,
    ) = (
        lax.all_gather(norm_gains, "seq", axis=1, tiled=True),
        lax.all_gather(norm_biases, "seq", axis=1, tiled=True),
        lax.all_gather(front_up, "seq", axis=0, tiled=True),
        lax.all_gather(front_down, "seq", axis=0, tiled=True),
        lax.all_gather(attend_in, "seq", axis=0, tiled=True),
        lax.all_gather(attend_out, "seq", axis=0, tiled=True),
        lax.all_gather(point_in, "seq", axis=0, tiled=True),
        lax.all_gather(depthwise, "seq", axis=1, tiled=True),
        lax.all_gather(point_out, "seq", axis=0, tiled=True),
        lax.all_gather(rear_up, "seq", axis=0, tiled=True),
        lax.all_gather(rear_down, "seq", axis=0, tiled=True),
    )
    gains_f = gains_w.astype(jnp.float32)
    biases_f = biases_w.astype(jnp.float32)
    depth_f = depth_w.astype(jnp.float32)
    kernel_len = depth_f.shape[0]
    half_k = kernel_len // 2
    segment_row = lax.all_gather(segments, "seq", axis=1, tiled=True)
    start_stream = frames.astype(jnp.float32).reshape(token_count, feature_count)
    after_front, front_saved = feed_forward(
        start_stream, gains_f[0], biases_f[0], front_up_w, front_down_w
    )
    attend_normed, attend_pull = jax.vjp(layer_norm, after_front, gains_f[1], biases_f[1])
    attend_low = attend_normed.astype(jnp.bfloat16)
    projected = jnp.dot(attend_low, attend_in_w, preferred_element_type=jnp.float32).astype(
        jnp.bfloat16
    )
    query_heads = projected[:, :feature_count].reshape(
        row_count, frame_count, head_count, head_size
    )
    key_low = projected[:, feature_count : 2 * feature_count].reshape(
        row_count, frame_count, feature_count
    )
    value_low = projected[:, 2 * feature_count :].reshape(row_count, frame_count, feature_count)
    stat_shape = (row_count, frame_count, head_count)
    start = jnp.int32(0)
    key_piece = lax.all_gather(key_low, "seq", axis=1, tiled=True)
    value_piece = lax.all_gather(value_low, "seq", axis=1, tiled=True)
    key_seg = segment_row
    row_top = jnp.full(stat_shape, -1e30, jnp.float32)
    logits, is_live, log_distance, key_heads = score_block(
        query_heads, key_piece, query_start, start, segments, key_seg, slopes
    )
    new_top = jnp.maximum(row_top, jnp.max(logits, axis=-1))
    row_exp = jnp.where(is_live, jnp.exp(logits - new_top[..., None]), 0.0)
    value_heads = value_piece.reshape(key_heads.shape)
    accum = jnp.einsum(
        "rqhk,rkhd->rqhd",
        row_exp.astype(jnp.bfloat16),
        value_heads,
        preferred_element_type=jnp.float32,
    )
    row_top, row_total, accum = (new_top, jnp.sum(row_exp, axis=-1), accum)
    attended = accum / row_total[..., None]
    log_sum = row_top + jnp.log(row_total)
    attended_low = attended.reshape(token_count, feature_count).astype(jnp.bfloat16)
    after_attend = after_front + jnp.dot(
        attended_low, attend_out_w, preferred_element_type=jnp.float32
    )
    conv_normed, conv_pull = jax.vjp(layer_norm, after_attend, gains_f[2], biases_f[2])
    conv_low = conv_normed.astype(jnp.bfloat16)
    conv_pre = jnp.dot(conv_low, point_in_w, preferred_element_type=jnp.float32)

    def gate_unit(inner_act):
        return inner_act[:, :feature_count] * jax.nn.sigmoid(inner_act[:, feature_count:])

    gated, gate_pull = jax.vjp(gate_unit, conv_pre)
    gated_low = gated.astype(jnp.bfloat16).reshape(row_count, frame_count, feature_count)
    gated_wide = padded(gated_low, (("seq", 1),), half_k).astype(jnp.float32)
    padded_seg = jnp.pad(segment_row, ((0, 0), (half_k, half_k)), constant_values=-1)
    seg_window = lax.dynamic_slice_in_dim(padded_seg, query_start, frame_count + 2 * half_k, 1)
    same_list = [
        (seg_window[:, offset : offset + frame_count] == segments)[..., None]
        for offset in range(kernel_len)
    ]
    mixed_conv = jnp.zeros((row_count, frame_count, feature_count), jnp.float32)
    for offset in range(kernel_len):
        mixed_conv = mixed_conv + jnp.where(
            same_list[offset], depth_f[offset] * gated_wide[:, offset : offset + frame_count], 0.0
        )

    def norm_silu(stream, norm_gain, norm_bias):
        return jax.nn.silu(layer_norm(stream, norm_gain, norm_bias))

    activated, activated_pull = jax.vjp(
        norm_silu, mixed_conv.reshape(token_count, feature_count), gains_f[3], biases_f[3]
    )
    activated_low = activated.astype(jnp.bfloat16)
    after_conv = after_attend + jnp.dot(
        activated_low, point_out_w, preferred_element_type=jnp.float32
    )
    after_rear, rear_saved = feed_forward(
        after_conv, gains_f[4], biases_f[4], rear_up_w, rear_down_w
    )
    final_out, final_pull = jax.vjp(layer_norm, after_rear, gains_f[5], biases_f[5])
    result = final_out.astype(jnp.bfloat16).reshape(row_count, frame_count, feature_count)
    grad_rear, gain_five, bias_five = final_pull(
        cotangent.astype(jnp.float32).reshape(token_count, feature_count)
    )
    grad_conv, gain_four, bias_four, rear_up_grad, rear_down_grad = feed_backward(
        grad_rear, rear_saved, rear_up_w, rear_down_w
    )
    conv_branch = grad_conv.astype(jnp.bfloat16)
    point_out_grad = jnp.einsum(
        "td,te->de", activated_low, conv_branch, preferred_element_type=jnp.float32
    )
    activated_grad = jnp.einsum(
        "te,de->td", conv_branch, point_out_w, preferred_element_type=jnp.float32
    )
    mixed_grad, gain_three, bias_three = activated_pull(activated_grad)
    mixed_low = mixed_grad.astype(jnp.bfloat16).reshape(row_count, frame_count, feature_count)
    grad_wide = padded(mixed_low, (("seq", 1),), half_k).astype(jnp.float32)
    mixed_back = mixed_low.astype(jnp.float32)
    depth_rows = [
        jnp.sum(
            jnp.where(
                same_list[offset], mixed_back * gated_wide[:, offset : offset + frame_count], 0.0
            ),
            axis=(0, 1),
        )
        for offset in range(kernel_len)
    ]
    depthwise_grad = jnp.stack(depth_rows)
    gated_grad = jnp.zeros((row_count, frame_count, feature_count), jnp.float32)
    for offset in range(kernel_len):
        mirror = 2 * half_k - offset
        gated_grad = gated_grad + jnp.where(
            same_list[mirror], depth_f[offset] * grad_wide[:, mirror : mirror + frame_count], 0.0
        )
    pre_grad = gate_pull(gated_grad.reshape(token_count, feature_count))[0].astype(jnp.bfloat16)
    point_in_grad = jnp.einsum("td,tc->dc", conv_low, pre_grad, preferred_element_type=jnp.float32)
    conv_normed_grad = jnp.einsum(
        "tc,dc->td", pre_grad, point_in_w, preferred_element_type=jnp.float32
    )
    conv_stream_grad, gain_two, bias_two = conv_pull(conv_normed_grad)
    grad_attend = grad_conv + conv_stream_grad
    attend_branch = grad_attend.astype(jnp.bfloat16)
    attend_out_grad = jnp.einsum(
        "td,te->de", attended_low, attend_branch, preferred_element_type=jnp.float32
    )
    attended_grad = jnp.einsum(
        "te,de->td", attend_branch, attend_out_w, preferred_element_type=jnp.float32
    )
    grad_heads = attended_grad.astype(jnp.bfloat16).reshape(
        row_count, frame_count, head_count, head_size
    )
    row_delta = jnp.sum(grad_heads.astype(jnp.float32) * attended, axis=-1)

    def query_terms(state, key_piece, value_piece, start, key_seg):
        query_grad, slope_grad = state
        row_prob, score_grad, score_low, log_distance, key_heads = prob_grads(
            query_heads,
            grad_heads,
            log_sum,
            row_delta,
            query_start,
            segments,
            key_piece,
            value_piece,
            start,
            key_seg,
            slopes,
        )
        query_grad = (
            query_grad
            + jnp.einsum(
                "rqhk,rkhd->rqhd", score_low, key_heads, preferred_element_type=jnp.float32
            )
            * score_scale
        )
        slope_grad = slope_grad - jnp.einsum("rqhk,qk->h", score_grad, log_distance)
        return (query_grad, slope_grad, row_prob, score_low)

    query_zero = jnp.zeros((row_count, frame_count, head_count, head_size), jnp.float32)
    slope_zero = jnp.zeros((head_count,), jnp.float32)
    local_zero = jnp.zeros((row_count, frame_count, feature_count), jnp.float32)

    def accumulate(step, query_grad, slope_grad, pair_kv, pair_acc):
        owner = (seq_index + step) % seq_size
        start = owner * frame_count
        key_seg = lax.dynamic_slice_in_dim(segment_row, start, frame_count, 1)
        grad_q = query_grad
        grad_s = slope_grad
        key_acc = pair_acc[0]
        value_acc = pair_acc[1]
        grad_q, grad_s, row_prob, score_low = query_terms(
            (grad_q, grad_s), pair_kv[0], pair_kv[1], start, key_seg
        )
        key_acc = key_acc + (
            jnp.einsum(
                "rqhk,rqhd->rkhd", score_low, query_heads, preferred_element_type=jnp.float32
            )
            * score_scale
        ).reshape(row_count, frame_count, feature_count)
        value_acc = value_acc + jnp.einsum(
            "rqhk,rqhd->rkhd",
            row_prob.astype(jnp.bfloat16),
            grad_heads,
            preferred_element_type=jnp.float32,
        ).reshape(row_count, frame_count, feature_count)
        query_grad, slope_grad, key_acc, value_acc = (grad_q, grad_s, key_acc, value_acc)
        pair_acc = shifted(jnp.stack([key_acc, value_acc]).astype(jnp.bfloat16), "seq", -1).astype(
            jnp.float32
        )
        return (query_grad, slope_grad, pair_acc)

    def cycle_step(step, carry):
        query_grad, slope_grad, pair_kv, pair_acc = carry
        next_kv = shifted(pair_kv, "seq", -1)
        query_grad, slope_grad, pair_acc = accumulate(
            step, query_grad, slope_grad, pair_kv, pair_acc
        )
        return (query_grad, slope_grad, next_kv, pair_acc)

    pair_start = jnp.stack([key_low, value_low])
    acc_start = jnp.stack([local_zero, local_zero])
    query_grad, slope_grad, pair_kv, pair_acc = lax.fori_loop(
        0, seq_size - 1, cycle_step, (query_zero, slope_zero, pair_start, acc_start)
    )
    query_grad, slope_grad, pair_acc = accumulate(
        seq_size - 1, query_grad, slope_grad, pair_kv, pair_acc
    )
    key_grad = pair_acc[0]
    value_grad = pair_acc[1]
    projected_grad = jnp.concatenate(
        [
            query_grad.reshape(token_count, feature_count),
            key_grad.reshape(token_count, feature_count),
            value_grad.reshape(token_count, feature_count),
        ],
        axis=1,
    ).astype(jnp.bfloat16)
    attend_in_grad = jnp.einsum(
        "td,tc->dc", attend_low, projected_grad, preferred_element_type=jnp.float32
    )
    attend_normed_grad = jnp.einsum(
        "tc,dc->td", projected_grad, attend_in_w, preferred_element_type=jnp.float32
    )
    attend_stream_grad, gain_one, bias_one = attend_pull(attend_normed_grad)
    grad_front = grad_attend + attend_stream_grad
    start_grad, gain_zero, bias_zero, front_up_grad, front_down_grad = feed_backward(
        grad_front, front_saved, front_up_w, front_down_w
    )
    frames_grad = start_grad.astype(jnp.bfloat16).reshape(row_count, frame_count, feature_count)
    gains_local = jnp.stack([gain_zero, gain_one, gain_two, gain_three, gain_four, gain_five])
    biases_local = jnp.stack([bias_zero, bias_one, bias_two, bias_three, bias_four, bias_five])
    slope_rows = jnp.broadcast_to(slope_grad[None, :], (seq_size, head_count))
    shares = (
        lax.psum_scatter(
            gains_local.astype(jnp.bfloat16), "seq", scatter_dimension=1, tiled=True
        ).astype(jnp.float32),
        lax.psum_scatter(
            biases_local.astype(jnp.bfloat16), "seq", scatter_dimension=1, tiled=True
        ).astype(jnp.float32),
        lax.psum_scatter(
            front_up_grad.astype(jnp.bfloat16), "seq", scatter_dimension=0, tiled=True
        ).astype(jnp.float32),
        lax.psum_scatter(
            front_down_grad.astype(jnp.bfloat16), "seq", scatter_dimension=0, tiled=True
        ).astype(jnp.float32),
        lax.psum_scatter(
            attend_in_grad.astype(jnp.bfloat16), "seq", scatter_dimension=0, tiled=True
        ).astype(jnp.float32),
        lax.psum_scatter(
            attend_out_grad.astype(jnp.bfloat16), "seq", scatter_dimension=0, tiled=True
        ).astype(jnp.float32),
        lax.psum_scatter(
            slope_rows.astype(jnp.bfloat16), "seq", scatter_dimension=0, tiled=True
        ).astype(jnp.float32),
        lax.psum_scatter(
            point_in_grad.astype(jnp.bfloat16), "seq", scatter_dimension=0, tiled=True
        ).astype(jnp.float32),
        lax.psum_scatter(
            depthwise_grad.astype(jnp.bfloat16), "seq", scatter_dimension=1, tiled=True
        ).astype(jnp.float32),
        lax.psum_scatter(
            point_out_grad.astype(jnp.bfloat16), "seq", scatter_dimension=0, tiled=True
        ).astype(jnp.float32),
        lax.psum_scatter(
            rear_up_grad.astype(jnp.bfloat16), "seq", scatter_dimension=0, tiled=True
        ).astype(jnp.float32),
        lax.psum_scatter(
            rear_down_grad.astype(jnp.bfloat16), "seq", scatter_dimension=0, tiled=True
        ).astype(jnp.float32),
    )
    totals = (
        lax.psum(shares[0].astype(jnp.bfloat16), "dp").astype(jnp.float32),
        lax.psum(shares[1].astype(jnp.bfloat16), "dp").astype(jnp.float32),
        lax.psum(shares[2].astype(jnp.bfloat16), "dp").astype(jnp.float32),
        lax.psum(shares[3].astype(jnp.bfloat16), "dp").astype(jnp.float32),
        lax.psum(shares[4].astype(jnp.bfloat16), "dp").astype(jnp.float32),
        lax.psum(shares[5].astype(jnp.bfloat16), "dp").astype(jnp.float32),
        lax.psum(shares[6].astype(jnp.bfloat16), "dp").astype(jnp.float32),
        lax.psum(shares[7].astype(jnp.bfloat16), "dp").astype(jnp.float32),
        lax.psum(shares[8].astype(jnp.bfloat16), "dp").astype(jnp.float32),
        lax.psum(shares[9].astype(jnp.bfloat16), "dp").astype(jnp.float32),
        lax.psum(shares[10].astype(jnp.bfloat16), "dp").astype(jnp.float32),
        lax.psum(shares[11].astype(jnp.bfloat16), "dp").astype(jnp.float32),
    )
    return (
        result,
        frames_grad,
        totals[0],
        totals[1],
        totals[2],
        totals[3],
        totals[4],
        totals[5],
        totals[6].reshape(head_count),
        totals[7],
        totals[8],
        totals[9],
        totals[10],
        totals[11],
    )


def solution(mesh):
    placed = (
        P("dp", "seq", None),
        P("dp", "seq"),
        P("dp", "seq", None),
        P(None, "seq"),
        P(None, "seq"),
        P("seq", None),
        P("seq", None),
        P("seq", None),
        P("seq", None),
        P(),
        P("seq", None),
        P(None, "seq"),
        P("seq", None),
        P("seq", None),
        P("seq", None),
    )
    return jax.shard_map(
        body,
        mesh=mesh,
        in_specs=placed,
        out_specs=(
            P("dp", "seq", None),
            P("dp", "seq", None),
            P(None, "seq"),
            P(None, "seq"),
            P("seq", None),
            P("seq", None),
            P("seq", None),
            P("seq", None),
            P(),
            P("seq", None),
            P(None, "seq"),
            P("seq", None),
            P("seq", None),
            P("seq", None),
        ),
        check_vma=False,
    )
```

profile of v0, /device:TPU:0, one launch (start us, length us, event | category | flops | bytes accessed | tf_op | source)
XLA Modules:
  0.0 1725.6 jit_solution(17239640497005358816)
XLA Ops:
  9.5 14.5 all_gather.43
  24.0 13.0 all_gather.42
  41.1 53.5 %all-gather.11.cloned.1.call-done = bf16[1024,4096]{1,0:T(8,128)(2,1)} async-done(((bf16[128,4096]{1,0:T(8,128)(2,1)}), bf16[1024,4096]{1,0:T(8,128)(2,1)}) %all-gather.11.cloned.1.call-update) | async-done | bytes 8388624 | tf_op jit(solution)/shard_map/all_gather | solution.py:140
  102.3 74.5 %all-gather.13.cloned.1.call-done = bf16[4096,1024]{1,0:T(8,128)(2,1)} async-done(((bf16[512,1024]{1,0:T(8,128)(2,1)}), bf16[4096,1024]{1,0:T(8,128)(2,1)}) %all-gather.13.cloned.1.call-update) | async-done | bytes 8388624 | tf_op jit(solution)/shard_map/all_gather | solution.py:141
  184.3 57.5 %all-gather.15.cloned.1.call-done = bf16[1024,3072]{1,0:T(8,128)(2,1)} async-done(((bf16[128,3072]{1,0:T(8,128)(2,1)}), bf16[1024,3072]{1,0:T(8,128)(2,1)}) %all-gather.15.cloned.1.call-update) | async-done | bytes 6291472 | tf_op jit(solution)/shard_map/all_gather | solution.py:142
  251.7 9.1 all_gather.48
  260.8 13.1 all_gather.51
  282.7 11.4 all-gather.19.cloned.1.call-done
  300.6 41.4 %all-gather.17.cloned.1.call-done = bf16[2,1024,1024]{2,1,0:T(8,128)(2,1)} async-done(((bf16[2,128,1024]{2,1,0:T(8,128)(2,1)}), bf16[2,1024,1024]{2,1,0:T(8,128)(2,1)}) %all-gather.17.cloned.1.call-update) | async-done | bytes 4194320 | tf_op jit(solution)/shard_map/all_gather | solution.py:175
  348.2 12.2 fusion.18
  360.4 8.7 fusion.16
  369.1 10.4 fusion.269
  383.3 36.2 %all-gather.23.cloned.1.call-done = bf16[1024,2048]{1,0:T(8,128)(2,1)} async-done(((bf16[128,2048]{1,0:T(8,128)(2,1)}), bf16[1024,2048]{1,0:T(8,128)(2,1)}) %all-gather.23.cloned.1.call-update) | async-done | bytes 4194320 | tf_op jit(solution)/shard_map/all_gather | solution.py:144
  429.1 15.7 fusion.256
  451.9 81.0 %all-gather.27.cloned.1.call-done = bf16[1024,4096]{1,0:T(8,128)(2,1)} async-done(((bf16[128,4096]{1,0:T(8,128)(2,1)}), bf16[1024,4096]{1,0:T(8,128)(2,1)}) %all-gather.27.cloned.1.call-update) | async-done | bytes 8388624 | tf_op jit(solution)/shard_map/all_gather | solution.py:147
  540.8 74.2 %all-gather.29.cloned.1.call-done = bf16[4096,1024]{1,0:T(8,128)(2,1)} async-done(((bf16[512,1024]{1,0:T(8,128)(2,1)}), bf16[4096,1024]{1,0:T(8,128)(2,1)}) %all-gather.29.cloned.1.call-update) | async-done | bytes 8388624 | tf_op jit(solution)/shard_map/all_gather | solution.py:148
  690.5 305.0 %while.22 = (s32[]{:T(128)}, f32[2,128,16,64]{1,3,2,0:T(8,128)}, f32[16]{0:T(128)S(1)}, bf16[2,2,128,1024]{2,3,1,0:T(8,128)(2,1)}, f32[2,2,128,1024]{2,3,1,0:T(8...) while((s32[]{:T(128)}, f32[2,128,16,64]{1,3,2,0:T(8,128)}, ...), condition=%wide.region_25.26_spmd.clone, body=%wide.region_23.25_spmd.clone.sunk | while | flops 345063744 | bytes 60594900 | solution.py:354
  708.9 12.6 collective-permute-done.1
  751.1 30.7 %collective-permute-done.1 = bf16[2,2,128,1024]{2,3,1,0:T(8,128)(2,1)} collective-permute-done((bf16[2,2,128,1024]{2,3,1,0:T(8,128)(2,1)}, bf16[2,2,128,1024]{2,3,1,0:T(8,128)(2,1)}, u32[]{:S(2)}, u32[]{:S(2)}) %collective-permute-start.1) | collective-permute-done | bytes 1048608 | tf_op jit(solution)/shard_map/while/body/eval_jaxpr/ppermute | solution.py:23
  784.5 21.1 %collective-permute-done = bf16[2,2,128,1024]{2,3,1,0:T(8,128)(2,1)} collective-permute-done((bf16[2,2,128,1024]{2,3,1,0:T(8,128)(2,1)S(1)}, bf16[2,2,128,1024]{2,3,1,0:T(8,128)(2,1)}, u32[]{:S(2)}, u32[]{:S(2)}) %collective-permute-start) | collective-permute-done | bytes 1048608 | tf_op jit(solution)/shard_map/while/body/eval_jaxpr/ppermute | solution.py:23
  911.1 8.5 collective-permute-done
  1021.9 11.2 collective-permute-done.6
  1110.6 90.1 %reduce-scatter.30.cloned.1.call-done = bf16[128,4096]{1,0:T(8,128)(2,1)} async-done(((bf16[1024,4096]{1,0:T(8,128)(2,1)}), bf16[128,4096]{1,0:T(8,128)(2,1)}) %reduce-scatter.30.cloned.1.call-update) | async-done | bytes 1048592 | tf_op jit(solution)/shard_map/reduce_scatter | solution.py:416
  1200.8 90.2 %reduce-scatter.32.cloned.1.call-done = bf16[512,1024]{1,0:T(8,128)(2,1)} async-done(((bf16[4096,1024]{1,0:T(8,128)(2,1)}), bf16[512,1024]{1,0:T(8,128)(2,1)}) %reduce-scatter.32.cloned.1.call-update) | async-done | bytes 1048592 | tf_op jit(solution)/shard_map/reduce_scatter | solution.py:419
  1290.9 90.1 %reduce-scatter.18.cloned.1.call-done = bf16[128,4096]{1,0:T(8,128)(2,1)} async-done(((bf16[1024,4096]{1,0:T(8,128)(2,1)}), bf16[128,4096]{1,0:T(8,128)(2,1)}) %reduce-scatter.18.cloned.1.call-update) | async-done | bytes 1048592 | tf_op jit(solution)/shard_map/reduce_scatter | solution.py:392
  1381.1 90.1 %reduce-scatter.20.cloned.1.call-done = bf16[512,1024]{1,0:T(8,128)(2,1)} async-done(((bf16[4096,1024]{1,0:T(8,128)(2,1)}), bf16[512,1024]{1,0:T(8,128)(2,1)}) %reduce-scatter.20.cloned.1.call-update) | async-done | bytes 1048592 | tf_op jit(solution)/shard_map/reduce_scatter | solution.py:395
  1472.3 13.6 all-reduce.3
  1486.5 16.2 reduce-scatter.38.cloned.1.call-done
  1504.8 29.3 %reduce-scatter.34.cloned.1.call-done = bf16[128,6]{1,0:T(8,128)(2,1)} async-done(((bf16[1024,6]{1,0:T(8,128)(2,1)}), bf16[128,6]{1,0:T(8,128)(2,1)}) %reduce-scatter.34.cloned.1.call-update) | async-done | bytes 1552
  1534.9 30.5 %reduce-scatter.36.cloned.1.call-done = bf16[128,6]{1,0:T(8,128)(2,1)} async-done(((bf16[1024,6]{1,0:T(8,128)(2,1)}), bf16[128,6]{1,0:T(8,128)(2,1)}) %reduce-scatter.36.cloned.1.call-update) | async-done | bytes 1552
  1566.2 16.1 all-reduce.4
  1584.7 120.8 %all-reduce.8.cloned.1.call-done = (bf16[128,4096]{1,0:T(8,128)(2,1)}, bf16[512,1024]{1,0:T(8,128)(2,1)}, bf16[128,3072]{1,0:T(8,128)(2,1)}, bf16[128,1024]{1,0:...) async-done(((bf16[128,4096]{1,0:T(8,128)(2,1)}, bf16[512,1024]{1,0:T(8,128)(2,1)}, ...) | async-done | bytes 6029328 | tf_op jit(solution)/shard_map/psum | solution.py:426
  (838 shorter events, 509.4 us)
Async XLA Ops:
  7.2 87.4 %all-gather.11.cloned.1.call-start = ((), (), s32[]{:S(2)}) async-start(), calls=%async_computation.11 | async-start | bytes 9437184 | tf_op jit(solution)/shard_map/all_gather | solution.py:140
  7.9 168.9 %all-gather.13.cloned.1.call-start = ((), (), s32[]{:S(2)}) async-start(), calls=%async_computation.12 | async-start | bytes 9437184 | tf_op jit(solution)/shard_map/all_gather | solution.py:141
  8.7 233.1 %all-gather.15.cloned.1.call-start = ((), (), s32[]{:S(2)}) async-start(), calls=%async_computation.13 | async-start | bytes 7077888 | tf_op jit(solution)/shard_map/all_gather | solution.py:142
  9.4 284.7 %all-gather.19.cloned.1.call-start = ((), (), s32[]{:S(2)}) async-start(), calls=%async_computation.15 | async-start | bytes 4718592 | tf_op jit(solution)/shard_map/all_gather | solution.py:174
  247.6 94.4 %all-gather.17.cloned.1.call-start = ((), (), s32[]{:S(2)}) async-start(), calls=%async_computation.14 | async-start | bytes 4718592 | tf_op jit(solution)/shard_map/all_gather | solution.py:175
  248.2 131.9 %all-gather.21.cloned.1.call-start = ((), (), s32[]{:S(2)}) async-start(), calls=%async_computation.16 | async-start | bytes 2359296 | tf_op jit(solution)/shard_map/all_gather | solution.py:143
  248.8 170.7 %all-gather.23.cloned.1.call-start = ((), (), s32[]{:S(2)}) async-start(), calls=%async_computation.17 | async-start | bytes 4718592 | tf_op jit(solution)/shard_map/all_gather | solution.py:144
  249.5 199.5 %all-gather.25.cloned.1.call-start = ((), (), s32[]{:S(2)}) async-start(), calls=%async_computation.18 | async-start | bytes 2359296 | tf_op jit(solution)/shard_map/all_gather | solution.py:146
  250.3 282.6 %all-gather.27.cloned.1.call-start = ((), (), s32[]{:S(2)}) async-start(), calls=%async_computation.19 | async-start | bytes 9437184 | tf_op jit(solution)/shard_map/all_gather | solution.py:147
  251.0 364.0 %all-gather.29.cloned.1.call-start = ((), (), s32[]{:S(2)}) async-start(), calls=%async_computation.20 | async-start | bytes 9437184 | tf_op jit(solution)/shard_map/all_gather | solution.py:148
  251.6 855.0 %reduce-scatter.28.cloned.1.call-start = ((), (), s32[]{:S(2)}) async-start(), calls=%async_computation.26 | async-start | bytes 2359296 | tf_op jit(solution)/shard_map/reduce_scatter | solution.py:413
  644.4 462.3 %reduce-scatter.24.cloned.1.call-start = ((), (), s32[]{:S(2)}) async-start(), calls=%async_computation.24 | async-start | bytes 2359296 | tf_op jit(solution)/shard_map/reduce_scatter | solution.py:401
  670.3 436.4 %reduce-scatter.26.cloned.1.call-start = ((), (), s32[]{:S(2)}) async-start(), calls=%async_computation.25 | async-start | bytes 4718592 | tf_op jit(solution)/shard_map/reduce_scatter | solution.py:407
  689.9 420.7 %reduce-scatter.22.cloned.1.call-start = ((), (), s32[]{:S(2)}) async-start(), calls=%async_computation.23 | async-start | bytes 7077888 | tf_op jit(solution)/shard_map/reduce_scatter | solution.py:398
  701.0 20.6 %collective-permute-start.1 = (bf16[2,2,128,1024]{2,3,1,0:T(8,128)(2,1)}, bf16[2,2,128,1024]{2,3,1,0:T(8,128)(2,1)}, u32[]{:S(2)}, u32[]{:S(2)}) collective-permute-start(bf16[2,2,128,1024]{2,3,1,0:T(8,128)(2,1)} %pad_maximum_fusion.7), channel_id=1, source_target_pairs={{1,0},{2,1},{3,2},{4,3},{5,4},{6,5},{7,6},{0,7},{9,8},{10,9},{11,1... | collective-permute-start | bytes 3145736 | tf_op jit(solution)/shard_map/while/body/eval_jaxpr/ppermute | solution.py:23
  702.7 30.0 %collective-permute-start = (bf16[2,2,128,1024]{2,3,1,0:T(8,128)(2,1)S(1)}, bf16[2,2,128,1024]{2,3,1,0:T(8,128)(2,1)}, u32[]{:S(2)}, u32[]{:S(2)}) collective-permute-start(bf16[2,2,128,1024]{2,3,1,0:T(8,128)(2,1)S(1)} %copy.151), channel_id=1, source_target_pairs={{1,0},{2,1},{3,2},{4,3},{5,4},{6,5},{7,6},{0,7},{9,8},{10,9},{11,1... | collective-permute-start | bytes 3145736 | tf_op jit(solution)/shard_map/while/body/eval_jaxpr/ppermute | solution.py:23
  743.1 38.8 %collective-permute-start.1 = (bf16[2,2,128,1024]{2,3,1,0:T(8,128)(2,1)}, bf16[2,2,128,1024]{2,3,1,0:T(8,128)(2,1)}, u32[]{:S(2)}, u32[]{:S(2)}) collective-permute-start(bf16[2,2,128,1024]{2,3,1,0:T(8,128)(2,1)} %pad_maximum_fusion.7), channel_id=1, source_target_pairs={{1,0},{2,1},{3,2},{4,3},{5,4},{6,5},{7,6},{0,7},{9,8},{10,9},{11,1... | collective-permute-start | bytes 3145736 | tf_op jit(solution)/shard_map/while/body/eval_jaxpr/ppermute | solution.py:23
  746.9 58.7 %collective-permute-start = (bf16[2,2,128,1024]{2,3,1,0:T(8,128)(2,1)S(1)}, bf16[2,2,128,1024]{2,3,1,0:T(8,128)(2,1)}, u32[]{:S(2)}, u32[]{:S(2)}) collective-permute-start(bf16[2,2,128,1024]{2,3,1,0:T(8,128)(2,1)S(1)} %copy.151), channel_id=1, source_target_pairs={{1,0},{2,1},{3,2},{4,3},{5,4},{6,5},{7,6},{0,7},{9,8},{10,9},{11,1... | collective-permute-start | bytes 3145736 | tf_op jit(solution)/shard_map/while/body/eval_jaxpr/ppermute | solution.py:23
  816.0 16.6 collective-permute-start.1
  819.9 23.8 %collective-permute-start = (bf16[2,2,128,1024]{2,3,1,0:T(8,128)(2,1)S(1)}, bf16[2,2,128,1024]{2,3,1,0:T(8,128)(2,1)}, u32[]{:S(2)}, u32[]{:S(2)}) collective-permute-start(bf16[2,2,128,1024]{2,3,1,0:T(8,128)(2,1)S(1)} %copy.151), channel_id=1, source_target_pairs={{1,0},{2,1},{3,2},{4,3},{5,4},{6,5},{7,6},{0,7},{9,8},{10,9},{11,1... | collective-permute-start | bytes 3145736 | tf_op jit(solution)/shard_map/while/body/eval_jaxpr/ppermute | solution.py:23
  857.8 23.8 %collective-permute-start = (bf16[2,2,128,1024]{2,3,1,0:T(8,128)(2,1)S(1)}, bf16[2,2,128,1024]{2,3,1,0:T(8,128)(2,1)}, u32[]{:S(2)}, u32[]{:S(2)}) collective-permute-start(bf16[2,2,128,1024]{2,3,1,0:T(8,128)(2,1)S(1)} %copy.151), channel_id=1, source_target_pairs={{1,0},{2,1},{3,2},{4,3},{5,4},{6,5},{7,6},{0,7},{9,8},{10,9},{11,1... | collective-permute-start | bytes 3145736 | tf_op jit(solution)/shard_map/while/body/eval_jaxpr/ppermute | solution.py:23
  895.8 23.8 %collective-permute-start = (bf16[2,2,128,1024]{2,3,1,0:T(8,128)(2,1)S(1)}, bf16[2,2,128,1024]{2,3,1,0:T(8,128)(2,1)}, u32[]{:S(2)}, u32[]{:S(2)}) collective-permute-start(bf16[2,2,128,1024]{2,3,1,0:T(8,128)(2,1)S(1)} %copy.151), channel_id=1, source_target_pairs={{1,0},{2,1},{3,2},{4,3},{5,4},{6,5},{7,6},{0,7},{9,8},{10,9},{11,1... | collective-permute-start | bytes 3145736 | tf_op jit(solution)/shard_map/while/body/eval_jaxpr/ppermute | solution.py:23
  933.8 23.8 %collective-permute-start = (bf16[2,2,128,1024]{2,3,1,0:T(8,128)(2,1)S(1)}, bf16[2,2,128,1024]{2,3,1,0:T(8,128)(2,1)}, u32[]{:S(2)}, u32[]{:S(2)}) collective-permute-start(bf16[2,2,128,1024]{2,3,1,0:T(8,128)(2,1)S(1)} %copy.151), channel_id=1, source_target_pairs={{1,0},{2,1},{3,2},{4,3},{5,4},{6,5},{7,6},{0,7},{9,8},{10,9},{11,1... | collective-permute-start | bytes 3145736 | tf_op jit(solution)/shard_map/while/body/eval_jaxpr/ppermute | solution.py:23
  971.7 23.8 %collective-permute-start = (bf16[2,2,128,1024]{2,3,1,0:T(8,128)(2,1)S(1)}, bf16[2,2,128,1024]{2,3,1,0:T(8,128)(2,1)}, u32[]{:S(2)}, u32[]{:S(2)}) collective-permute-start(bf16[2,2,128,1024]{2,3,1,0:T(8,128)(2,1)S(1)} %copy.151), channel_id=1, source_target_pairs={{1,0},{2,1},{3,2},{4,3},{5,4},{6,5},{7,6},{0,7},{9,8},{10,9},{11,1... | collective-permute-start | bytes 3145736 | tf_op jit(solution)/shard_map/while/body/eval_jaxpr/ppermute | solution.py:23
  1039.2 161.6 %reduce-scatter.30.cloned.1.call-start = ((), (), s32[]{:S(2)}) async-start(), calls=%async_computation.27 | async-start | bytes 9437184 | tf_op jit(solution)/shard_map/reduce_scatter | solution.py:416
  1047.9 243.1 %reduce-scatter.32.cloned.1.call-start = ((), (), s32[]{:S(2)}) async-start(), calls=%async_computation.28 | async-start | bytes 9437184 | tf_op jit(solution)/shard_map/reduce_scatter | solution.py:419
  1057.3 323.8 %reduce-scatter.18.cloned.1.call-start = ((), (), s32[]{:S(2)}) async-start(), calls=%async_computation.21 | async-start | bytes 9437184 | tf_op jit(solution)/shard_map/reduce_scatter | solution.py:392
  1079.5 391.7 %reduce-scatter.20.cloned.1.call-start = ((), (), s32[]{:S(2)}) async-start(), calls=%async_computation.22 | async-start | bytes 9437184 | tf_op jit(solution)/shard_map/reduce_scatter | solution.py:395
  1087.7 415.0 %reduce-scatter.38.cloned.1.call-start = ((), (), s32[]{:S(2)}) async-start(), calls=%async_computation.31 | async-start | bytes 294912
  1096.8 437.3 %reduce-scatter.34.cloned.1.call-start = ((), (), s32[]{:S(2)}) async-start(), calls=%async_computation.29 | async-start | bytes 294912
  1105.3 460.1 %reduce-scatter.36.cloned.1.call-start = ((), (), s32[]{:S(2)}) async-start(), calls=%async_computation.30 | async-start | bytes 294912
  1106.6 598.8 %all-reduce.8.cloned.1.call-start = ((), (), s32[]{:S(2)}) async-start(), calls=%async_computation.32 | async-start | bytes 12058624 | tf_op jit(solution)/shard_map/psum | solution.py:426
  (225 other events, 9111.2 us)
Sparse Core Ops, SparseCore 0:
  9.6 84.8 all-gather.10
  96.1 80.6 all-gather.12
  178.5 63.2 all-gather.14
  247.7 46.3 all-gather.18
  296.1 45.7 all-gather.16
  343.4 27.8 all-gather.20
  372.9 46.5 all-gather.22
  421.1 27.8 all-gather.24
  450.6 82.2 all-gather.26
  534.4 80.5 all-gather.28
  644.5 34.6 reduce-scatter.27
  681.9 36.3 reduce-scatter.23
  720.5 86.1 reduce-scatter.25
  1039.3 71.3 reduce-scatter.21
  1112.8 87.9 reduce-scatter.29
  1202.9 87.9 reduce-scatter.31
  1293.1 87.9 reduce-scatter.17
  1383.2 87.9 reduce-scatter.19
  1474.0 28.6 reduce-scatter.37
  1505.5 28.5 reduce-scatter.33
  1536.9 28.4 reduce-scatter.35
  1570.7 134.6 all-reduce.7
where the time goes:
time: 1740 us; the launch traced here: 1730 us
  waiting for transfers between devices  1170 us (67%)
  matrix products  233 us (13%)
  other arithmetic  123 us (7%)
  blocking collectives  79.5 us (5%)
  local copies, waits for them, and re-layouts  61.1 us (4%)
  starting transfers between devices  42.3 us (2%)
  between operations  18 us (1%)
    ppermute x15, waiting for transfers between devices, shifted(): return lax.ppermute(block, axis, route)  169 us
    psum x1, waiting for transfers between devices, body(): lax.psum(shares[2].astype(jnp.bfloat16), 'dp').astype(jnp.float32)  121 us
    reduce_scatter x1, waiting for transfers between devices, body(): lax.psum_scatter(rear_down_grad.astype(jnp.bfloat16), 'seq', scatter_dime...  90.2 us
    reduce_scatter x1, waiting for transfers between devices, body(): lax.psum_scatter(front_down_grad.astype(jnp.bfloat16), 'seq', scatter_dim...  90.1 us
    reduce_scatter x1, waiting for transfers between devices, body(): lax.psum_scatter(front_up_grad.astype(jnp.bfloat16), 'seq', scatter_dimen...  90.1 us
    reduce_scatter x1, waiting for transfers between devices, body(): lax.psum_scatter(rear_up_grad.astype(jnp.bfloat16), 'seq', scatter_dimens...  90.1 us
    unnamed x25, waiting for transfers between devices  81.9 us
    all_gather x1, waiting for transfers between devices, body(): lax.all_gather(rear_up, 'seq', axis=0, tiled=True)  81 us
  transfers between devices with their start and end apart: 41, of which 35 were waited for; matrix products, arithmetic and copies ran while one was open for 21% of the time, Pallas kernels for 0%

commit v1 on v0

--- a/solution.py
+++ b/solution.py
@@ -1,6 +1,10 @@
+import functools
+
 import jax
 import jax.numpy as jnp
 from jax import lax
+from jax.experimental import pallas as pl
+from jax.experimental.pallas import tpu as pltpu
 from jax.sharding import PartitionSpec as P
 
 
@@ -452,6 +456,926 @@
     )
 
 
+def grid_pairs(target):
+    pairs = []
+    for dp in range(4):
+        for seq in range(8):
+            there = target(dp // 2, dp % 2, seq // 2, seq % 2)
+            if there is not None:
+                y, x, z, core = there
+                pairs.append((dp * 8 + seq, (y * 2 + x) * 8 + z * 2 + core))
+    return pairs
+
+
+OVER_X = grid_pairs(lambda y, x, z, core: (y, 1 - x, z, core))
+OVER_Y = grid_pairs(lambda y, x, z, core: (1 - y, x, z, core))
+OVER_CORE = grid_pairs(lambda y, x, z, core: (y, x, z, 1 - core))
+OVER_PAIR = grid_pairs(lambda y, x, z, core: (y, x, z + 1 - 2 * (z % 2), core))
+OVER_MIDDLE = grid_pairs(lambda y, x, z, core: (y, x, 3 - z, core) if z in (1, 2) else None)
+OUTWARD = grid_pairs(lambda y, x, z, core: (y, x, z + (1 if z == 2 else -1), core) if z in (1, 2) else None)
+ALONG_Z = [
+    grid_pairs(lambda y, x, z, core, k=k: (y, x, (z + k) % 4, core)) for k in range(4)
+]
+
+
+def send(value, pairs):
+    return lax.ppermute(value, ("dp", "seq"), pairs)
+
+
+def place():
+    dp, seq = lax.axis_index("dp"), lax.axis_index("seq")
+    return dp // 2, dp % 2, seq // 2, seq % 2
+
+
+def pick(value, index, axis):
+    return lax.dynamic_index_in_dim(value, index, axis, keepdims=False)
+
+
+MESH_ID = pl.DeviceIdType.MESH
+PIECE = 32
+
+
+def chunk_at(ref, lead, chunk, first, rows, tall):
+    if tall:
+        at = pl.ds(pl.multiple_of(128 * chunk + first, 16), rows)
+        return ref.at[lead, at, :] if lead is not None else ref.at[at, :]
+    at, cols = pl.ds(pl.multiple_of(first, 16), rows), pl.ds(1024 * chunk, 1024)
+    return ref.at[lead, at, cols] if lead is not None else ref.at[at, cols]
+
+
+def gather_kernel(*refs):
+    up, down, inward, vectors, segments = refs[:5]
+    up_all, down_all, in_all, vectors_all, segments_all = refs[5:10]
+    sems = refs[10:]
+    (z_sem, x_sem, y_sem, ax_sem, ay_sem, core_sem, own_sem, small_sem) = sems
+    y, x, z, core = place()
+    dp, seq = y * 2 + x, z * 2 + core
+    over_x = (y * 2 + 1 - x, seq)
+    over_y = ((1 - y) * 2 + x, seq)
+    over_core = (dp, z * 2 + 1 - core)
+    peers = [(dp, lax.rem(seq + k, 8)) for k in range(1, 8)]
+    barrier = pltpu.get_barrier_semaphore()
+    for there in peers + [over_x, over_y]:
+        pl.semaphore_signal(barrier, inc=1, device_id=there, device_id_type=MESH_ID)
+    pl.semaphore_wait(barrier, 9)
+
+    def remote(src, dst, sem, at, there):
+        copy = pltpu.make_async_remote_copy(
+            src_ref=src,
+            dst_ref=dst,
+            send_sem=sem.at[(0,) + at],
+            recv_sem=sem.at[(1,) + at],
+            device_id=there,
+            device_id_type=MESH_ID,
+        )
+        copy.start()
+        return copy
+
+    waits = []
+    for k, there in enumerate(peers):
+        waits.append(remote(vectors, vectors_all.at[seq], small_sem, (0, k), there))
+        waits.append(remote(segments, segments_all.at[seq], small_sem, (1, k), there))
+    chunks = [(up, up_all, j, False) for j in range(4)]
+    chunks += [(down, down_all, j, True) for j in range(4)]
+    chunks += [(inward, in_all, j, False) for j in range(3)]
+    mine = PIECE * dp
+    z_copies = {}
+    for t, (shard, full, j, tall) in enumerate(chunks):
+        for k in (1, 2, 3):
+            there = (dp, lax.rem(z + k, 4) * 2 + core)
+            z_copies[t, k] = remote(
+                chunk_at(shard, None, j, mine, PIECE, tall),
+                chunk_at(full, seq, j, mine, PIECE, tall),
+                z_sem,
+                (t, k - 1),
+                there,
+            )
+    local = []
+    for i, (shard, full) in enumerate(((up, up_all), (down, down_all), (inward, in_all))):
+        waits.append(remote(shard, full.at[seq], own_sem, (i,), over_core))
+        local.append(pltpu.make_async_copy(shard, full.at[seq], own_sem.at[2, i]))
+    local.append(pltpu.make_async_copy(vectors, vectors_all.at[seq], own_sem.at[2, 3]))
+    local.append(pltpu.make_async_copy(segments, segments_all.at[seq], own_sem.at[2, 4]))
+    for copy in local:
+        copy.start()
+
+    x_copies, y_copies, ax_copies, ay_copies = {}, {}, {}, {}
+    q_x, q_y = PIECE * (y * 2 + 1 - x), PIECE * ((1 - y) * 2 + x)
+
+    def source(k):
+        return lax.rem(z - k + 4, 4) * 2 + core
+
+    def forward(copies, t, k, first, rows, sem, there):
+        _, full, j, tall = chunks[t]
+        where = chunk_at(full, source(k), j, first, rows, tall)
+        copies[t, k] = remote(where, where, sem, (t, k - 1), there)
+
+    count = len(chunks)
+    for step in range(count + 2):
+        for k in (1, 2, 3):
+            if step < count:
+                z_copies[step, k].wait_recv()
+                forward(x_copies, step, k, mine, PIECE, x_sem, over_x)
+                forward(y_copies, step, k, mine, PIECE, y_sem, over_y)
+        for k in (1, 2, 3):
+            t = step - 1
+            if 0 <= t < count:
+                y_copies[t, k].wait_recv()
+                forward(ax_copies, t, k, q_y, PIECE // 2, ax_sem, over_x)
+                x_copies[t, k].wait_recv()
+                forward(ay_copies, t, k, q_x + PIECE // 2, PIECE // 2, ay_sem, over_y)
+        for k in (1, 2, 3):
+            t = step - 2
+            if 0 <= t < count:
+                ax_copies[t, k].wait_recv()
+                ay_copies[t, k].wait_recv()
+                _, full, j, tall = chunks[t]
+                where = chunk_at(full, source(k), j, 0, 128, tall)
+                waits.append(remote(where, where, core_sem, (t, k - 1), over_core))
+    for copy in waits:
+        copy.wait()
+    for group in (z_copies, x_copies, y_copies, ax_copies, ay_copies):
+        for copy in group.values():
+            copy.wait_send()
+    for copy in local:
+        copy.wait()
+
+
+def gather_front(front_up, front_down, attend_in, vectors, segments):
+    args = (front_up, front_down, attend_in, vectors, segments)
+    dma = pltpu.SemaphoreType.DMA
+    return pl.pallas_call(
+        gather_kernel,
+        in_specs=[pl.BlockSpec(memory_space=pltpu.HBM)] * 5,
+        out_specs=[pl.BlockSpec(memory_space=pltpu.HBM)] * 5,
+        out_shape=[jax.ShapeDtypeStruct((8,) + a.shape, a.dtype) for a in args],
+        scratch_shapes=[dma((2, 11, 3))] * 6 + [dma((3, 5)), dma((2, 2, 7))],
+        compiler_params=pltpu.CompilerParams(collective_id=0, has_side_effects=True),
+        name="gather_front",
+    )(*args)
+
+
+def place_kernel(where, shard, line, over_x, over_y, across_one, across_two, out):
+    y, x, z = where[0], where[1], where[2]
+    slot = lax.rem(z - pl.program_id(0) + 4, 4)
+    half = across_one.shape[1]
+
+    @pl.when(slot == 0)
+    def _():
+        out[0] = shard[...].reshape(out.shape[1:])
+
+    @pl.when(slot != 0)
+    def _():
+        out[0, y * 2 + x] = line[0]
+        out[0, y * 2 + 1 - x] = over_x[0]
+        out[0, (1 - y) * 2 + x] = over_y[0]
+        out[0, (1 - y) * 2 + 1 - x, :half] = across_one[0]
+        out[0, (1 - y) * 2 + 1 - x, half:] = across_two[0]
+
+
+def gather_halves(shard):
+    y, x, z, core = place()
+    rows, cols = shard.shape
+    part = rows // 4
+    own = lax.dynamic_slice_in_dim(shard, (y * 2 + x) * part, part, 0)
+    line = jnp.stack([send(own, ALONG_Z[k]) for k in (1, 2, 3)])
+    from_x = send(line, OVER_X)
+    from_y = send(line, OVER_Y)
+    across_one = send(from_y[:, : part // 2], OVER_X)
+    across_two = send(from_x[:, part // 2 :], OVER_Y)
+
+    def spec(height):
+        return pl.BlockSpec(
+            (1, height, cols),
+            lambda i, w: (lax.rem(jnp.maximum(lax.rem(w[2] - i + 4, 4), 1) + 2, 3), 0, 0),
+        )
+
+    half = pl.pallas_call(
+        place_kernel,
+        grid_spec=pltpu.PrefetchScalarGridSpec(
+            num_scalar_prefetch=1,
+            grid=(4,),
+            in_specs=[pl.BlockSpec((rows, cols), lambda i, w: (0, 0))]
+            + [spec(part)] * 3
+            + [spec(part // 2)] * 2,
+            out_specs=pl.BlockSpec((1, 4, part, cols), lambda i, w: (i, 0, 0, 0)),
+        ),
+        out_shape=jax.ShapeDtypeStruct((4, 4, part, cols), shard.dtype),
+        compiler_params=pltpu.CompilerParams(vmem_limit_bytes=32 * 2**20),
+        cost_estimate=pl.CostEstimate(
+            flops=0, bytes_accessed=rows * cols * 16, transcendentals=0
+        ),
+        name="place",
+    )(jnp.stack([y, x, z]).astype(jnp.int32), shard, line, from_x, from_y, across_one, across_two)
+    half = half.reshape(4 * rows, cols)
+    return half, send(half, OVER_CORE)
+
+
+def split_cols(value):
+    core = lax.axis_index("seq") % 2
+    width = value.shape[1] // 8
+    blocks = [value[:, i * width : (i + 1) * width] for i in range(8)]
+    first = jnp.concatenate(blocks[0::2], axis=1)
+    second = jnp.concatenate(blocks[1::2], axis=1)
+    is_first = core == 0
+    return jnp.where(is_first, first, second), jnp.where(is_first, second, first)
+
+
+def merge_cols(own, other):
+    core = lax.axis_index("seq") % 2
+    width = own.shape[1] // 4
+    is_first = core == 0
+    first = jnp.where(is_first, own, other)
+    second = jnp.where(is_first, other, own)
+    blocks = []
+    for i in range(4):
+        blocks += [first[:, i * width : (i + 1) * width], second[:, i * width : (i + 1) * width]]
+    return jnp.concatenate(blocks, axis=1)
+
+
+def mul(halves, weight):
+    if not isinstance(weight, tuple):
+        return jnp.dot(merge_cols(*halves), weight, preferred_element_type=jnp.float32)
+    out = jnp.dot(halves[0], weight[0], preferred_element_type=jnp.float32)
+    return out + jnp.dot(halves[1], weight[1], preferred_element_type=jnp.float32)
+
+
+def mul_back(grad, weight):
+    if not isinstance(weight, tuple):
+        return jnp.einsum("tc,dc->td", grad, weight, preferred_element_type=jnp.float32)
+    own = jnp.einsum("tc,dc->td", grad, weight[0], preferred_element_type=jnp.float32)
+    other = jnp.einsum("tc,dc->td", grad, weight[1], preferred_element_type=jnp.float32)
+    return merge_cols(own, other)
+
+
+def plus(a, b):
+    return (a.astype(jnp.float32) + b.astype(jnp.float32)).astype(jnp.bfloat16)
+
+
+LAG = 1
+
+
+def reduce_kernel(count, left, right, vec, out, vec_out, *scratch):
+    (g_buf, h_buf, a_buf, b_buf, q_buf, core_in, a_in, b_in, a2_in, b2_in, z_in, o_buf) = scratch[:12]
+    vec_in, vec_dp, sem, vec_sem = scratch[12:]
+    step = pl.program_id(0)
+    y, x, z, core = place()
+    dp, seq = y * 2 + x, z * 2 + core
+    over_x = (y * 2 + 1 - x, seq)
+    over_y = ((1 - y) * 2 + x, seq)
+    across = ((1 - y) * 2 + 1 - x, seq)
+    over_core = (dp, z * 2 + 1 - core)
+    peers = [(dp, lax.rem(seq + k, 8)) for k in range(1, 8)]
+    dp_peers = [(lax.rem(dp + k, 4), seq) for k in range(1, 4)]
+
+    @pl.when(step == 0)
+    def _():
+        barrier = pltpu.get_barrier_semaphore()
+        for there in peers + dp_peers:
+            pl.semaphore_signal(barrier, inc=1, device_id=there, device_id_type=MESH_ID)
+        pl.semaphore_wait(barrier, 10)
+
+    def remote(src, dst, t, slot, there):
+        return pltpu.make_async_remote_copy(
+            src_ref=src,
+            dst_ref=dst,
+            send_sem=sem.at[0, slot, t],
+            recv_sem=sem.at[1, slot, t],
+            device_id=there,
+            device_id_type=MESH_ID,
+        )
+
+    def f32(value):
+        return value.astype(jnp.float32)
+
+    def low(value):
+        return value.astype(jnp.bfloat16)
+
+    def core_copies(t, slot):
+        return [remote(g_buf.at[slot, 1], core_in.at[t], t, 0, over_core)]
+
+    def first_copies(t, slot):
+        return [
+            remote(h_buf.at[slot, pl.ds(0, 2), :, 1 - x], a_in.at[t], t, 1, over_x),
+            remote(h_buf.at[slot, pl.ds(2, 2), 1 - y], b_in.at[t], t, 2, over_y),
+        ]
+
+    def second_copies(t, slot):
+        return [
+            remote(a_buf.at[slot, :, 1 - y], a2_in.at[t], t, 3, over_y),
+            remote(b_buf.at[slot, :, 1 - x], b2_in.at[t], t, 4, over_x),
+        ]
+
+    def line_copies(t, slot):
+        copies = []
+        for k in (1, 2, 3):
+            to = lax.rem(z + k, 4)
+            there = (dp, to * 2 + core)
+            copies.append(remote(q_buf.at[slot, to], z_in.at[t, k - 1], t, 4 + k, there))
+        return copies
+
+    def share_copies(t, slot):
+        where = o_buf.at[t, dp]
+        return [remote(where, where, t, 8, over_x), remote(where, where, t, 9, over_y)]
+
+    def across_copies(t, slot):
+        one = o_buf.at[t, (1 - y) * 2 + x, pl.ds(0, PIECE // 2)]
+        two = o_buf.at[t, y * 2 + 1 - x, pl.ds(PIECE // 2, PIECE // 2)]
+        return [remote(one, one, t, 10, over_x), remote(two, two, t, 11, over_y)]
+
+    def finish(copies):
+        for copy in copies:
+            copy.wait()
+
+    def begin(copies):
+        for copy in copies:
+            copy.start()
+
+    def write_out(t, slot):
+        finish(across_copies(t, slot))
+        out[0] = f32(o_buf[t].reshape(128, 1024))
+
+    def pass_on(t, slot):
+        finish(share_copies(t, slot))
+        begin(across_copies(t, slot))
+
+    def total_line(t, slot):
+        finish(line_copies(t, slot))
+        total = f32(q_buf[slot, z]) + f32(z_in[t, 0]) + f32(z_in[t, 1]) + f32(z_in[t, 2])
+        o_buf[t, dp] = low(total)
+        begin(share_copies(t, slot))
+
+    def total_second(t, slot):
+        finish(second_copies(t, slot))
+        q_buf[slot, 0:2] = low(f32(a_buf[slot, :, y]) + f32(a2_in[t]))
+        q_buf[slot, 2:4] = low(f32(b_buf[slot, :, x]) + f32(b2_in[t]))
+        begin(line_copies(t, slot))
+
+    def total_first(t, slot):
+        finish(first_copies(t, slot))
+        a_buf[slot] = low(f32(h_buf[slot, 0:2, :, x]) + f32(a_in[t]))
+        b_buf[slot] = low(f32(h_buf[slot, 2:4, y]) + f32(b_in[t]))
+        begin(second_copies(t, slot))
+
+    def total_core(t, slot):
+        finish(core_copies(t, slot))
+        for i in range(4):
+            total = low(f32(g_buf[slot, 0, i]) + f32(core_in[t, i]))
+            h_buf[slot, i] = total.reshape(2, 2, PIECE, 1024)
+        begin(first_copies(t, slot))
+
+    def product(t, slot):
+        rows = left[0]
+        for i in range(8):
+            part = lax.dot_general(
+                rows[:, 128 * i : 128 * i + 128],
+                right[0],
+                (((0,), (0,)), ((), ())),
+                preferred_element_type=jnp.float32,
+            )
+            g_buf[slot, lax.rem(core + i, 2), i // 2] = low(part)
+        begin(core_copies(t, slot))
+
+    stages = [product, total_core, total_first, total_second, total_line, pass_on, write_out]
+    for depth in reversed(range(len(stages))):
+        t = step - LAG * depth
+
+        @pl.when((t >= 0) & (t < count))
+        def _(t=t, depth=depth):
+            stages[depth](t, lax.rem(t, LAG))
+
+    def vec_copies():
+        copies = []
+        for k, there in enumerate(peers):
+            copies.append(
+                pltpu.make_async_remote_copy(
+                    src_ref=vec.at[lax.rem(seq + k + 1, 8)],
+                    dst_ref=vec_in.at[seq],
+                    send_sem=vec_sem.at[0, k],
+                    recv_sem=vec_sem.at[1, k],
+                    device_id=there,
+                    device_id_type=MESH_ID,
+                )
+            )
+        return copies
+
+    def vec_dp_copies():
+        copies = []
+        for k, there in enumerate(dp_peers):
+            copies.append(
+                pltpu.make_async_remote_copy(
+                    src_ref=vec_dp.at[dp],
+                    dst_ref=vec_dp.at[dp],
+                    send_sem=vec_sem.at[0, 7 + k],
+                    recv_sem=vec_sem.at[1, 7 + k],
+                    device_id=there,
+                    device_id_type=MESH_ID,
+                )
+            )
+        return copies
+
+    @pl.when(step == 0)
+    def _():
+        begin(vec_copies())
+        vec_in[seq] = vec[seq]
+
+    @pl.when(step == 2)
+    def _():
+        finish(vec_copies())
+        total = vec_in[0]
+        for i in range(1, 8):
+            total = total + vec_in[i]
+        vec_dp[dp] = total
+        begin(vec_dp_copies())
+
+    @pl.when(step == 4)
+    def _():
+        finish(vec_dp_copies())
+        vec_out[...] = (vec_dp[0] + vec_dp[1]) + (vec_dp[2] + vec_dp[3])
+
+
+def reduce_grads(left, right, vec):
+    count, tokens, width = left.shape
+    bf16 = jnp.bfloat16
+    quarter = (PIECE, width)
+    return pl.pallas_call(
+        functools.partial(reduce_kernel, count),
+        grid=(count + 6 * LAG,),
+        in_specs=[
+            pl.BlockSpec((1, tokens, width), lambda t: (lax.min(t, count - 1), 0, 0)),
+            pl.BlockSpec((1, tokens, width), lambda t: (lax.min(t, count - 1), 0, 0)),
+            pl.BlockSpec(vec.shape, lambda t: (0, 0, 0)),
+        ],
+        out_specs=[
+            pl.BlockSpec((1, 128, width), lambda t: (lax.max(t - 6 * LAG, 0), 0, 0)),
+            pl.BlockSpec(vec.shape[1:], lambda t: (0, 0)),
+        ],
+        out_shape=[
+            jax.ShapeDtypeStruct((count, 128, width), jnp.float32),
+            jax.ShapeDtypeStruct(vec.shape[1:], jnp.float32),
+        ],
+        scratch_shapes=[
+            pltpu.VMEM((LAG, 2, 4, 128, width), bf16),
+            pltpu.VMEM((LAG, 4, 2, 2) + quarter, bf16),
+            pltpu.VMEM((LAG, 2, 2) + quarter, bf16),
+            pltpu.VMEM((LAG, 2, 2) + quarter, bf16),
+            pltpu.VMEM((LAG, 4) + quarter, bf16),
+            pltpu.VMEM((count, 4, 128, width), bf16),
+            pltpu.VMEM((count, 2, 2) + quarter, bf16),
+            pltpu.VMEM((count, 2, 2) + quarter, bf16),
+            pltpu.VMEM((count, 2) + quarter, bf16),
+            pltpu.VMEM((count, 2) + quarter, bf16),
+            pltpu.VMEM((count, 3) + quarter, bf16),
+            pltpu.VMEM((count, 4) + quarter, bf16),
+            pltpu.VMEM(vec.shape, jnp.float32),
+            pltpu.VMEM((4,) + vec.shape[1:], jnp.float32),
+            pltpu.SemaphoreType.DMA((2, 12, count)),
+            pltpu.SemaphoreType.DMA((2, 10)),
+        ],
+        compiler_params=pltpu.CompilerParams(
+            collective_id=1, has_side_effects=True, vmem_limit_bytes=56 * 2**20
+        ),
+        name="reduce_grads",
+    )(left, right, vec)
+
+
+def reduce_grad(halves, grad):
+    y, x, z, core = place()
+    cols = grad.shape[1]
+    part = halves[0].shape[1] // 16
+    away = jnp.einsum("td,tc->dc", halves[1], grad, preferred_element_type=jnp.float32)
+    away = away.astype(jnp.bfloat16)
+    keep = jnp.einsum("td,tc->dc", halves[0], grad, preferred_element_type=jnp.float32)
+    keep = keep.astype(jnp.bfloat16)
+    came = send(away, OVER_CORE)
+    keep = keep.reshape(2, 2, 2, 2, part, cols)
+    came = came.reshape(2, 2, 2, 2, part, cols)
+
+    def take(value, index, axis):
+        return pick(value, index, axis)
+
+    one_away = plus(take(keep[0], 1 - x, 2), take(came[0], 1 - x, 2))
+    two_away = plus(take(keep[1], 1 - y, 1), take(came[1], 1 - y, 1))
+    one_came = send(one_away, OVER_X)
+    two_came = send(two_away, OVER_Y)
+
+    def sum_one(iy):
+        total = take(take(keep[0], x, 2), iy, 1).astype(jnp.float32)
+        total += take(take(came[0], x, 2), iy, 1).astype(jnp.float32)
+        return (total + take(one_came, iy, 1).astype(jnp.float32)).astype(jnp.bfloat16)
+
+    def sum_two(ix):
+        total = take(take(keep[1], y, 1), ix, 1).astype(jnp.float32)
+        total += take(take(came[1], y, 1), ix, 1).astype(jnp.float32)
+        return (total + take(two_came, ix, 1).astype(jnp.float32)).astype(jnp.bfloat16)
+
+    one_next = send(sum_one(1 - y), OVER_Y)
+    two_next = send(sum_two(1 - x), OVER_X)
+    line = jnp.concatenate([plus(sum_one(y), one_next), plus(sum_two(x), two_next)])
+    total = pick(line, z, 0).astype(jnp.float32)
+    for k in (1, 2, 3):
+        total += send(pick(line, (z + k) % 4, 0), ALONG_Z[k]).astype(jnp.float32)
+    own = total.astype(jnp.bfloat16)
+    from_x = send(own, OVER_X)
+    from_y = send(own, OVER_Y)
+    across_one = send(from_y[: part // 2], OVER_X)
+    across_two = send(from_x[part // 2 :], OVER_Y)
+    across = jnp.concatenate([across_one, across_two])
+    low_x, high_x = jnp.where(x == 0, own, from_x), jnp.where(x == 0, from_x, own)
+    low_a, high_a = jnp.where(x == 0, from_y, across), jnp.where(x == 0, across, from_y)
+    parts = [
+        jnp.where(y == 0, low_x, low_a),
+        jnp.where(y == 0, high_x, high_a),
+        jnp.where(y == 0, low_a, low_x),
+        jnp.where(y == 0, high_a, high_x),
+    ]
+    return jnp.concatenate(parts).astype(jnp.float32)
+
+
+QUERIES = 256
+
+
+def log_distance_block(length, start):
+    keys = lax.broadcasted_iota(jnp.int32, (length, QUERIES), 0)
+    queries = lax.broadcasted_iota(jnp.int32, (length, QUERIES), 1) + start
+    return jnp.log(1.0 + jnp.abs(keys - queries).astype(jnp.float32))
+
+
+def head_lanes(value, head, scale=1.0):
+    lane = lax.broadcasted_iota(jnp.int32, value.shape, 1)
+    mine = (lane >= 64 * head) & (lane < 64 * head + 64)
+    return jnp.where(mine, value * jnp.asarray(scale, value.dtype), jnp.zeros_like(value))
+
+
+def nt(a, b):
+    return lax.dot_general(a, b, (((1,), (1,)), ((), ())), preferred_element_type=jnp.float32)
+
+
+def attend_kernel(slopes, key_seg, query_seg, q_ref, k_ref, v_ref, out_ref):
+    length = key_seg.shape[1]
+    distance = log_distance_block(length, pl.program_id(1) * QUERIES)
+    same = key_seg[0] == query_seg[0]
+    q = q_ref[...].reshape(QUERIES, 128)
+    k = k_ref[...].reshape(length, 128)
+    value_t = v_ref[...].reshape(length, 128).T
+    outs = []
+    for head in range(2):
+        logit = nt(k, head_lanes(q, head, 0.125)) - slopes[head] * distance
+        logit = jnp.where(same, logit, -1e30)
+        top = jnp.max(logit, axis=0, keepdims=True)
+        power = jnp.exp(logit - top)
+        total = jnp.sum(power, axis=0, keepdims=True)
+        out = jnp.dot(value_t, power.astype(jnp.bfloat16), preferred_element_type=jnp.float32)
+        outs.append(out[64 * head : 64 * head + 64] / total)
+    out = jnp.concatenate(outs, axis=0).T
+    out_ref[...] = out.astype(jnp.bfloat16).reshape(out_ref.shape)
+
+
+def attend_back_kernel(
+    slopes, key_seg, query_seg, q_ref, k_ref, v_ref, g_ref, out_ref, slope_ref, key_sum, value_sum
+):
+    length = key_seg.shape[1]
+    step = pl.program_id(1)
+    distance = log_distance_block(length, step * QUERIES)
+    same = key_seg[0] == query_seg[0]
+    q = q_ref[...].reshape(QUERIES, 128)
+    k = k_ref[...].reshape(length, 128)
+    v = v_ref[...].reshape(length, 128)
+    g = g_ref[...].reshape(QUERIES, 128)
+    key_t = k.T
+
+    @pl.when(step == 0)
+    def _():
+        key_sum[...] = jnp.zeros_like(key_sum)
+        value_sum[...] = jnp.zeros_like(value_sum)
+        slope_ref[...] = jnp.zeros_like(slope_ref)
+
+    outs = []
+    for head in range(2):
+        q_head = head_lanes(q, head, 0.125)
+        g_head = head_lanes(g, head)
+        logit = nt(k, q_head) - slopes[head] * distance
+        logit = jnp.where(same, logit, -1e30)
+        top = jnp.max(logit, axis=0, keepdims=True)
+        power = jnp.exp(logit - top)
+        prob = power * (1.0 / jnp.sum(power, axis=0, keepdims=True))
+        prob_grad = nt(v, g_head)
+        delta = jnp.sum(prob * prob_grad, axis=0, keepdims=True)
+        logit_grad = prob * (prob_grad - delta)
+        slope = jnp.sum(logit_grad * distance, axis=0, keepdims=True)
+        slope_ref[0, head : head + 1, :] -= slope
+        low = logit_grad.astype(jnp.bfloat16)
+        key_sum[...] += jnp.dot(low, q_head, preferred_element_type=jnp.float32)
+        value_sum[...] += jnp.dot(
+            prob.astype(jnp.bfloat16), g_head, preferred_element_type=jnp.float32
+        )
+        query_t = jnp.dot(key_t, low, preferred_element_type=jnp.float32)
+        outs.append(query_t[64 * head : 64 * head + 64] * 0.125)
+    query = jnp.concatenate(outs, axis=0).T.astype(jnp.bfloat16)
+    blocks = QUERIES // 128
+    out_ref[pl.ds(step * blocks, blocks), 0, 0] = query.reshape(blocks, 128, 128)
+
+    @pl.when(step == pl.num_programs(1) - 1)
+    def _():
+        out_ref[:, 1, 0] = key_sum[...].astype(jnp.bfloat16).reshape(length // 128, 128, 128)
+        out_ref[:, 2, 0] = value_sum[...].astype(jnp.bfloat16).reshape(length // 128, 128, 128)
+
+
+def attend_specs(peers, frames):
+    length = peers * frames
+    blocks = QUERIES // frames
+    return [
+        pl.BlockSpec(memory_space=pltpu.SMEM),
+        pl.BlockSpec((1, length, 1), lambda r, i: (r, 0, 0)),
+        pl.BlockSpec((1, 1, QUERIES), lambda r, i: (r, 0, i)),
+        pl.BlockSpec((blocks, 1, 1, frames, 128), lambda r, i: (i, 0, r, 0, 0)),
+        pl.BlockSpec((peers, 1, 1, frames, 128), lambda r, i: (0, 1, r, 0, 0)),
+        pl.BlockSpec((peers, 1, 1, frames, 128), lambda r, i: (0, 2, r, 0, 0)),
+    ]
+
+
+def attend(slopes, segment_row, packed):
+    peers, _, rows, frames, _ = packed.shape
+    length = peers * frames
+    blocks = QUERIES // frames
+    pairs = rows * length * length * 2
+    return pl.pallas_call(
+        attend_kernel,
+        grid=(rows, length // QUERIES),
+        in_specs=attend_specs(peers, frames),
+        out_specs=pl.BlockSpec((blocks, 1, frames, 128), lambda r, i: (i, r, 0, 0)),
+        out_shape=jax.ShapeDtypeStruct((peers, rows, frames, 128), jnp.bfloat16),
+        compiler_params=pltpu.CompilerParams(vmem_limit_bytes=48 * 2**20),
+        cost_estimate=pl.CostEstimate(
+            flops=pairs * 512, bytes_accessed=packed.size * 3, transcendentals=pairs
+        ),
+        name="attend",
+    )(slopes, segment_row[:, :, None], segment_row[:, None, :], packed, packed, packed)
+
+
+def attend_back(slopes, segment_row, packed, grads):
+    peers, _, rows, frames, _ = packed.shape
+    length = peers * frames
+    blocks = QUERIES // frames
+    pairs = rows * length * length * 2
+    return pl.pallas_call(
+        attend_back_kernel,
+        grid=(rows, length // QUERIES),
+        in_specs=attend_specs(peers, frames)
+        + [pl.BlockSpec((blocks, 1, frames, 128), lambda r, i: (i, r, 0, 0))],
+        out_specs=[
+            pl.BlockSpec((peers, 3, 1, frames, 128), lambda r, i: (0, 0, r, 0, 0)),
+            pl.BlockSpec((1, 2, QUERIES), lambda r, i: (r, 0, 0)),
+        ],
+        out_shape=[
+            jax.ShapeDtypeStruct(packed.shape, jnp.bfloat16),
+            jax.ShapeDtypeStruct((rows, 2, QUERIES), jnp.float32),
+        ],
+        scratch_shapes=[pltpu.VMEM((length, 128), jnp.float32)] * 2,
+        compiler_params=pltpu.CompilerParams(vmem_limit_bytes=56 * 2**20),
+        cost_estimate=pl.CostEstimate(
+            flops=pairs * 1280, bytes_accessed=packed.size * 5, transcendentals=pairs
+        ),
+        name="attend_back",
+    )(slopes, segment_row[:, :, None], segment_row[:, None, :], packed, packed, packed, grads)
+
+
+def to_heads(value, count, rows, frames):
+    peers = lax.axis_size("seq")
+    value = value.reshape(rows, frames, count, peers, 128).transpose(3, 2, 0, 1, 4)
+    return lax.all_to_all(value, "seq", 0, 0, tiled=True)
+
+
+def from_heads(value):
+    peers, count, rows, frames, _ = value.shape
+    value = lax.all_to_all(value, "seq", 0, 0, tiled=True)
+    return value.transpose(2, 3, 1, 0, 4).reshape(rows * frames, count * peers * 128)
+
+
+def silu_back(pre, grad):
+    gate = jax.nn.sigmoid(pre)
+    return grad * gate * (1.0 + pre * (1.0 - gate))
+
+
+def half_layer(stream, gain, bias, up, down):
+    normed, pull = jax.vjp(layer_norm, stream, gain, bias)
+    normed = split_cols(normed.astype(jnp.bfloat16))
+    pre = mul(normed, up)
+    hidden = split_cols(jax.nn.silu(pre).astype(jnp.bfloat16))
+    return stream + 0.5 * mul(hidden, down), (pull, normed, pre, hidden)
+
+
+def half_layer_back(grad, saved, up, down):
+    pull, normed, pre, hidden = saved
+    branch = (0.5 * grad).astype(jnp.bfloat16)
+    hidden_grad = mul_back(branch, down)
+    pre_grad = silu_back(pre, hidden_grad).astype(jnp.bfloat16)
+    stream_grad, gain_grad, bias_grad = pull(mul_back(pre_grad, up))
+    return grad + stream_grad, gain_grad, bias_grad, (normed, pre_grad), (hidden, branch)
+
+
+def body_staged(
+    frames,
+    segments,
+    cotangent,
+    norm_gains,
+    norm_biases,
+    front_up,
+    front_down,
+    attend_in,
+    attend_out,
+    slopes,
+    point_in,
+    depthwise,
+    point_out,
+    rear_up,
+    rear_down,
+):
+    row_count, frame_count, width = frames.shape
+    token_count = row_count * frame_count
+    seq = lax.axis_index("seq")
+    query_start = seq * frame_count
+    taps = depthwise.shape[0]
+    half_k = taps // 2
+
+    vector_shard = jnp.concatenate([norm_gains, norm_biases, depthwise])
+    vector_shard = jnp.pad(vector_shard, ((0, 48 - vector_shard.shape[0]), (0, 0)))
+    segment_shard = jnp.pad(segments, ((0, 8 - row_count), (0, 0)))
+    front_up_w, front_down_w, attend_in_w, vectors, segment_row = gather_front(
+        front_up, front_down, attend_in, vector_shard, segment_shard
+    )
+    vectors = vectors.transpose(1, 0, 2).reshape(48, width).astype(jnp.float32)
+    gains, biases, depth = vectors[:6], vectors[6:12], vectors[12 : 12 + taps]
+    segment_row = segment_row[:, :row_count].transpose(1, 0, 2).reshape(row_count, -1)
+    front_up_w = front_up_w.reshape(width, -1)
+    front_down_w = front_down_w.reshape(-1, width)
+    attend_in_w = attend_in_w.reshape(width, -1)
+
+    middle = jnp.concatenate([attend_out, point_in, point_out], axis=1)
+    middle, rear_up, rear_down, front_up_w, front_down_w, attend_in_w = lax.optimization_barrier(
+        (middle, rear_up, rear_down, front_up_w, front_down_w, attend_in_w)
+    )
+    middle_w = gather_halves(middle)
+    attend_out_w = tuple(w[:, :width] for w in middle_w)
+    point_in_w = tuple(w[:, width : 3 * width] for w in middle_w)
+    point_out_w = tuple(w[:, 3 * width :] for w in middle_w)
+    rear_up_w = gather_halves(rear_up)
+    rear_down_w = gather_halves(rear_down)
+
+    stream = frames.astype(jnp.float32).reshape(token_count, width)
+    after_front, front_saved = half_layer(stream, gains[0], biases[0], front_up_w, front_down_w)
+
+    attend_norm, attend_pull = jax.vjp(layer_norm, after_front, gains[1], biases[1])
+    attend_norm = split_cols(attend_norm.astype(jnp.bfloat16))
+    projected = mul(attend_norm, attend_in_w).astype(jnp.bfloat16)
+    packed = to_heads(projected, 3, row_count, frame_count)
+    my_slopes = lax.dynamic_slice_in_dim(slopes, seq * 2, 2, 0)
+    heads_out = attend(my_slopes, segment_row, packed)
+    attended = split_cols(from_heads(heads_out[:, None]))
+    after_attend = after_front + mul(attended, attend_out_w)
+
+    conv_norm, conv_pull = jax.vjp(layer_norm, after_attend, gains[2], biases[2])
+    conv_norm = split_cols(conv_norm.astype(jnp.bfloat16))
+    conv_pre = mul(conv_norm, point_in_w)
+
+    def gate_unit(inner_act):
+        return inner_act[:, :width] * jax.nn.sigmoid(inner_act[:, width:])
+
+    gated, gate_pull = jax.vjp(gate_unit, conv_pre)
+    gated_low = gated.astype(jnp.bfloat16).reshape(row_count, frame_count, width)
+    gated_wide = padded(gated_low, (("seq", 1),), half_k).astype(jnp.float32)
+    padded_seg = jnp.pad(segment_row, ((0, 0), (half_k, half_k)), constant_values=-1)
+    seg_window = lax.dynamic_slice_in_dim(padded_seg, query_start, frame_count + 2 * half_k, 1)
+    same_list = [
+        (seg_window[:, offset : offset + frame_count] == segments)[..., None]
+        for offset in range(taps)
+    ]
+    mixed = jnp.zeros((row_count, frame_count, width), jnp.float32)
+    for offset in range(taps):
+        mixed = mixed + jnp.where(
+            same_list[offset], depth[offset] * gated_wide[:, offset : offset + frame_count], 0.0
+        )
+
+    def norm_silu(stream, norm_gain, norm_bias):
+        return jax.nn.silu(layer_norm(stream, norm_gain, norm_bias))
+
+    activated, activated_pull = jax.vjp(
+        norm_silu, mixed.reshape(token_count, width), gains[3], biases[3]
+    )
+    activated = split_cols(activated.astype(jnp.bfloat16))
+    after_conv = after_attend + mul(activated, point_out_w)
+    after_rear, rear_saved = half_layer(after_conv, gains[4], biases[4], rear_up_w, rear_down_w)
+    final_out, final_pull = jax.vjp(layer_norm, after_rear, gains[5], biases[5])
+    result = final_out.astype(jnp.bfloat16).reshape(row_count, frame_count, width)
+
+    grad_rear, gain_five, bias_five = final_pull(
+        cotangent.astype(jnp.float32).reshape(token_count, width)
+    )
+    grad_conv, gain_four, bias_four, rear_up_terms, rear_down_terms = half_layer_back(
+        grad_rear, rear_saved, rear_up_w, rear_down_w
+    )
+    rear_down_grad = reduce_grad(*rear_down_terms)
+    rear_up_grad = reduce_grad(*rear_up_terms)
+    conv_branch = grad_conv.astype(jnp.bfloat16)
+    mixed_grad, gain_three, bias_three = activated_pull(mul_back(conv_branch, point_out_w))
+    mixed_low = mixed_grad.astype(jnp.bfloat16).reshape(row_count, frame_count, width)
+    grad_wide = padded(mixed_low, (("seq", 1),), half_k).astype(jnp.float32)
+    mixed_back = mixed_low.astype(jnp.float32)
+    depth_grad = jnp.stack(
+        [
+            jnp.sum(
+                jnp.where(
+                    same_list[offset],
+                    mixed_back * gated_wide[:, offset : offset + frame_count],
+                    0.0,
+                ),
+                axis=(0, 1),
+            )
+            for offset in range(taps)
+        ]
+    )
+    gated_grad = jnp.zeros((row_count, frame_count, width), jnp.float32)
+    for offset in range(taps):
+        mirror = 2 * half_k - offset
+        gated_grad = gated_grad + jnp.where(
+            same_list[mirror], depth[offset] * grad_wide[:, mirror : mirror + frame_count], 0.0
+        )
+    pre_grad = gate_pull(gated_grad.reshape(token_count, width))[0].astype(jnp.bfloat16)
+    conv_stream_grad, gain_two, bias_two = conv_pull(mul_back(pre_grad, point_in_w))
+    grad_attend = grad_conv + conv_stream_grad
+
+    attend_branch = grad_attend.astype(jnp.bfloat16)
+    attended_grad = mul_back(attend_branch, attend_out_w).astype(jnp.bfloat16)
+    head_grads = to_heads(attended_grad, 1, row_count, frame_count)[:, 0]
+    packed_grad, slope_parts = attend_back(my_slopes, segment_row, packed, head_grads)
+    projected_grad = from_heads(packed_grad)
+    attend_stream_grad, gain_one, bias_one = attend_pull(mul_back(projected_grad, attend_in_w))
+    grad_front = grad_attend + attend_stream_grad
+    start_grad, gain_zero, bias_zero, front_up_terms, front_down_terms = half_layer_back(
+        grad_front, front_saved, front_up_w, front_down_w
+    )
+    frames_grad = start_grad.astype(jnp.bfloat16).reshape(row_count, frame_count, width)
+
+    small = jnp.concatenate(
+        [
+            jnp.stack([gain_zero, gain_one, gain_two, gain_three, gain_four, gain_five]),
+            jnp.stack([bias_zero, bias_one, bias_two, bias_three, bias_four, bias_five]),
+            depth_grad,
+            jnp.zeros((48 - 12 - taps, width), jnp.float32),
+        ]
+    )
+    peers = lax.axis_size("seq")
+    small = small.reshape(48, peers, width // peers).transpose(1, 0, 2)
+    my_slope_grad = jnp.sum(slope_parts, axis=(0, 2))
+    slope_row = jnp.zeros((peers, 1, width // peers), jnp.float32)
+    slope_row = lax.dynamic_update_slice(
+        slope_row, jnp.broadcast_to(my_slope_grad, (peers, 1, 2)), (0, 0, seq * 2)
+    )
+    small = lax.dynamic_update_slice(small, slope_row, (0, 12 + taps, 0))
+
+    def wide(terms):
+        left, right = merge_cols(*terms[0]), terms[1]
+        blocks = right.shape[1] // width
+        return [(left, right[:, i * width : (i + 1) * width]) for i in range(blocks)]
+
+    def tall(terms):
+        left, right = merge_cols(*terms[0]), terms[1]
+        blocks = left.shape[1] // width
+        left = left.reshape(token_count, peers, blocks, width // peers)
+        return [(left[:, :, i].reshape(token_count, width), right) for i in range(blocks)]
+
+    jobs = wide((attended, attend_branch)) + wide((conv_norm, pre_grad))
+    jobs += wide((activated, conv_branch)) + wide((attend_norm, projected_grad))
+    jobs += tall(front_down_terms) + wide(front_up_terms)
+    shares, share = reduce_grads(
+        jnp.stack([job[0] for job in jobs]), jnp.stack([job[1] for job in jobs]), small
+    )
+
+    def beside(first, count):
+        return jnp.concatenate([shares[first + i] for i in range(count)], axis=1)
+
+    attend_out_grad, point_in_grad, point_out_grad = shares[0], beside(1, 2), shares[3]
+    attend_in_grad = beside(4, 3)
+    front_down_grad = shares[7:11].reshape(-1, width)
+    front_up_grad = beside(11, 4)
+    return (
+        result,
+        frames_grad,
+        share[:6],
+        share[6:12],
+        front_up_grad,
+        front_down_grad,
+        attend_in_grad,
+        attend_out_grad,
+        share[12 + taps, : slopes.shape[0]],
+        point_in_grad,
+        share[12 : 12 + taps],
+        point_out_grad,
+        rear_up_grad,
+        rear_down_grad,
+    )
+
+
 def solution(mesh):
     placed = (
         P("dp", "seq", None),
@@ -470,8 +1394,10 @@
         P("seq", None),
         P("seq", None),
     )
+    sizes = mesh.shape
+    staged = sizes["dp"] == 4 and sizes["seq"] == 8
     return jax.shard_map(
-        body,
+        body_staged if staged else body,
         mesh=mesh,
         in_specs=placed,
         out_specs=(

time: 1740 us -> 886 us (0.51)
  waiting for transfers between devices: 1170 us -> 139 us
  Pallas kernels: 0 us -> 345 us
  matrix products: 233 us -> 92 us
  blocking collectives: 79.5 us -> 0 us
  starting transfers between devices: 42.3 us -> 115 us
  other arithmetic: 123 us -> 62.1 us
  local copies, waits for them, and re-layouts: 61.1 us -> 119 us
    all_gather x10 -> x0, waiting for transfers between devices: 431 us -> none  [the longest x1 81 us: body(): lax.all_gather(rear_up, 'seq', axis=0, tiled=True)]
    reduce_scatter x8 -> x0, waiting for transfers between devices: 365 us -> none  [the longest x1 90.2 us: body(): lax.psum_scatter(rear_down_grad.astype(jnp.bfloat16), 'seq', scatter_dime...]
    pallas_call x0 -> x7, Pallas kernels: none -> 345 us  [the longest x1 183 us: reduce_grads(): pl.pallas_call(functools.partial(reduce_kernel, count), grid=(count + 6 *...]
    dot_general x74 -> x30, matrix products: 233 us -> 92 us  [the longest x3 15.6 us: mul_back(): jnp.einsum('tc,dc->td', grad, weight, preferred_element_type=jnp.float32)]
    psum x1 -> x0, waiting for transfers between devices: 121 us -> none  [body(): lax.psum(shares[2].astype(jnp.bfloat16), 'dp').astype(jnp.float32)]
    unnamed x25 -> x0, waiting for transfers between devices: 81.9 us -> none
    ppermute x15 -> x48, waiting for transfers between devices: 169 us -> 101 us  [send(): return lax.ppermute(value, ('dp', 'seq'), pairs)]
    ppermute x15 -> x48, starting transfers between devices: 32.3 us -> 87 us  [send(): return lax.ppermute(value, ('dp', 'seq'), pairs)]
  transfers between devices with their start and end apart: 41 -> 56, of which waited for: 35 -> 17; matrix products, arithmetic and copies ran while one was open for 21% -> 24% of each run, Pallas kernels for 0% -> 27%
where the time goes in v1:
time: 886 us; the launch traced here: 876 us
  Pallas kernels  345 us (39%)
  waiting for transfers between devices  139 us (16%)
  local copies, waits for them, and re-layouts  119 us (13%)
  starting transfers between devices  115 us (13%)
  matrix products  92 us (10%)
  other arithmetic  62.1 us (7%)
    pallas_call x1, Pallas kernels, reduce_grads(): pl.pallas_call(functools.partial(reduce_kernel, count), grid=(count + 6 *...  183 us
    pallas_call x1, Pallas kernels, gather_front(): pl.pallas_call(gather_kernel, in_specs=[pl.BlockSpec(memory_space=pltpu.H...  104 us
    ppermute x48, waiting for transfers between devices, send(): return lax.ppermute(value, ('dp', 'seq'), pairs)  101 us
    ppermute x48, starting transfers between devices, send(): return lax.ppermute(value, ('dp', 'seq'), pairs)  87 us
    unnamed x449, local copies, waits for them, and re-layouts  49.9 us
    pallas_call x1, Pallas kernels, attend_back(): pl.pallas_call(attend_back_kernel, grid=(rows, length // QUERIES), in_spe...  28.4 us
    all_to_all x2, waiting for transfers between devices, from_heads(): value = lax.all_to_all(value, 'seq', 0, 0, tiled=True)  26.2 us
  transfers between devices with their start and end apart: 56, of which 17 were waited for; matrix products, arithmetic and copies ran while one was open for 24% of the time, Pallas kernels for 27%

profile of v1, /device:TPU:0, one launch (start us, length us, event | category | flops | bytes accessed | tf_op | source)
XLA Modules:
  0.0 876.1 jit_solution(2724629658003209788)
XLA Ops:
  4.5 104.1 %gather_front.1 = (bf16[8,128,4096]{2,1,0:T(8,128)(2,1)}, bf16[8,512,1024]{2,1,0:T(8,128)(2,1)}, bf16[8,128,3072]{2,1,0:T(8,128)(2,1)}, bf16[8,48,128]{2,1,0:T(8,128)(2,1)}, s32[8,8,128]{2,1,0:T(8,128)}) custom-call(bf16[128,4096]{1,0:T(8,128)(2,1)} %refs_0_.1, bf16[512,1024]{1,0:T(8,128)(2,1)} %refs_1_.1, bf16[128,3072]{1,0:T(8,128)(2,1)} %refs_2_.1, ...), custom_call_target="tpu_custom_call" | custom-call | tf_op jit(solution)/shard_map/gather_front/pallas_call | solution.py:607
  117.2 8.1 multiply_convert_fusion.2
  134.2 5.1 all-to-all-start
  148.1 4.4 reshape.863
  154.4 5.0 collective-permute-done.4.over_y
  164.5 7.1 collective-permute-done.20
  171.6 35.2 %collective-permute-start.10 = (bf16[32,4096]{1,0:T(8,128)(2,1)}, bf16[32,4096]{1,0:T(8,128)(2,1)}, u32[]{:S(2)}, u32[]{:S(2)}) collective-permute-start(bf16[32,4096]{1,0:T(8,128)(2,1)} %constant_dynamic-slice_fusion.39), channel_id=1, source_target_pairs={{0,2},{1,3},{2,4},{3,5},{4,6},{5,7},{6,0},{7,1},{8,10},{9,11},{10,... | collective-permute-start | bytes 786440 | tf_op jit(solution)/shard_map/ppermute | solution.py:482
  206.8 4.6 collective-permute-done.19
  213.5 4.5 fusion.272
  224.0 4.6 place.3
  235.4 15.3 %attend.1 = bf16[8,2,128,128]{3,2,1,0:T(8,128)(2,1)S(1)} custom-call(f32[2]{0:T(128)S(1)} %dynamic_slice.159.slopes, s32[2,1024,1]{2,1,0:T(8,128)S(1)} %copy-done.6, s32[2,1,1024]{2,1,0:T(1,128)S(1)} %bitcast.459, bf16[8,3,2,128,128]{4,3,2,1,0:T(8,128)(2,1)} %all-to-all-done.q_ref.k_ref.v_ref, bf16[8,3,2,128,128]{4,3,2,1,0:T(8,128)(2,1)} %all-to-all-done.q_ref.k_ref.v_ref, ...), custom_call_target="tpu_custom_call" | custom-call | flops 2147483648 | bytes 2359296 | tf_op jit(solution)/shard_map/attend/pallas_call | solution.py:1102
  251.5 4.1 all-to-all-start.1
  292.8 4.8 place.5
  297.6 4.8 place.4
  321.7 6.3 fusion.267
  336.7 3.9 multiply_convert_fusion.1
  391.1 4.8 collective-permute-start.26
  409.7 6.0 fusion.85
  428.8 4.5 all-to-all-start.2
  439.2 9.6 %all-to-all-done.2 = bf16[8,1,2,128,128]{4,3,2,1,0:T(8,128)(2,1)} async-done(((bf16[8,1,2,128,128]{4,3,2,1,0:T(8,128)(2,1)}), bf16[8,1,2,128,128]{4,3,2,1,0:T(8,128)(2,1)}, u32[]{:S(2)}, u32[]{:S(2)}) %all-to-all-start.2) | async-done | bytes 524320 | tf_op jit(solution)/shard_map/all_to_all | solution.py:1146
  448.8 28.4 %attend_back.1 = (bf16[8,3,2,128,128]{4,3,2,1,0:T(8,128)(2,1)}, f32[2,2,256]{2,1,0:T(2,128)}) custom-call(f32[2]{0:T(128)} %copy-done.9, s32[2,1024,1]{2,1,0:T(8,128)} %copy.99.key_seg, s32[2,1,1024]{2,1,0:T(1,128)} %bitcast.460, bf16[8,3,2,128,128]{4,3,2,1,0:T(8,128)(2,1)} %all-to-all-done.q_ref.k_ref.v_ref, ...), custom_call_target="tpu_custom_call" | custom-call | flops 5368709120 | bytes 3932160 | tf_op jit(solution)/shard_map/attend_back/pallas_call | solution.py:1121
  477.3 4.5 all-to-all-start.3
  493.4 26.2 %all-to-all-done.3 = bf16[8,3,2,128,128]{4,3,2,1,0:T(8,128)(2,1)} async-done(((bf16[8,3,2,128,128]{4,3,2,1,0:T(8,128)(2,1)}), bf16[8,3,2,128,128]{4,3,2,1,0:T(8,128)(2,1)}, u32[]{:S(2)}, u32[]{:S(2)}) %all-to-all-start.3) | async-done | bytes 1572896 | tf_op jit(solution)/shard_map/all_to_all | solution.py:1151
  526.9 6.0 multiply_reduce_fusion.3
  538.0 6.6 fusion.1
  558.3 182.8 %reduce_grads.1 = (f32[15,128,1024]{2,1,0:T(8,128)}, f32[48,128]{1,0:T(8,128)}) custom-call(bf16[15,256,1024]{2,1,0:T(8,128)(2,1)} %bitcast_dynamic-update-slice_fusion.9.left, bf16[15,256,1024]{2,1,0:T(8,128)(2,1)} %fusion.177.right, f32[8,48,128]{2,1,0:T(8,128)} %copy-done.39), custom_call_target="tpu_custom_call" | custom-call | tf_op jit(solution)/shard_map/reduce_grads/pallas_call | solution.py:901
  741.1 4.2 slice_bitcast_fusion.9
  763.0 15.7 %collective-permute-done.41 = bf16[2,2,128,1024]{3,2,0,1:T(8,128)(2,1)S(1)} collective-permute-done((bf16[2,2,128,1024]{3,2,0,1:T(8,128)(2,1)S(1)}, bf16[2,2,128,1024]{3,2,0,1:T(8,128)(2,1)S(1)}, u32[]{:S(2)}, u32[]{:S(2)}) %collective-permute-start.41) | collective-permute-done | bytes 1048608 | tf_op jit(solution)/shard_map/ppermute | solution.py:482
  780.4 17.3 %collective-permute-done.29 = bf16[2,2,32,4096]{3,2,0,1:T(8,128)(2,1)S(1)} collective-permute-done((bf16[2,2,32,4096]{3,2,0,1:T(8,128)(2,1)S(1)}, bf16[2,2,32,4096]{3,2,0,1:T(8,128)(2,1)S(1)}, u32[]{:S(2)}, u32[]{:S(2)}) %collective-permute-start.29) | collective-permute-done | bytes 1048608 | tf_op jit(solution)/shard_map/ppermute | solution.py:482
  804.6 13.2 %collective-permute-done.30 = bf16[2,32,4096]{2,1,0:T(8,128)(2,1)S(1)} collective-permute-done((bf16[2,32,4096]{2,1,0:T(8,128)(2,1)S(1)}, bf16[2,32,4096]{2,1,0:T(8,128)(2,1)S(1)}, u32[]{:S(2)}, u32[]{:S(2)}) %collective-permute-start.30) | collective-permute-done | bytes 524320 | tf_op jit(solution)/shard_map/ppermute | solution.py:482
  829.8 16.6 %collective-permute-done.34 = bf16[32,4096]{1,0:T(8,128)(2,1)S(1)} collective-permute-done((bf16[32,4096]{1,0:T(8,128)(2,1)S(1)}, bf16[32,4096]{1,0:T(8,128)(2,1)S(1)}, u32[]{:S(2)}, u32[]{:S(2)}) %collective-permute-start.34) | collective-permute-done | bytes 262176 | tf_op jit(solution)/shard_map/ppermute | solution.py:482
  847.0 10.5 %collective-permute-done.46 = bf16[128,1024]{1,0:T(8,128)(2,1)S(1)} collective-permute-done((bf16[128,1024]{1,0:T(8,128)(2,1)S(1)}, bf16[128,1024]{1,0:T(8,128)(2,1)S(1)}, u32[]{:S(2)}, u32[]{:S(2)}) %collective-permute-start.46) | collective-permute-done | bytes 262176 | tf_op jit(solution)/shard_map/ppermute | solution.py:482
  (752 shorter events, 292.4 us)
Async XLA Ops:
  108.7 30.6 %collective-permute-start.2 = (bf16[32,4096]{1,0:T(8,128)(2,1)S(1)}, bf16[32,4096]{1,0:T(8,128)(2,1)S(1)}, u32[]{:S(2)}, u32[]{:S(2)}) collective-permute-start(bf16[32,4096]{1,0:T(8,128)(2,1)S(1)} %constant_dynamic-slice_fusion.41), channel_id=1, source_target_pairs={{0,6},{1,7},{2,0},{3,1},{4,2},{5,3},{6,4},{7,5},{8,14},{9,15},{10,... | collective-permute-start | bytes 786440 | tf_op jit(solution)/shard_map/ppermute | solution.py:482
  112.4 26.9 %collective-permute-start.1 = (bf16[32,4096]{1,0:T(8,128)(2,1)S(1)}, bf16[32,4096]{1,0:T(8,128)(2,1)S(1)}, u32[]{:S(2)}, u32[]{:S(2)}) collective-permute-start(bf16[32,4096]{1,0:T(8,128)(2,1)S(1)} %constant_dynamic-slice_fusion.41), channel_id=1, source_target_pairs={{0,4},{1,5},{2,6},{3,7},{4,0},{5,1},{6,2},{7,3},{8,12},{9,13},{10,... | collective-permute-start | bytes 786440 | tf_op jit(solution)/shard_map/ppermute | solution.py:482
  134.2 100.0 %all-to-all-start = ((bf16[8,3,2,128,128]{4,3,2,1,0:T(8,128)(2,1)}), bf16[8,3,2,128,128]{4,3,2,1,0:T(8,128)(2,1)}, u32[]{:S(2)}, u32[]{:S(2)}) async-start(bf16[8,3,2,128,128]{4,3,2,1,0:T(8,128)(2,1)} %bitcast.455), calls=%async_computation | async-start | bytes 3145728 | tf_op jit(solution)/shard_map/all_to_all | solution.py:1146
  143.2 28.5 %collective-permute-start.20 = (bf16[128,1024]{1,0:T(8,128)(2,1)}, bf16[128,1024]{1,0:T(8,128)(2,1)}, u32[]{:S(2)}, u32[]{:S(2)}) collective-permute-start(bf16[128,1024]{1,0:T(8,128)(2,1)} %constant_dynamic-slice_fusion.38), channel_id=1, source_target_pairs={{0,6},{1,7},{2,0},{3,1},{4,2},{5,3},{6,4},{7,5},{8,14},{9,15},{10,... | collective-permute-start | bytes 786440 | tf_op jit(solution)/shard_map/ppermute | solution.py:482
  147.0 64.5 %collective-permute-start.19 = (bf16[128,1024]{1,0:T(8,128)(2,1)}, bf16[128,1024]{1,0:T(8,128)(2,1)}, u32[]{:S(2)}, u32[]{:S(2)}) collective-permute-start(bf16[128,1024]{1,0:T(8,128)(2,1)} %constant_dynamic-slice_fusion.38), channel_id=1, source_target_pairs={{0,4},{1,5},{2,6},{3,7},{4,0},{5,1},{6,2},{7,3},{8,12},{9,13},{10,... | collective-permute-start | bytes 786440 | tf_op jit(solution)/shard_map/ppermute | solution.py:482
  147.0 65.9 %collective-permute-start.18 = (bf16[128,1024]{1,0:T(8,128)(2,1)}, bf16[128,1024]{1,0:T(8,128)(2,1)}, u32[]{:S(2)}, u32[]{:S(2)}) collective-permute-start(bf16[128,1024]{1,0:T(8,128)(2,1)} %constant_dynamic-slice_fusion.38), channel_id=1, source_target_pairs={{0,2},{1,3},{2,4},{3,5},{4,6},{5,7},{6,0},{7,1},{8,10},{9,11},{10,... | collective-permute-start | bytes 786440 | tf_op jit(solution)/shard_map/ppermute | solution.py:482
  159.4 69.2 %collective-permute-start.12 = (bf16[32,4096]{1,0:T(8,128)(2,1)}, bf16[32,4096]{1,0:T(8,128)(2,1)}, u32[]{:S(2)}, u32[]{:S(2)}) collective-permute-start(bf16[32,4096]{1,0:T(8,128)(2,1)} %constant_dynamic-slice_fusion.39), channel_id=1, source_target_pairs={{0,6},{1,7},{2,0},{3,1},{4,2},{5,3},{6,4},{7,5},{8,14},{9,15},{10,... | collective-permute-start | bytes 786440 | tf_op jit(solution)/shard_map/ppermute | solution.py:482
  163.7 65.0 %collective-permute-start.11 = (bf16[32,4096]{1,0:T(8,128)(2,1)}, bf16[32,4096]{1,0:T(8,128)(2,1)}, u32[]{:S(2)}, u32[]{:S(2)}) collective-permute-start(bf16[32,4096]{1,0:T(8,128)(2,1)} %constant_dynamic-slice_fusion.39), channel_id=1, source_target_pairs={{0,4},{1,5},{2,6},{3,7},{4,0},{5,1},{6,2},{7,3},{8,12},{9,13},{10,... | collective-permute-start | bytes 786440 | tf_op jit(solution)/shard_map/ppermute | solution.py:482
  171.6 57.1 %collective-permute-start.10 = (bf16[32,4096]{1,0:T(8,128)(2,1)}, bf16[32,4096]{1,0:T(8,128)(2,1)}, u32[]{:S(2)}, u32[]{:S(2)}) collective-permute-start(bf16[32,4096]{1,0:T(8,128)(2,1)} %constant_dynamic-slice_fusion.39), channel_id=1, source_target_pairs={{0,2},{1,3},{2,4},{3,5},{4,6},{5,7},{6,0},{7,1},{8,10},{9,11},{10,... | collective-permute-start | bytes 786440 | tf_op jit(solution)/shard_map/ppermute | solution.py:482
  221.9 35.2 %collective-permute-start.22 = (bf16[3,128,1024]{2,1,0:T(8,128)(2,1)S(1)}, bf16[3,128,1024]{2,1,0:T(8,128)(2,1)S(1)}, u32[]{:S(2)}, u32[]{:S(2)}) collective-permute-start(bf16[3,128,1024]{2,1,0:T(8,128)(2,1)S(1)} %pad_maximum_fusion.10.line), channel_id=1, source_target_pairs={{0,16},{1,17},{2,18},{3,19},{4,20},{5,21},{6,22},{7,23},{8,24},{9,... | collective-permute-start | bytes 2359304 | tf_op jit(solution)/shard_map/ppermute | solution.py:482
  223.3 36.0 %collective-permute-start.21 = (bf16[3,128,1024]{2,1,0:T(8,128)(2,1)S(1)}, bf16[3,128,1024]{2,1,0:T(8,128)(2,1)}, u32[]{:S(2)}, u32[]{:S(2)}) collective-permute-start(bf16[3,128,1024]{2,1,0:T(8,128)(2,1)S(1)} %pad_maximum_fusion.10.line), channel_id=1, source_target_pairs={{0,8},{1,9},{2,10},{3,11},{4,12},{5,13},{6,14},{7,15},{8,0},{9,1},... | collective-permute-start | bytes 2359304 | tf_op jit(solution)/shard_map/ppermute | solution.py:482
  228.6 76.4 %collective-permute-start.7 = (bf16[512,4096]{1,0:T(8,128)(2,1)}, bf16[512,4096]{1,0:T(8,128)(2,1)}, u32[]{:S(2)}, u32[]{:S(2)}) collective-permute-start(bf16[512,4096]{1,0:T(8,128)(2,1)} %bitcast.24), channel_id=1, source_target_pairs={{0,1},{1,0},{2,3},{3,2},{4,5},{5,4},{6,7},{7,6},{8,9},{9,8},{10,11... | collective-permute-start | bytes 12582920 | tf_op jit(solution)/shard_map/ppermute | solution.py:482
  229.9 31.8 %collective-permute-start.14 = (bf16[3,32,4096]{2,1,0:T(8,128)(2,1)S(1)}, bf16[3,32,4096]{2,1,0:T(8,128)(2,1)S(1)}, u32[]{:S(2)}, u32[]{:S(2)}) collective-permute-start(bf16[3,32,4096]{2,1,0:T(8,128)(2,1)S(1)} %pad_maximum_fusion.9.line), channel_id=1, source_target_pairs={{0,16},{1,17},{2,18},{3,19},{4,20},{5,21},{6,22},{7,23},{8,24},{9,... | collective-permute-start | bytes 2359304 | tf_op jit(solution)/shard_map/ppermute | solution.py:482
  231.4 32.5 %collective-permute-start.13 = (bf16[3,32,4096]{2,1,0:T(8,128)(2,1)S(1)}, bf16[3,32,4096]{2,1,0:T(8,128)(2,1)}, u32[]{:S(2)}, u32[]{:S(2)}) collective-permute-start(bf16[3,32,4096]{2,1,0:T(8,128)(2,1)S(1)} %pad_maximum_fusion.9.line), channel_id=1, source_target_pairs={{0,8},{1,9},{2,10},{3,11},{4,12},{5,13},{6,14},{7,15},{8,0},{9,1},... | collective-permute-start | bytes 2359304 | tf_op jit(solution)/shard_map/ppermute | solution.py:482
  251.5 51.4 %all-to-all-start.1 = ((bf16[8,1,2,128,128]{4,3,2,1,0:T(8,128)(2,1)}), bf16[8,1,2,128,128]{4,3,2,1,0:T(8,128)(2,1)}, u32[]{:S(2)}, u32[]{:S(2)}) async-start(bf16[8,1,2,128,128]{4,3,2,1,0:T(8,128)(2,1)} %bitcast.458), calls=%async_computation.1 | async-start | bytes 1048576 | tf_op jit(solution)/shard_map/all_to_all | solution.py:1151
  257.9 33.6 %collective-permute-start.23 = (bf16[3,64,1024]{2,1,0:T(8,128)(2,1)}, bf16[3,64,1024]{2,1,0:T(8,128)(2,1)}, u32[]{:S(2)}, u32[]{:S(2)}) collective-permute-start(bf16[3,64,1024]{2,1,0:T(8,128)(2,1)} %slice.1773), channel_id=1, source_target_pairs={{0,8},{1,9},{2,10},{3,11},{4,12},{5,13},{6,14},{7,15},{8,0},{9,1},... | collective-permute-start | bytes 1179656 | tf_op jit(solution)/shard_map/ppermute | solution.py:482
  261.1 30.5 %collective-permute-start.24 = (bf16[3,64,1024]{2,1,0:T(8,128)(2,1)}, bf16[3,64,1024]{2,1,0:T(8,128)(2,1)}, u32[]{:S(2)}, u32[]{:S(2)}) collective-permute-start(bf16[3,64,1024]{2,1,0:T(8,128)(2,1)} %slice.1774), channel_id=1, source_target_pairs={{0,16},{1,17},{2,18},{3,19},{4,20},{5,21},{6,22},{7,23},{8,24},{9,... | collective-permute-start | bytes 1179656 | tf_op jit(solution)/shard_map/ppermute | solution.py:482
  262.5 35.1 %collective-permute-start.15 = (bf16[3,16,4096]{2,1,0:T(8,128)(2,1)}, bf16[3,16,4096]{2,1,0:T(8,128)(2,1)}, u32[]{:S(2)}, u32[]{:S(2)}) collective-permute-start(bf16[3,16,4096]{2,1,0:T(8,128)(2,1)} %slice.1763), channel_id=1, source_target_pairs={{0,8},{1,9},{2,10},{3,11},{4,12},{5,13},{6,14},{7,15},{8,0},{9,1},... | collective-permute-start | bytes 1179656 | tf_op jit(solution)/shard_map/ppermute | solution.py:482
  265.7 32.0 %collective-permute-start.16 = (bf16[3,16,4096]{2,1,0:T(8,128)(2,1)}, bf16[3,16,4096]{2,1,0:T(8,128)(2,1)}, u32[]{:S(2)}, u32[]{:S(2)}) collective-permute-start(bf16[3,16,4096]{2,1,0:T(8,128)(2,1)} %slice.1764), channel_id=1, source_target_pairs={{0,16},{1,17},{2,18},{3,19},{4,20},{5,21},{6,22},{7,23},{8,24},{9,... | collective-permute-start | bytes 1179656 | tf_op jit(solution)/shard_map/ppermute | solution.py:482
  297.6 43.2 %collective-permute-start.25 = (bf16[2048,1024]{1,0:T(8,128)(2,1)}, bf16[2048,1024]{1,0:T(8,128)(2,1)}, u32[]{:S(2)}, u32[]{:S(2)}) collective-permute-start(bf16[2048,1024]{1,0:T(8,128)(2,1)} %bitcast.74), channel_id=1, source_target_pairs={{0,1},{1,0},{2,3},{3,2},{4,5},{5,4},{6,7},{7,6},{8,9},{9,8},{10,11... | collective-permute-start | bytes 12582920 | tf_op jit(solution)/shard_map/ppermute | solution.py:482
  302.4 30.9 %collective-permute-start.17 = (bf16[512,4096]{1,0:T(8,128)(2,1)}, bf16[512,4096]{1,0:T(8,128)(2,1)}, u32[]{:S(2)}, u32[]{:S(2)}) collective-permute-start(bf16[512,4096]{1,0:T(8,128)(2,1)} %bitcast.70), channel_id=1, source_target_pairs={{0,1},{1,0},{2,3},{3,2},{4,5},{5,4},{6,7},{7,6},{8,9},{9,8},{10,11... | collective-permute-start | bytes 12582920 | tf_op jit(solution)/shard_map/ppermute | solution.py:482
  399.7 349.4 %collective-permute-start.40 = (bf16[2048,1024]{1,0:T(8,128)(2,1)}, bf16[2048,1024]{1,0:T(8,128)(2,1)}, u32[]{:S(2)}, u32[]{:S(2)}) collective-permute-start(bf16[2048,1024]{1,0:T(8,128)(2,1)} %convolution_convert_fusion.3), channel_id=1, source_target_pairs={{0,1},{1,0},{2,3},{3,2},{4,5},{5,4},{6,7},{7,6},{8,9},{9,8},{10,11... | collective-permute-start | bytes 12582920 | tf_op jit(solution)/shard_map/ppermute | solution.py:482
  400.8 354.9 %collective-permute-start.28 = (bf16[512,4096]{1,0:T(8,128)(2,1)}, bf16[512,4096]{1,0:T(8,128)(2,1)}, u32[]{:S(2)}, u32[]{:S(2)}) collective-permute-start(bf16[512,4096]{1,0:T(8,128)(2,1)} %convolution_convert_fusion), channel_id=1, source_target_pairs={{0,1},{1,0},{2,3},{3,2},{4,5},{5,4},{6,7},{7,6},{8,9},{9,8},{10,11... | collective-permute-start | bytes 12582920 | tf_op jit(solution)/shard_map/ppermute | solution.py:482
  477.3 42.4 %all-to-all-start.3 = ((bf16[8,3,2,128,128]{4,3,2,1,0:T(8,128)(2,1)}), bf16[8,3,2,128,128]{4,3,2,1,0:T(8,128)(2,1)}, u32[]{:S(2)}, u32[]{:S(2)}) async-start(bf16[8,3,2,128,128]{4,3,2,1,0:T(8,128)(2,1)} %get-tuple-element.40), calls=%async_computation.3 | async-start | bytes 3145728 | tf_op jit(solution)/shard_map/all_to_all | solution.py:1151
  752.5 26.2 %collective-permute-start.41 = (bf16[2,2,128,1024]{3,2,0,1:T(8,128)(2,1)S(1)}, bf16[2,2,128,1024]{3,2,0,1:T(8,128)(2,1)S(1)}, u32[]{:S(2)}, u32[]{:S(2)}) collective-permute-start(bf16[2,2,128,1024]{3,2,0,1:T(8,128)(2,1)S(1)} %fusion.20), channel_id=1, source_target_pairs={{0,8},{1,9},{2,10},{3,11},{4,12},{5,13},{6,14},{7,15},{8,0},{9,1},... | collective-permute-start | bytes 3145736 | tf_op jit(solution)/shard_map/ppermute | solution.py:482
  754.6 43.4 %collective-permute-start.43 = (bf16[2,2,128,1024]{3,2,0,1:T(8,128)(2,1)S(1)}, bf16[2,2,128,1024]{3,2,0,1:T(8,128)(2,1)S(1)}, u32[]{:S(2)}, u32[]{:S(2)}) collective-permute-start(bf16[2,2,128,1024]{3,2,0,1:T(8,128)(2,1)S(1)} %fusion.21), channel_id=1, source_target_pairs={{0,16},{1,17},{2,18},{3,19},{4,20},{5,21},{6,22},{7,23},{8,24},{9,... | collective-permute-start | bytes 3145736 | tf_op jit(solution)/shard_map/ppermute | solution.py:482
  759.0 38.8 %collective-permute-start.29 = (bf16[2,2,32,4096]{3,2,0,1:T(8,128)(2,1)S(1)}, bf16[2,2,32,4096]{3,2,0,1:T(8,128)(2,1)S(1)}, u32[]{:S(2)}, u32[]{:S(2)}) collective-permute-start(bf16[2,2,32,4096]{3,2,0,1:T(8,128)(2,1)S(1)} %fusion.18), channel_id=1, source_target_pairs={{0,8},{1,9},{2,10},{3,11},{4,12},{5,13},{6,14},{7,15},{8,0},{9,1},... | collective-permute-start | bytes 3145736 | tf_op jit(solution)/shard_map/ppermute | solution.py:482
  760.8 42.4 %collective-permute-start.31 = (bf16[2,2,32,4096]{3,2,0,1:T(8,128)(2,1)S(1)}, bf16[2,2,32,4096]{3,2,0,1:T(8,128)(2,1)S(1)}, u32[]{:S(2)}, u32[]{:S(2)}) collective-permute-start(bf16[2,2,32,4096]{3,2,0,1:T(8,128)(2,1)S(1)} %fusion.19), channel_id=1, source_target_pairs={{0,16},{1,17},{2,18},{3,19},{4,20},{5,21},{6,22},{7,23},{8,24},{9,... | collective-permute-start | bytes 3145736 | tf_op jit(solution)/shard_map/ppermute | solution.py:482
  778.9 44.2 %collective-permute-start.42 = (bf16[2,128,1024]{2,1,0:T(8,128)(2,1)S(1)}, bf16[2,128,1024]{2,1,0:T(8,128)(2,1)S(1)}, u32[]{:S(2)}, u32[]{:S(2)}) collective-permute-start(bf16[2,128,1024]{2,1,0:T(8,128)(2,1)S(1)} %fusion.150), channel_id=1, source_target_pairs={{0,16},{1,17},{2,18},{3,19},{4,20},{5,21},{6,22},{7,23},{8,24},{9,... | collective-permute-start | bytes 1572872 | tf_op jit(solution)/shard_map/ppermute | solution.py:482
  820.2 26.1 %collective-permute-start.34 = (bf16[32,4096]{1,0:T(8,128)(2,1)S(1)}, bf16[32,4096]{1,0:T(8,128)(2,1)S(1)}, u32[]{:S(2)}, u32[]{:S(2)}) collective-permute-start(bf16[32,4096]{1,0:T(8,128)(2,1)S(1)} %get-tuple-element.178), channel_id=1, source_target_pairs={{0,4},{1,5},{2,6},{3,7},{4,0},{5,1},{6,2},{7,3},{8,12},{9,13},{10,... | collective-permute-start | bytes 786440 | tf_op jit(solution)/shard_map/ppermute | solution.py:482
  824.4 33.1 %collective-permute-start.46 = (bf16[128,1024]{1,0:T(8,128)(2,1)S(1)}, bf16[128,1024]{1,0:T(8,128)(2,1)S(1)}, u32[]{:S(2)}, u32[]{:S(2)}) collective-permute-start(bf16[128,1024]{1,0:T(8,128)(2,1)S(1)} %get-tuple-element.171), channel_id=1, source_target_pairs={{0,4},{1,5},{2,6},{3,7},{4,0},{5,1},{6,2},{7,3},{8,12},{9,13},{10,... | collective-permute-start | bytes 786440 | tf_op jit(solution)/shard_map/ppermute | solution.py:482
  829.8 27.6 %collective-permute-start.47 = (bf16[128,1024]{1,0:T(8,128)(2,1)S(1)}, bf16[128,1024]{1,0:T(8,128)(2,1)S(1)}, u32[]{:S(2)}, u32[]{:S(2)}) collective-permute-start(bf16[128,1024]{1,0:T(8,128)(2,1)S(1)} %get-tuple-element.172), channel_id=1, source_target_pairs={{0,6},{1,7},{2,0},{3,1},{4,2},{5,3},{6,4},{7,5},{8,14},{9,15},{10,... | collective-permute-start | bytes 786440 | tf_op jit(solution)/shard_map/ppermute | solution.py:482
  (193 other events, 1473.6 us)

commit v2 on v0

--- a/solution.py
+++ b/solution.py
@@ -1,6 +1,8 @@
 import jax
 import jax.numpy as jnp
 from jax import lax
+from jax.experimental import pallas as pl
+from jax.experimental.pallas import tpu as pltpu
 from jax.sharding import PartitionSpec as P
 
 
@@ -452,6 +454,1347 @@
     )
 
 
+def place():
+    dp, seq = lax.axis_index("dp"), lax.axis_index("seq")
+    return dp // 2, dp % 2, seq // 2, seq % 2
+
+
+QUERIES = 256
+
+
+def log_distance_block(length, start):
+    keys = lax.broadcasted_iota(jnp.int32, (length, QUERIES), 0)
+    queries = lax.broadcasted_iota(jnp.int32, (length, QUERIES), 1) + start
+    return jnp.log(1.0 + jnp.abs(keys - queries).astype(jnp.float32))
+
+
+def head_lanes(value, head, scale=1.0):
+    lane = lax.broadcasted_iota(jnp.int32, value.shape, 1)
+    mine = (lane >= 64 * head) & (lane < 64 * head + 64)
+    return jnp.where(mine, value * jnp.asarray(scale, value.dtype), jnp.zeros_like(value))
+
+
+def nt(a, b):
+    return lax.dot_general(a, b, (((1,), (1,)), ((), ())), preferred_element_type=jnp.float32)
+
+
+MESH_ID = pl.DeviceIdType.MESH
+PIECE = 32
+HALO = 16
+UP, DOWN, PROJECT, ATTEND_OUT, POINT_IN, POINT_OUT, REAR_UP, REAR_DOWN = 0, 4, 8, 11, 12, 14, 15, 19
+CHUNKS = 23
+LEAD = 3
+STAGE = 1
+STEP = 4 * STAGE
+VECTORS = 48
+
+
+def low(value):
+    return value.astype(jnp.bfloat16)
+
+
+def f32(value):
+    return value.astype(jnp.float32)
+
+
+def dot(a, b):
+    return jnp.dot(a, b, preferred_element_type=jnp.float32)
+
+
+def norm_rows(v, gain, bias):
+    centred = v - jnp.mean(v, axis=-1, keepdims=True)
+    spread = jnp.mean(centred * centred, axis=-1, keepdims=True)
+    return centred * lax.rsqrt(spread + 1e-05) * gain + bias
+
+
+def logistic(v):
+    return 1.0 / (1.0 + jnp.exp(-v))
+
+
+def remote_copy(src, dst, send_sem, recv_sem, there):
+    return pltpu.make_async_remote_copy(
+        src_ref=src,
+        dst_ref=dst,
+        send_sem=send_sem,
+        recv_sem=recv_sem,
+        device_id=there,
+        device_id_type=MESH_ID,
+    )
+
+
+def attend_block(packed, slopes, seg_cols, seg_rows, row, block, length):
+    distance = log_distance_block(length, block * QUERIES)
+    same = seg_cols == seg_rows
+    q = packed[pl.ds(block * 2, 2), 0, row].reshape(QUERIES, 128)
+    k = packed[:, 1, row].reshape(length, 128)
+    value_t = packed[:, 2, row].reshape(length, 128).T
+    outs = []
+    for head in range(2):
+        logit = nt(k, head_lanes(q, head, 0.125)) - slopes[head] * distance
+        logit = jnp.where(same, logit, -1e30)
+        top = jnp.max(logit, axis=0, keepdims=True)
+        power = jnp.exp(logit - top)
+        total = jnp.sum(power, axis=0, keepdims=True)
+        out = dot(value_t, low(power))
+        outs.append(out[64 * head : 64 * head + 64] / total)
+    return low(jnp.concatenate(outs, axis=0).T)
+
+
+def forward_kernel(*refs):
+    shards, vec, seg, frames, slopes = refs[:5]
+    (full, vec_all, seg_all, norm0, pre_f, hid_f, after_front, norm1, packed, attended, after_attend) = refs[5:16]
+    (norm2, conv_pre, gated, mixed, act, after_conv, norm4, pre_r, hid_r, after_rear) = refs[16:26]
+    (wbuf, vectors, pk_out, att_out, att_in, gated_f, seg_plane, seg_cols, seg_rows, acc) = refs[26:36]
+    (gather_sem, own_sem, small_sem, pk_sem, att_sem, halo_sem, load_sem) = refs[36:]
+    y, x, z, core = place()
+    dp, seq = y * 2 + x, z * 2 + core
+    rows, width = 2, 1024
+    frame_count = 128
+    length = 8 * frame_count
+    over_x = (y * 2 + 1 - x, seq)
+    over_y = ((1 - y) * 2 + x, seq)
+    over_core = (dp, z * 2 + 1 - core)
+
+    def peer(k):
+        return lax.rem(seq + k, 8)
+
+    barrier = pltpu.get_barrier_semaphore()
+    for there in [(dp, peer(k)) for k in range(1, 8)] + [over_x, over_y]:
+        pl.semaphore_signal(barrier, inc=1, device_id=there, device_id_type=MESH_ID)
+    pl.semaphore_wait(barrier, 9)
+
+    q_own, q_x, q_y = PIECE * dp, PIECE * (y * 2 + 1 - x), PIECE * ((1 - y) * 2 + x)
+
+    def travel(kind, t, k, first, rows_, there, src=None):
+        source = seq if src is not None else lax.rem(z - k + 4, 4) * 2 + core
+        where = full.at[t, source, pl.ds(pl.multiple_of(first, 16), rows_)]
+        return remote_copy(
+            where if src is None else src,
+            where,
+            gather_sem.at[0, kind, t, k - 1],
+            gather_sem.at[1, kind, t, k - 1],
+            there,
+        )
+
+    def line(t, k):
+        src = shards.at[t, pl.ds(pl.multiple_of(q_own, 16), PIECE)]
+        return travel(0, t, k, q_own, PIECE, (dp, lax.rem(z + k, 4) * 2 + core), src)
+
+    def to_x(t, k):
+        return travel(1, t, k, q_own, PIECE, over_x)
+
+    def to_y(t, k):
+        return travel(2, t, k, q_own, PIECE, over_y)
+
+    def on_x(t, k):
+        return travel(3, t, k, q_y, PIECE // 2, over_x)
+
+    def on_y(t, k):
+        return travel(4, t, k, q_x + PIECE // 2, PIECE // 2, over_y)
+
+    def to_core(t, k):
+        return travel(5, t, k, 0, 4 * PIECE, over_core)
+
+    def own_to_core():
+        return remote_copy(shards, full.at[:, seq], own_sem.at[0], own_sem.at[1], over_core)
+
+    def own_to_full():
+        return pltpu.make_async_copy(shards, full.at[:, seq], own_sem.at[2])
+
+    def small_copies():
+        copies = []
+        for k in range(1, 8):
+            for i, (src, dst) in enumerate(((vec, vec_all), (seg, seg_all))):
+                copies.append(
+                    remote_copy(
+                        src,
+                        dst.at[seq],
+                        small_sem.at[0, i, k - 1],
+                        small_sem.at[1, i, k - 1],
+                        (dp, peer(k)),
+                    )
+                )
+        return copies
+
+    for copy in small_copies():
+        copy.start()
+    own_to_core().start()
+    own_to_full().start()
+    vec_all[seq] = vec[...]
+    seg_all[seq] = seg[...]
+    def relay(t):
+        where = full.at[t, lax.rem(z + 2, 4) * 2 + core, pl.ds(pl.multiple_of(q_own, 16), PIECE)]
+        return remote_copy(
+            where,
+            where,
+            gather_sem.at[0, 6, t, 0],
+            gather_sem.at[1, 0, t, 2 * z - 2],
+            (dp, 3 * (z - 1) * 2 + core),
+        )
+
+    def direct(k):
+        return {1: z != 3, 2: z >= 0, 3: z != 0}[k]
+
+    def in_time(k):
+        return {1: z != 0, 2: z >= 0, 3: z != 3}[k]
+
+    relays = (z == 1) | (z == 2)
+
+    def start_line(t):
+        for k in (1, 2, 3):
+
+            @pl.when(direct(k))
+            def _():
+                line(t, k).start()
+
+    def arrived(t, k):
+        line(t, k).wait_recv()
+        to_x(t, k).start()
+        to_y(t, k).start()
+
+    for t in range(LEAD):
+        start_line(t)
+
+    def gather_step(step):
+        @pl.when(step + LEAD < CHUNKS)
+        def _():
+            start_line(step + LEAD)
+
+        @pl.when(step < CHUNKS)
+        def _():
+            for k in (2, 1, 3):
+
+                @pl.when(in_time(k))
+                def _():
+                    arrived(step, k)
+
+                if k == 2:
+
+                    @pl.when(relays)
+                    def _():
+                        relay(step).start()
+
+        late = step - STAGE
+
+        @pl.when((late >= 0) & (late < CHUNKS))
+        def _():
+            for k in (1, 3):
+
+                @pl.when(jnp.logical_not(in_time(k)))
+                def _():
+                    arrived(late, k)
+
+        second, third, last = step - 2 * STAGE, step - 3 * STAGE, step - 4 * STAGE
+
+        @pl.when((second >= 0) & (second < CHUNKS))
+        def _():
+            for k in (1, 2, 3):
+                to_y(second, k).wait_recv()
+                on_x(second, k).start()
+                to_x(second, k).wait_recv()
+                on_y(second, k).start()
+
+        @pl.when((third >= 0) & (third < CHUNKS))
+        def _():
+            for k in (1, 2, 3):
+                on_x(third, k).wait_recv()
+                on_y(third, k).wait_recv()
+                to_core(third, k).start()
+
+        @pl.when((last >= 0) & (last < CHUNKS))
+        def _():
+            for k in (1, 2, 3):
+                to_core(last, k).wait_recv()
+
+    def load(u):
+        return pltpu.make_async_copy(full.at[u], wbuf.at[lax.rem(u, 2)], load_sem.at[lax.rem(u, 2)])
+
+    def weight(u):
+        load(u).wait()
+        return wbuf[lax.rem(u, 2)].reshape(width, width)
+
+    def vector(i):
+        return vectors[i : i + 1, :]
+
+    def norm(v, i):
+        return low(norm_rows(v, vector(i), vector(6 + i)))
+
+    def prepare():
+        own_to_full().wait()
+        own_to_core().wait()
+        for copy in small_copies():
+            copy.wait()
+        for s in range(8):
+            vectors[:, s * 128 : s * 128 + 128] = f32(vec_all[s])
+            columns = f32(seg_all[s]).T
+            for r in range(rows):
+                seg_cols[r, s * 128 : s * 128 + 128, :] = columns[:, r : r + 1]
+                seg_rows[r : r + 1, s * 128 : s * 128 + 128] = f32(seg_all[s, r : r + 1, :])
+        before = jnp.where(seq > 0, f32(seg_all[lax.max(seq - 1, 0)]), -1.0).T
+        middle = f32(seg_all[seq]).T
+        after = jnp.where(seq < 7, f32(seg_all[lax.min(seq + 1, 7)]), -1.0).T
+        for r in range(rows):
+            for first, col in (
+                (0, before[frame_count - HALO :, r : r + 1]),
+                (HALO, middle[:, r : r + 1]),
+                (HALO + frame_count, after[:HALO, r : r + 1]),
+            ):
+                seg_plane[r, first : first + col.shape[0], :] = jnp.broadcast_to(col, (col.shape[0], 128))
+        gated[:, :HALO] = jnp.zeros((rows, HALO, width), jnp.bfloat16)
+        gated[:, HALO + frame_count :] = jnp.zeros((rows, HALO, width), jnp.bfloat16)
+        norm0[...] = norm(f32(frames[...]), 0)
+
+    def up(u, j, source, pre, hid):
+        value = dot(source[...], weight(u))
+        pre[j] = low(value)
+        hid[j] = low(value * logistic(value))
+
+    def down(u, j, stream, hid, target):
+        value = dot(hid[j], weight(u))
+
+        @pl.when(j == 0)
+        def _():
+            acc[...] = value
+
+        @pl.when(j > 0)
+        def _():
+            acc[...] += value
+
+        @pl.when(j == 3)
+        def _():
+            target[...] = f32(stream[...]) + 0.5 * acc[...]
+
+    def pk_copy(c, k, recv=False):
+        there = peer(k)
+        return remote_copy(
+            pk_out.at[there, c],
+            packed.at[there if recv else seq, c],
+            pk_sem.at[0, there, c],
+            pk_sem.at[1, there if recv else seq, c],
+            (dp, there),
+        )
+
+    def project(u, c):
+        value = low(dot(norm1[...], weight(u)))
+        for s in range(8):
+            pk_out[s, c] = value[:, s * 128 : s * 128 + 128].reshape(rows, frame_count, 128)
+        packed[seq, c] = pk_out[seq, c]
+        for k in range(1, 8):
+            pk_copy(c, k).start()
+
+    def att_copy(b, r, recv=False):
+        return remote_copy(
+            att_out.at[b, r],
+            att_in.at[b if recv else seq, r],
+            att_sem.at[0, b, r],
+            att_sem.at[1, b if recv else seq, r],
+            (dp, b),
+        )
+
+    def attend_step(i):
+        row, block = i // 4, lax.rem(i, 4)
+        cols = seg_cols[row]
+        first = pl.multiple_of(block * QUERIES, QUERIES)
+        out = attend_block(
+            packed, slopes, cols, seg_rows[pl.ds(row, 1), pl.ds(first, QUERIES)], row, block, length
+        )
+        for half in range(2):
+            b = block * 2 + half
+            att_out[b, row] = out[half * 128 : half * 128 + 128]
+
+            @pl.when(b != seq)
+            def _():
+                att_copy(b, row).start()
+
+            @pl.when(b == seq)
+            def _():
+                att_in[b, row] = out[half * 128 : half * 128 + 128]
+
+    def halo_copy(side):
+        if side == 0:
+            src, dst, there = gated.at[:, pl.ds(HALO, HALO)], gated.at[:, pl.ds(HALO + frame_count, HALO)], lax.rem(seq + 7, 8)
+        else:
+            src, dst, there = gated.at[:, pl.ds(frame_count, HALO)], gated.at[:, pl.ds(0, HALO)], lax.rem(seq + 1, 8)
+        return remote_copy(src, dst, halo_sem.at[0, side], halo_sem.at[1, side], (dp, there))
+
+    def convolve():
+        @pl.when(seq > 0)
+        def _():
+            halo_copy(0).wait_send()
+            halo_copy(1).wait_recv()
+
+        @pl.when(seq < 7)
+        def _():
+            halo_copy(1).wait_send()
+            halo_copy(0).wait_recv()
+
+        gated_f[...] = f32(gated[...])
+
+        def lanes(i, _):
+            at = pl.ds(pl.multiple_of(i * 128, 128), 128)
+            for r in range(rows):
+                own = seg_plane[r, HALO : HALO + frame_count, :]
+                total = jnp.zeros((frame_count, 128), jnp.float32)
+                for tap in range(31):
+                    first = tap + HALO - 15
+                    same = seg_plane[r, first : first + frame_count, :] == own
+                    term = gated_f[r, first : first + frame_count, at] * vectors[12 + tap : 13 + tap, at]
+                    total = total + jnp.where(same, term, 0.0)
+                mixed[r * frame_count : (r + 1) * frame_count, at] = total
+            return 0
+
+        lax.fori_loop(0, width // 128, lanes, 0)
+
+    def step_work(step, _):
+        gather_step(step)
+
+        now = step - STEP
+
+        def at(first, count=1):
+            return pl.when((now >= first) & (now < first + count))
+
+        @at(0)
+        def _():
+            prepare()
+
+        @at(1, 4)
+        def _():
+            up(now - 1, now - 1, norm0, pre_f, hid_f)
+
+        @at(5, 4)
+        def _():
+            down(now - 1, now - 5, frames, hid_f, after_front)
+
+        @at(9, 3)
+        def _():
+            @pl.when(now == 9)
+            def _():
+                norm1[...] = norm(after_front[...], 1)
+
+            project(now - 1, now - 9)
+
+        @at(13)
+        def _():
+            for c in range(3):
+                for k in range(1, 8):
+                    pk_copy(c, k, True).wait_recv()
+
+        @at(13, 4)
+        def _():
+            attend_step((now - 13) * 2)
+            attend_step((now - 13) * 2 + 1)
+
+        @at(17)
+        def _():
+            for r in range(rows):
+                for k in range(1, 8):
+                    att_copy(peer(k), r, True).wait_recv()
+            for s in range(8):
+                attended[:, s * 128 : s * 128 + 128] = att_in[s].reshape(rows * frame_count, 128)
+            after_attend[...] = after_front[...] + dot(attended[...], weight(ATTEND_OUT))
+            norm2[...] = norm(after_attend[...], 2)
+
+        @at(18)
+        def _():
+            acc[...] = dot(norm2[...], weight(POINT_IN))
+            conv_pre[0] = low(acc[...])
+
+        @at(19)
+        def _():
+            gate = dot(norm2[...], weight(POINT_IN + 1))
+            conv_pre[1] = low(gate)
+            value = low(acc[...] * logistic(gate))
+            gated[:, HALO : HALO + frame_count] = value.reshape(rows, frame_count, width)
+
+            @pl.when(seq > 0)
+            def _():
+                halo_copy(0).start()
+
+            @pl.when(seq < 7)
+            def _():
+                halo_copy(1).start()
+
+        @at(20)
+        def _():
+            convolve()
+            value = norm_rows(mixed[...], vector(3), vector(9))
+            act[...] = low(value * logistic(value))
+            after_conv[...] = after_attend[...] + dot(act[...], weight(POINT_OUT))
+            norm4[...] = norm(after_conv[...], 4)
+
+        @at(21, 4)
+        def _():
+            up(now - 21 + REAR_UP, now - 21, norm4, pre_r, hid_r)
+
+        @at(25, 4)
+        def _():
+            down(now - 25 + REAR_DOWN, now - 25, after_conv, hid_r, after_rear)
+
+        @at(0, 11)
+        def _():
+            load(now - 0).start()
+
+        @at(16, 12)
+        def _():
+            load(now - 5).start()
+
+        return 0
+
+    lax.fori_loop(0, STEP + 29, step_work, 0)
+
+    def drain(t, _):
+        for kind in (to_x, to_y, on_x, on_y, to_core):
+            for k in (1, 2, 3):
+                kind(t, k).wait_send()
+        for k in (1, 2, 3):
+
+            @pl.when(direct(k))
+            def _():
+                line(t, k).wait_send()
+
+        @pl.when(relays)
+        def _():
+            relay(t).wait_send()
+
+        return 0
+
+    lax.fori_loop(0, CHUNKS, drain, 0)
+    for c in range(3):
+        for k in range(1, 8):
+            pk_copy(c, k).wait_send()
+    for r in range(rows):
+        for k in range(1, 8):
+            att_copy(peer(k), r).wait_send()
+
+
+def forward_layer(shards, vec, seg, frames, slopes):
+    bf16, tokens, width = jnp.bfloat16, frames.shape[0], frames.shape[1]
+    dma = pltpu.SemaphoreType.DMA
+
+    def shape(kind, *sizes):
+        return jax.ShapeDtypeStruct(sizes, kind)
+
+    plain, single = shape(bf16, tokens, width), shape(jnp.float32, tokens, width)
+    four = shape(bf16, 4, tokens, width)
+    outs = [
+        shape(bf16, CHUNKS, 8, 128, width),
+        shape(bf16, 8, VECTORS, 128),
+        shape(jnp.int32, 8, 8, 128),
+        plain,
+        four,
+        four,
+        single,
+        plain,
+        shape(bf16, 8, 3, 2, 128, 128),
+        plain,
+        single,
+        plain,
+        shape(bf16, 2, tokens, width),
+        shape(bf16, 2, 128 + 2 * HALO, width),
+        single,
+        plain,
+        single,
+        plain,
+        four,
+        four,
+        single,
+    ]
+    vmem, hbm = pl.BlockSpec(memory_space=pltpu.VMEM), pl.BlockSpec(memory_space=pltpu.HBM)
+    return pl.pallas_call(
+        forward_kernel,
+        in_specs=[vmem, vmem, vmem, vmem, pl.BlockSpec(memory_space=pltpu.SMEM)],
+        out_specs=[hbm] + [vmem] * (len(outs) - 1),
+        out_shape=outs,
+        scratch_shapes=[
+            pltpu.VMEM((2, 8, 128, width), bf16),
+            pltpu.VMEM((VECTORS, width), jnp.float32),
+            pltpu.VMEM((8, 3, 2, 128, 128), bf16),
+            pltpu.VMEM((8, 2, 128, 128), bf16),
+            pltpu.VMEM((8, 2, 128, 128), bf16),
+            pltpu.VMEM((2, 128 + 2 * HALO, width), jnp.float32),
+            pltpu.VMEM((2, 128 + 2 * HALO, 128), jnp.float32),
+            pltpu.VMEM((2, 1024, 1), jnp.float32),
+            pltpu.VMEM((8, 1024), jnp.float32),
+            pltpu.VMEM((tokens, width), jnp.float32),
+            dma((2, 7, CHUNKS, 3)),
+            dma((3,)),
+            dma((2, 2, 7)),
+            dma((2, 8, 3)),
+            dma((2, 8, 2)),
+            dma((2, 2)),
+            dma((2,)),
+        ],
+        compiler_params=pltpu.CompilerParams(
+            collective_id=0, has_side_effects=True, vmem_limit_bytes=60 * 2**20
+        ),
+        name="forward_layer",
+    )(shards, vec, seg, frames, slopes)
+
+
+JOB_RU, JOB_PO, JOB_PI, JOB_AO, JOB_P, JOB_FD, JOB_FU, JOBS = 4, 8, 9, 11, 12, 15, 19, 23
+RING = 4
+OUT_LAG = 6
+
+
+def silu_slope(pre, grad):
+    gate = logistic(pre)
+    return grad * gate * (1.0 + pre * (1.0 - gate))
+
+
+def tn(a, b):
+    return lax.dot_general(a, b, (((0,), (0,)), ((), ())), preferred_element_type=jnp.float32)
+
+
+def backward_kernel(*refs):
+    (full, vec_all, seg_all, norm0, pre_f, hid_f, after_front, norm1, packed, attended, after_attend) = refs[:11]
+    (norm2, conv_pre, gated, mixed, act, after_conv, norm4, pre_r, hid_r, after_rear) = refs[11:21]
+    (frames, cotangent, slopes) = refs[21:24]
+    (result, frames_grad, shares, vec_out) = refs[24:28]
+    (wbuf, pre_buf, hid_buf, v_buf, vectors, small, left, right) = refs[28:36]
+    (branch, pre_grads, conv_branch, gate_grads, attend_branch, parts) = refs[36:42]
+    (grad, total, gated_f, mixed_w, mixed_f, seg_plane, seg_cols, seg_rows) = refs[42:50]
+    (g_out, g_in, p_out, p_in, key_sum, value_sum, slope_sum, out_buf) = refs[50:58]
+    (g_buf, h_buf, a_buf, b_buf, q_buf, core_in, a_in, b_in, a2_in, b2_in, z_in, o_buf) = refs[58:70]
+    (vec_send, vec_in, vec_dp) = refs[70:73]
+    (sem, vec_sem, load_sem, pre_sem, hid_sem, v_sem, ga_sem, pk_sem, halo_sem, out_sem) = refs[73:]
+    y, x, z, core = place()
+    dp, seq = y * 2 + x, z * 2 + core
+    rows, width, frame_count = 2, 1024, 128
+    length = 8 * frame_count
+    over_x = (y * 2 + 1 - x, seq)
+    over_y = ((1 - y) * 2 + x, seq)
+    over_core = (dp, z * 2 + 1 - core)
+
+    def peer(k):
+        return lax.rem(seq + k, 8)
+
+    def dp_peer(k):
+        return (lax.rem(dp + k, 4), seq)
+
+    mixed_w[:, :HALO] = jnp.zeros((rows, HALO, width), jnp.bfloat16)
+    mixed_w[:, HALO + frame_count :] = jnp.zeros((rows, HALO, width), jnp.bfloat16)
+    barrier = pltpu.get_barrier_semaphore()
+    for there in [(dp, peer(k)) for k in range(1, 8)] + [dp_peer(k) for k in range(1, 4)]:
+        pl.semaphore_signal(barrier, inc=1, device_id=there, device_id_type=MESH_ID)
+    pl.semaphore_wait(barrier, 10)
+
+    def remote(src, dst, t, slot, there):
+        return remote_copy(
+            src, dst, sem.at[0, slot, lax.rem(t, RING)], sem.at[1, slot, lax.rem(t, RING)], there
+        )
+
+    def core_copies(t, r):
+        return [remote(g_buf.at[1], core_in.at[r], t, 0, over_core)]
+
+    def first_copies(t, r):
+        return [
+            remote(h_buf.at[pl.ds(0, 2), :, 1 - x], a_in.at[r], t, 1, over_x),
+            remote(h_buf.at[pl.ds(2, 2), 1 - y], b_in.at[r], t, 2, over_y),
+        ]
+
+    def second_copies(t, r):
+        return [
+            remote(a_buf.at[:, 1 - y], a2_in.at[r], t, 3, over_y),
+            remote(b_buf.at[:, 1 - x], b2_in.at[r], t, 4, over_x),
+        ]
+
+    def line_copies(t, r):
+        copies = []
+        for k in (1, 2, 3):
+            to = lax.rem(z + k, 4)
+            copies.append(remote(q_buf.at[to], z_in.at[r, k - 1], t, 4 + k, (dp, to * 2 + core)))
+        return copies
+
+    def share_copies(t, r):
+        where = o_buf.at[r, dp]
+        return [remote(where, where, t, 8, over_x), remote(where, where, t, 9, over_y)]
+
+    def across_copies(t, r):
+        one = o_buf.at[r, (1 - y) * 2 + x, pl.ds(0, PIECE // 2)]
+        two = o_buf.at[r, y * 2 + 1 - x, pl.ds(PIECE // 2, PIECE // 2)]
+        return [remote(one, one, t, 10, over_x), remote(two, two, t, 11, over_y)]
+
+    def out_copy(t):
+        slot = lax.rem(t, 2)
+        return pltpu.make_async_copy(out_buf.at[slot], shares.at[t], out_sem.at[slot])
+
+    def finish(copies):
+        for copy in copies:
+            copy.wait()
+
+    def begin(copies):
+        for copy in copies:
+            copy.start()
+
+    def write_out(t, r):
+        finish(across_copies(t, r))
+
+        @pl.when(t >= 2)
+        def _():
+            out_copy(t - 2).wait()
+
+        out_buf[lax.rem(t, 2)] = f32(o_buf[r].reshape(128, width))
+        out_copy(t).start()
+
+    def pass_on(t, r):
+        finish(share_copies(t, r))
+        begin(across_copies(t, r))
+
+    def total_line(t, r):
+        finish(line_copies(t, r))
+        value = f32(q_buf[z]) + f32(z_in[r, 0]) + f32(z_in[r, 1]) + f32(z_in[r, 2])
+        o_buf[r, dp] = low(value)
+        begin(share_copies(t, r))
+
+    def total_second(t, r):
+        finish(second_copies(t, r))
+        q_buf[0:2] = low(f32(a_buf[:, y]) + f32(a2_in[r]))
+        q_buf[2:4] = low(f32(b_buf[:, x]) + f32(b2_in[r]))
+        begin(line_copies(t, r))
+
+    def total_first(t, r):
+        finish(first_copies(t, r))
+        a_buf[...] = low(f32(h_buf[0:2, :, x]) + f32(a_in[r]))
+        b_buf[...] = low(f32(h_buf[2:4, y]) + f32(b_in[r]))
+        begin(second_copies(t, r))
+
+    def total_core(t, r):
+        finish(core_copies(t, r))
+        for i in range(4):
+            value = low(f32(g_buf[0, i]) + f32(core_in[r, i]))
+            h_buf[i] = value.reshape(2, 2, PIECE, width)
+        begin(first_copies(t, r))
+
+    def product(t, r):
+        for i in range(8):
+            part = tn(left[:, 128 * i : 128 * i + 128], right[...])
+            g_buf[lax.rem(core + i, 2), i // 2] = low(part)
+        begin(core_copies(t, r))
+
+    sums = [total_core, total_first, total_second, total_line, pass_on, write_out]
+
+    def sum_step(step):
+        for depth in reversed(range(1, 7)):
+            t = step - depth
+
+            @pl.when((t >= 0) & (t < JOBS))
+            def _(t=t, depth=depth):
+                sums[depth - 1](t, lax.rem(t, RING))
+
+    def load(i, u):
+        return pltpu.make_async_copy(full.at[u], wbuf.at[i], load_sem.at[i])
+
+    def weight(i, u):
+        load(i, u).wait()
+        return wbuf[i].reshape(width, width)
+
+    def fetch_pre(source, j):
+        return pltpu.make_async_copy(source.at[j], pre_buf, pre_sem.at[0])
+
+    def fetch_hid(source, j):
+        return pltpu.make_async_copy(source.at[j], hid_buf, hid_sem.at[0])
+
+    def fetch(source):
+        return pltpu.make_async_copy(source, v_buf, v_sem.at[0])
+
+    def vector(i):
+        return vectors[i : i + 1, :]
+
+    def norm_back(v, i, dy):
+        centred = v - jnp.mean(v, axis=-1, keepdims=True)
+        rstd = lax.rsqrt(jnp.mean(centred * centred, axis=-1, keepdims=True) + 1e-05)
+        n = centred * rstd
+        small[i : i + 1, :] = jnp.sum(dy * n, axis=0, keepdims=True)
+        small[6 + i : 7 + i, :] = jnp.sum(dy, axis=0, keepdims=True)
+        dn = dy * vector(i)
+        first = jnp.mean(dn, axis=-1, keepdims=True)
+        second = jnp.mean(dn * n, axis=-1, keepdims=True)
+        return rstd * (dn - first - n * second)
+
+    def half_back(j, pre, up, down):
+        hidden_grad = nt(branch[...], weight(0, down + j))
+        fetch_pre(pre, j).wait()
+        pre_grads[j] = low(silu_slope(f32(pre_buf[...]), hidden_grad))
+        value = nt(pre_grads[j], weight(1, up + j))
+
+        @pl.when(j == 0)
+        def _():
+            total[...] = value
+
+        @pl.when(j > 0)
+        def _():
+            total[...] += value
+
+    def prepare():
+        small[...] = jnp.zeros_like(small)
+        slope_sum[...] = jnp.zeros_like(slope_sum)
+        for s in range(8):
+            vectors[:, s * 128 : s * 128 + 128] = f32(vec_all[s])
+            columns = f32(seg_all[s]).T
+            for r in range(rows):
+                seg_cols[r, s * 128 : s * 128 + 128, :] = columns[:, r : r + 1]
+                seg_rows[r : r + 1, s * 128 : s * 128 + 128] = f32(seg_all[s, r : r + 1, :])
+        before = jnp.where(seq > 0, f32(seg_all[lax.max(seq - 1, 0)]), -1.0).T
+        middle = f32(seg_all[seq]).T
+        after = jnp.where(seq < 7, f32(seg_all[lax.min(seq + 1, 7)]), -1.0).T
+        for r in range(rows):
+            for first, col in (
+                (0, before[frame_count - HALO :, r : r + 1]),
+                (HALO, middle[:, r : r + 1]),
+                (HALO + frame_count, after[:HALO, r : r + 1]),
+            ):
+                seg_plane[r, first : first + col.shape[0], :] = jnp.broadcast_to(
+                    col, (col.shape[0], 128)
+                )
+        gated_f[...] = f32(gated[...])
+
+    def halo_copy(side):
+        if side == 0:
+            src, dst = pl.ds(HALO, HALO), pl.ds(HALO + frame_count, HALO)
+            there = lax.rem(seq + 7, 8)
+        else:
+            src, dst = pl.ds(frame_count, HALO), pl.ds(0, HALO)
+            there = lax.rem(seq + 1, 8)
+        return remote_copy(
+            mixed_w.at[:, src],
+            mixed_w.at[:, dst],
+            halo_sem.at[0, side],
+            halo_sem.at[1, side],
+            (dp, there),
+        )
+
+    def convolve_back(r):
+        def lanes(i, _):
+            at = pl.ds(pl.multiple_of(i * 128, 128), 128)
+            own = seg_plane[r, HALO : HALO + frame_count, :]
+            mine = mixed_f[r, HALO : HALO + frame_count, at]
+            value = jnp.zeros((frame_count, 128), jnp.float32)
+            for tap in range(31):
+                first = tap + HALO - 15
+                same = seg_plane[r, first : first + frame_count, :] == own
+                near = jnp.where(same, gated_f[r, first : first + frame_count, at], 0.0)
+                small[12 + tap : 13 + tap, at] += jnp.sum(near * mine, axis=0, keepdims=True)
+                came = jnp.where(same, mixed_f[r, first : first + frame_count, at], 0.0)
+                value = value + came * vectors[12 + 30 - tap : 13 + 30 - tap, at]
+            total[r * frame_count : (r + 1) * frame_count, at] = value
+            return 0
+
+        lax.fori_loop(0, width // 128, lanes, 0)
+
+    def ga_copy(k, recv=False):
+        there = peer(k)
+        return remote_copy(
+            g_out.at[there],
+            g_in.at[there if recv else seq],
+            ga_sem.at[0, there],
+            ga_sem.at[1, there if recv else seq],
+            (dp, there),
+        )
+
+    def pk_copy(there, c, r, recv=False):
+        return remote_copy(
+            p_out.at[there, c, r],
+            p_in.at[there if recv else seq, c, r],
+            pk_sem.at[0, there, c, r],
+            pk_sem.at[1, there if recv else seq, c, r],
+            (dp, there),
+        )
+
+    def attend_back_step(i):
+        row, block = i // 4, lax.rem(i, 4)
+        first = pl.multiple_of(block * QUERIES, QUERIES)
+        distance = log_distance_block(length, block * QUERIES)
+        same = seg_cols[row] == seg_rows[pl.ds(row, 1), pl.ds(first, QUERIES)]
+        q = packed[pl.ds(block * 2, 2), 0, row].reshape(QUERIES, 128)
+        k = packed[:, 1, row].reshape(length, 128)
+        v = packed[:, 2, row].reshape(length, 128)
+        g = g_in[pl.ds(block * 2, 2), row].reshape(QUERIES, 128)
+        key_t = k.T
+
+        @pl.when(block == 0)
+        def _():
+            key_sum[...] = jnp.zeros_like(key_sum)
+            value_sum[...] = jnp.zeros_like(value_sum)
+
+        outs = []
+        for head in range(2):
+            q_head = head_lanes(q, head, 0.125)
+            g_head = head_lanes(g, head)
+            logit = nt(k, q_head) - slopes[head] * distance
+            logit = jnp.where(same, logit, -1e30)
+            top = jnp.max(logit, axis=0, keepdims=True)
+            power = jnp.exp(logit - top)
+            prob = power * (1.0 / jnp.sum(power, axis=0, keepdims=True))
+            prob_grad = nt(v, g_head)
+            delta = jnp.sum(prob * prob_grad, axis=0, keepdims=True)
+            logit_grad = prob * (prob_grad - delta)
+            slope = jnp.sum(logit_grad * distance, axis=0, keepdims=True)
+            slope_sum[head : head + 1, :] -= slope
+            score = low(logit_grad)
+            key_sum[...] += dot(score, q_head)
+            value_sum[...] += dot(low(prob), g_head)
+            query_t = dot(key_t, score)
+            outs.append(query_t[64 * head : 64 * head + 64] * 0.125)
+        query = low(jnp.concatenate(outs, axis=0).T)
+
+        def deliver(b, c, value):
+            p_out[b, c, row] = value
+
+            @pl.when(b != seq)
+            def _():
+                pk_copy(b, c, row).start()
+
+            @pl.when(b == seq)
+            def _():
+                p_in[b, c, row] = value
+
+        for half in range(2):
+            deliver(block * 2 + half, 0, query[half * 128 : half * 128 + 128])
+
+        @pl.when(block == 3)
+        def _():
+            for b in range(8):
+                at = slice(b * 128, b * 128 + 128)
+                deliver(b, 1, low(key_sum[at, :]))
+                deliver(b, 2, low(value_sum[at, :]))
+
+    def vec_copies():
+        copies = []
+        for k in range(1, 8):
+            copies.append(
+                remote_copy(
+                    vec_send.at[peer(k)],
+                    vec_in.at[seq],
+                    vec_sem.at[0, k - 1],
+                    vec_sem.at[1, k - 1],
+                    (dp, peer(k)),
+                )
+            )
+        return copies
+
+    def vec_dp_copies():
+        where = vec_dp.at[dp]
+        return [
+            remote_copy(where, where, vec_sem.at[0, 6 + k], vec_sem.at[1, 6 + k], dp_peer(k))
+            for k in (1, 2, 3)
+        ]
+
+    def send_vectors():
+        lane = lax.broadcasted_iota(jnp.int32, (1, 128), 1)
+        mine = jnp.zeros((1, 128), jnp.float32)
+        for head in range(2):
+            value = jnp.sum(slope_sum[head : head + 1, :], axis=-1, keepdims=True)
+            mine = mine + jnp.where(lane == seq * 2 + head, value, 0.0)
+        for s in range(8):
+            vec_send[s] = small[:, s * 128 : s * 128 + 128]
+            vec_send[s, 43:44, :] = mine
+        vec_in[seq] = vec_send[seq]
+        begin(vec_copies())
+
+    def sum_vectors():
+        finish(vec_copies())
+        value = vec_in[0]
+        for i in range(1, 8):
+            value = value + vec_in[i]
+        vec_dp[dp] = value
+        begin(vec_dp_copies())
+
+    def finish_vectors():
+        finish(vec_dp_copies())
+        vec_out[...] = (vec_dp[0] + vec_dp[1]) + (vec_dp[2] + vec_dp[3])
+
+    def stage(first, second):
+        left[...] = first
+        right[...] = second
+
+    def strided(b):
+        blocks = []
+        for e in range(2):
+            at = pl.ds(pl.multiple_of((b * 2 + e) * 128, 128), 128)
+            blocks += [pre_grads[j, :, at] for j in range(4)]
+        return jnp.concatenate(blocks, axis=1)
+
+    def step_work(step, _):
+        sum_step(step)
+
+        def at(first, count=1):
+            return pl.when((step >= first) & (step < first + count))
+
+        @at(0)
+        def _():
+            load(0, REAR_DOWN).start()
+            load(1, REAR_UP).start()
+            fetch_pre(pre_r, 0).start()
+            fetch(after_rear).start()
+            prepare()
+            fetch(after_rear).wait()
+            result[...] = low(norm_rows(v_buf[...], vector(5), vector(11)))
+            grad[...] = norm_back(v_buf[...], 5, f32(cotangent[...]))
+            branch[...] = low(0.5 * grad[...])
+            fetch(after_conv).start()
+
+        @at(0, 2)
+        def _():
+            for e in range(2):
+                j = step * 2 + e
+                half_back(j, pre_r, REAR_UP, REAR_DOWN)
+
+                @pl.when(j < 3)
+                def _():
+                    load(0, REAR_DOWN + j + 1).start()
+                    load(1, REAR_UP + j + 1).start()
+                    fetch_pre(pre_r, j + 1).start()
+
+        @at(1)
+        def _():
+            fetch(after_conv).wait()
+            grad[...] += norm_back(v_buf[...], 4, total[...])
+            conv_branch[...] = low(grad[...])
+            fetch(mixed).start()
+            load(0, POINT_OUT).start()
+
+        @at(2)
+        def _():
+            act_grad = nt(conv_branch[...], weight(0, POINT_OUT))
+            fetch(mixed).wait()
+            act_grad = silu_slope(norm_rows(v_buf[...], vector(3), vector(9)), act_grad)
+            value = low(norm_back(v_buf[...], 3, act_grad))
+            mixed_w[:, HALO : HALO + frame_count] = value.reshape(rows, frame_count, width)
+
+            @pl.when(seq > 0)
+            def _():
+                halo_copy(0).start()
+
+            @pl.when(seq < 7)
+            def _():
+                halo_copy(1).start()
+
+            fetch(after_attend).start()
+            load(0, POINT_IN).start()
+            load(1, POINT_IN + 1).start()
+
+        @at(3)
+        def _():
+            @pl.when(seq > 0)
+            def _():
+                halo_copy(0).wait_send()
+                halo_copy(1).wait_recv()
+
+            @pl.when(seq < 7)
+            def _():
+                halo_copy(1).wait_send()
+                halo_copy(0).wait_recv()
+
+            mixed_f[...] = f32(mixed_w[...])
+            convolve_back(0)
+
+        @at(4)
+        def _():
+            convolve_back(1)
+
+        @at(5)
+        def _():
+            gate = logistic(f32(conv_pre[1]))
+            gate_grads[0] = low(total[...] * gate)
+            gate_grads[1] = low(total[...] * f32(conv_pre[0]) * gate * (1.0 - gate))
+            norm_grad = nt(gate_grads[0], weight(0, POINT_IN))
+            load(0, ATTEND_OUT).start()
+            norm_grad = norm_grad + nt(gate_grads[1], weight(1, POINT_IN + 1))
+            fetch(after_attend).wait()
+            grad[...] += norm_back(v_buf[...], 2, norm_grad)
+            attend_branch[...] = low(grad[...])
+            fetch(after_front).start()
+            value = low(nt(attend_branch[...], weight(0, ATTEND_OUT)))
+            for s in range(8):
+                g_out[s] = value[:, s * 128 : s * 128 + 128].reshape(rows, frame_count, 128)
+            g_in[seq] = g_out[seq]
+            for k in range(1, 8):
+                ga_copy(k).start()
+            load(0, PROJECT).start()
+            load(1, PROJECT + 1).start()
+
+        @at(7)
+        def _():
+            for k in range(1, 8):
+                ga_copy(k, True).wait_recv()
+                ga_copy(k).wait_send()
+
+        @at(7, 4)
+        def _():
+            attend_back_step((step - 7) * 2)
+            attend_back_step((step - 7) * 2 + 1)
+
+        @at(12)
+        def _():
+            for c in range(3):
+                for r in range(rows):
+                    for k in range(1, 8):
+                        pk_copy(peer(k), c, r, True).wait_recv()
+                        pk_copy(peer(k), c, r).wait_send()
+                for s in range(8):
+                    parts[c, :, s * 128 : s * 128 + 128] = p_in[s, c].reshape(
+                        rows * frame_count, 128
+                    )
+            norm_grad = nt(parts[0], weight(0, PROJECT))
+            load(0, PROJECT + 2).start()
+            norm_grad = norm_grad + nt(parts[1], weight(1, PROJECT + 1))
+            load(1, UP).start()
+            fetch_pre(pre_f, 0).start()
+            norm_grad = norm_grad + nt(parts[2], weight(0, PROJECT + 2))
+            load(0, DOWN).start()
+            fetch(after_front).wait()
+            grad[...] += norm_back(v_buf[...], 1, norm_grad)
+            branch[...] = low(0.5 * grad[...])
+
+        @at(13, 4)
+        def _():
+            j = step - 13
+            half_back(j, pre_f, UP, DOWN)
+
+            @pl.when(j < 3)
+            def _():
+                load(0, DOWN + j + 1).start()
+                load(1, UP + j + 1).start()
+                fetch_pre(pre_f, j + 1).start()
+
+        @at(17)
+        def _():
+            frames_grad[...] = low(
+                grad[...] + norm_back(f32(frames[...]), 0, total[...])
+            )
+            send_vectors()
+
+        @at(19)
+        def _():
+            sum_vectors()
+
+        @at(21)
+        def _():
+            finish_vectors()
+
+        @at(0)
+        def _():
+            fetch_hid(hid_r, 0).start()
+
+        @at(0, JOB_RU)
+        def _():
+            fetch_hid(hid_r, step).wait()
+            stage(hid_buf[...], branch[...])
+
+            @pl.when(step < 3)
+            def _():
+                fetch_hid(hid_r, step + 1).start()
+
+        @at(JOB_RU, 4)
+        def _():
+            stage(norm4[...], strided(step - JOB_RU))
+
+        @at(JOB_PO)
+        def _():
+            stage(act[...], conv_branch[...])
+
+        @at(JOB_PI, 2)
+        def _():
+            stage(norm2[...], gate_grads[step - JOB_PI])
+
+        @at(JOB_AO)
+        def _():
+            stage(attended[...], attend_branch[...])
+
+        @at(JOB_P, 3)
+        def _():
+            stage(norm1[...], parts[step - JOB_P])
+
+        @at(JOB_FD - 1)
+        def _():
+            fetch_hid(hid_f, 0).start()
+
+        @at(JOB_FD, 4)
+        def _():
+            fetch_hid(hid_f, step - JOB_FD).wait()
+            stage(hid_buf[...], branch[...])
+
+            @pl.when(step < JOB_FD + 3)
+            def _():
+                fetch_hid(hid_f, step - JOB_FD + 1).start()
+
+        @at(JOB_FU, 4)
+        def _():
+            stage(norm0[...], strided(step - JOB_FU))
+
+        @at(0, JOBS)
+        def _():
+            product(step, lax.rem(step, RING))
+
+        return 0
+
+    lax.fori_loop(0, JOBS + OUT_LAG, step_work, 0)
+    out_copy(JOBS - 2).wait()
+    out_copy(JOBS - 1).wait()
+
+
+def backward_layer(saved, frames, cotangent, slopes):
+    bf16, single = jnp.bfloat16, jnp.float32
+    tokens, width = frames.shape
+    dma = pltpu.SemaphoreType.DMA
+    vmem, hbm = pl.BlockSpec(memory_space=pltpu.VMEM), pl.BlockSpec(memory_space=pltpu.HBM)
+    kept = (0, 4, 5, 6, 10, 14, 16, 18, 19, 20)
+
+    def buf(kind, *sizes):
+        return pltpu.VMEM(sizes, kind)
+
+    low_buf, wide_buf = buf(bf16, tokens, width), buf(single, tokens, width)
+    frame_count = 128
+    tall = frame_count + 2 * HALO
+    return pl.pallas_call(
+        backward_kernel,
+        in_specs=[hbm if i in kept else vmem for i in range(21)]
+        + [vmem, vmem, pl.BlockSpec(memory_space=pltpu.SMEM)],
+        out_specs=[vmem, vmem, hbm, vmem],
+        out_shape=[
+            jax.ShapeDtypeStruct((tokens, width), bf16),
+            jax.ShapeDtypeStruct((tokens, width), bf16),
+            jax.ShapeDtypeStruct((JOBS, 128, width), single),
+            jax.ShapeDtypeStruct((VECTORS, 128), single),
+        ],
+        scratch_shapes=[
+            buf(bf16, 2, 8, 128, width),
+            low_buf,
+            low_buf,
+            wide_buf,
+            buf(single, VECTORS, width),
+            buf(single, VECTORS, width),
+            low_buf,
+            low_buf,
+            low_buf,
+            buf(bf16, 4, tokens, width),
+            low_buf,
+            buf(bf16, 2, tokens, width),
+            low_buf,
+            buf(bf16, 3, tokens, width),
+            wide_buf,
+            wide_buf,
+            buf(single, 2, tall, width),
+            buf(bf16, 2, tall, width),
+            buf(single, 2, tall, width),
+            buf(single, 2, tall, 128),
+            buf(single, 2, 1024, 1),
+            buf(single, 8, 1024),
+            buf(bf16, 8, 2, 128, 128),
+            buf(bf16, 8, 2, 128, 128),
+            buf(bf16, 8, 3, 2, 128, 128),
+            buf(bf16, 8, 3, 2, 128, 128),
+            buf(single, 1024, 128),
+            buf(single, 1024, 128),
+            buf(single, 8, QUERIES),
+            buf(single, 2, 128, width),
+            buf(bf16, 2, 4, 128, width),
+            buf(bf16, 4, 2, 2, PIECE, width),
+            buf(bf16, 2, 2, PIECE, width),
+            buf(bf16, 2, 2, PIECE, width),
+            buf(bf16, 4, PIECE, width),
+            buf(bf16, RING, 4, 128, width),
+            buf(bf16, RING, 2, 2, PIECE, width),
+            buf(bf16, RING, 2, 2, PIECE, width),
+            buf(bf16, RING, 2, PIECE, width),
+            buf(bf16, RING, 2, PIECE, width),
+            buf(bf16, RING, 3, PIECE, width),
+            buf(bf16, RING, 4, PIECE, width),
+            buf(single, 8, VECTORS, 128),
+            buf(single, 8, VECTORS, 128),
+            buf(single, 4, VECTORS, 128),
+            dma((2, 12, RING)),
+            dma((2, 10)),
+            dma((2,)),
+            dma((1,)),
+            dma((1,)),
+            dma((1,)),
+            dma((2, 8)),
+            dma((2, 8, 3, 2)),
+            dma((2, 2)),
+            dma((2,)),
+        ],
+        compiler_params=pltpu.CompilerParams(
+            collective_id=1, has_side_effects=True, vmem_limit_bytes=62 * 2**20
+        ),
+        name="backward_layer",
+    )(*saved, frames, cotangent, slopes)
+
+
+def body_staged(
+    frames,
+    segments,
+    cotangent,
+    norm_gains,
+    norm_biases,
+    front_up,
+    front_down,
+    attend_in,
+    attend_out,
+    slopes,
+    point_in,
+    depthwise,
+    point_out,
+    rear_up,
+    rear_down,
+):
+    row_count, frame_count, width = frames.shape
+    token_count = row_count * frame_count
+    seq = lax.axis_index("seq")
+    taps = depthwise.shape[0]
+
+    def wide(shard):
+        return shard.reshape(128, -1, width).transpose(1, 0, 2)
+
+    def dealt(shard):
+        return shard.reshape(128, 8, 4, 128).transpose(2, 0, 1, 3).reshape(4, 128, width)
+
+    shards = jnp.concatenate(
+        [
+            dealt(front_up),
+            front_down.reshape(4, 128, width),
+            wide(attend_in),
+            wide(attend_out),
+            wide(point_in),
+            wide(point_out),
+            dealt(rear_up),
+            rear_down.reshape(4, 128, width),
+        ]
+    )
+    vector_shard = jnp.concatenate([norm_gains, norm_biases, depthwise])
+    vector_shard = jnp.pad(vector_shard, ((0, VECTORS - vector_shard.shape[0]), (0, 0)))
+    segment_shard = jnp.pad(segments, ((0, 8 - row_count), (0, 0)))
+    my_slopes = lax.dynamic_slice_in_dim(slopes, seq * 2, 2, 0)
+    tokens = frames.reshape(token_count, width)
+    saved = forward_layer(shards, vector_shard, segment_shard, tokens, my_slopes)
+    result, frames_grad, shares, vectors = backward_layer(
+        saved, tokens, cotangent.reshape(token_count, width), my_slopes
+    )
+
+    def beside(first, count):
+        return jnp.concatenate([shares[first + i] for i in range(count)], axis=1)
+
+    def below(first):
+        return shares[first : first + 4].reshape(-1, width)
+
+    return (
+        result.reshape(frames.shape),
+        frames_grad.reshape(frames.shape),
+        vectors[:6],
+        vectors[6:12],
+        beside(JOB_FU, 4),
+        below(JOB_FD),
+        beside(JOB_P, 3),
+        shares[JOB_AO],
+        vectors[12 + taps, : slopes.shape[0]],
+        beside(JOB_PI, 2),
+        vectors[12 : 12 + taps],
+        shares[JOB_PO],
+        beside(JOB_RU, 4),
+        below(0),
+    )
+
+
 def solution(mesh):
     placed = (
         P("dp", "seq", None),
@@ -470,8 +1813,10 @@
         P("seq", None),
         P("seq", None),
     )
+    sizes = mesh.shape
+    staged = sizes["dp"] == 4 and sizes["seq"] == 8
     return jax.shard_map(
-        body,
+        body_staged if staged else body,
         mesh=mesh,
         in_specs=placed,
         out_specs=(

time: 1740 us -> 584 us (0.34)
  waiting for transfers between devices: 1170 us -> 0 us
  Pallas kernels: 0 us -> 540 us
  matrix products: 233 us -> 0 us
  other arithmetic: 123 us -> 5.91 us
  blocking collectives: 79.5 us -> 0 us
  starting transfers between devices: 42.3 us -> 0 us
  local copies, waits for them, and re-layouts: 61.1 us -> 33.2 us
    pallas_call x0 -> x2, Pallas kernels: none -> 540 us  [the longest x1 309 us: backward_layer(): pl.pallas_call(backward_kernel, in_specs=[hbm if i in kept else vmem for...]
    all_gather x10 -> x0, waiting for transfers between devices: 431 us -> none  [the longest x1 81 us: body(): lax.all_gather(rear_up, 'seq', axis=0, tiled=True)]
    reduce_scatter x8 -> x0, waiting for transfers between devices: 365 us -> none  [the longest x1 90.2 us: body(): lax.psum_scatter(rear_down_grad.astype(jnp.bfloat16), 'seq', scatter_dime...]
    dot_general x74 -> x0, matrix products: 233 us -> none  [the longest x9 29.5 us: score_block(): jnp.einsum('rqhd,rkhd->rqhk', query_heads, key_heads, preferred_element_t...]
    ppermute x19 -> x0, waiting for transfers between devices: 169 us -> none  [the longest x15 169 us: shifted(): return lax.ppermute(block, axis, route)]
    psum x1 -> x0, waiting for transfers between devices: 121 us -> none  [body(): lax.psum(shares[2].astype(jnp.bfloat16), 'dp').astype(jnp.float32)]
    unnamed x25 -> x0, waiting for transfers between devices: 81.9 us -> none
    all_gather x4 -> x0, blocking collectives: 49.8 us -> none  [the longest x1 14.5 us: body(): lax.all_gather(norm_biases, 'seq', axis=1, tiled=True)]
  transfers between devices with their start and end apart: 41 -> 0, of which waited for: 35 -> 0; matrix products, arithmetic and copies ran while one was open for 21% -> 0% of each run, Pallas kernels for 0% -> 0%
where the time goes in v2:
time: 584 us; the launch traced here: 580 us
  Pallas kernels  540 us (92%)
  local copies, waits for them, and re-layouts  33.2 us (6%)
  other arithmetic  5.91 us (1%)
    pallas_call x1, Pallas kernels, backward_layer(): pl.pallas_call(backward_kernel, in_specs=[hbm if i in kept else vmem for...  309 us
    pallas_call x1, Pallas kernels, forward_layer(): pl.pallas_call(forward_kernel, in_specs=[vmem, vmem, vmem, vmem, pl.Block...  232 us

profile of v2, /device:TPU:0, one launch (start us, length us, event | category | flops | bytes accessed | tf_op | source)
XLA Modules:
  0.0 580.4 jit_solution(18194793460437959862)
XLA Ops:
  0.7 1.3 dynamic_slice.3.refs_4_.refs_23_
  2.0 1.3 pad.9.refs_2_
  3.2 1.3 fusion.4.refs_1_
  4.6 1.3 copy.34
  5.9 1.0 copy.35
  7.3 1.2 copy.33
  8.5 0.8 reshape.70
  9.4 0.5 reshape.71
  9.9 0.6 copy-done.3
  10.4 0.7 reshape.75
  11.3 0.5 reshape.76
  11.9 1.1 constant_dynamic-update-slice_fusion.3
  12.9 0.5 copy-done.4
  13.5 1.1 constant_dynamic-update-slice_fusion.2
  14.5 0.9 bitcast_dynamic-update-slice_fusion
  15.5 0.7 bitcast_dynamic-update-slice_fusion.3
  16.2 0.8 bitcast_dynamic-update-slice_fusion.1
  17.0 0.7 bitcast_dynamic-update-slice_fusion.2
  17.8 1.1 constant_dynamic-update-slice_fusion.1
  18.8 1.1 constant_dynamic-update-slice_fusion.refs_0_
  19.9 231.7 %forward_layer.1 = (bf16[23,8,128,1024]{3,2,1,0:T(8,128)(2,1)}, bf16[8,48,128]{2,1,0:T(8,128)(2,1)}, s32[8,8,128]{2,1,0:T(8,128)}, bf16[256,1024]{1,0:T(8,128)(2...) custom-call(bf16[23,128,1024]{2,1,0:T(8,128)(2,1)} %constant_dynamic, ...), custom_call_target="tpu_custom_call" | custom-call | tf_op jit(solution)/shard_map/forward_layer/pallas_call | solution.py:1003
  251.6 308.6 %backward_layer.1 = (bf16[256,1024]{1,0:T(8,128)(2,1)}, bf16[256,1024]{1,0:T(8,128)(2,1)}, f32[23,128,1024]{2,1,0:T(8,128)}, f32[48,128]{1,0:T(8,128)}) custom-call(bf16[23,8,128,1024]{3,2,1,0:T(8,128)(2,1)} %get-tuple-element.39.refs_0_, bf16[8,48,128]{2,1,0:T(8,128)(2,1)} %get-tuple-element.40.refs_1_, s32[8,8,128]{2,1,0:T(8,128)} %get-tuple-element.41.refs_2_, ...), custom_call_target="tpu_custom_call" | custom-call | tf_op jit(solution)/shard_map/backward_layer/pallas_call | solution.py:1649
  560.2 1.2 slice_bitcast_fusion.15
  561.4 1.4 fusion.6
  562.8 1.3 slice.77
  564.1 4.8 fusion.5
  568.9 5.1 slice_bitcast_fusion.3
  574.1 2.3 pad_maximum_fusion
  576.4 1.0 pad_maximum_fusion.3
  577.4 1.2 pad_maximum_fusion.2
  578.6 0.8 copy.50
  579.4 0.8 copy.51
  (23 shorter events, 0.7 us)
Async XLA Ops:
  0.6 6.3 %copy-start.6 = (bf16[128,3072]{1,0:T(8,128)(2,1)S(1)}, bf16[128,3072]{1,0:T(8,128)(2,1)}, u32[]{:S(2)}) copy-start(bf16[128,3072]{1,0:T(8,128)(2,1)} %param.22) | copy-start | bytes 2359300
  5.9 2.6 copy-start.2
  9.2 1.2 copy-start.3
  11.9 1.6 copy-start.4
  11.9 2.7 copy-start
  13.5 2.0 copy-start.9
  13.5 2.7 copy-start.1
  14.5 2.5 copy-start.10
  15.5 3.3 copy-start.5
  577.4 1.3 copy-start.8
  577.4 2.1 copy-start.7

commit v3 on v2

--- a/solution.py
+++ b/solution.py
@@ -462,12 +462,6 @@
 QUERIES = 256
 
 
-def log_distance_block(length, start):
-    keys = lax.broadcasted_iota(jnp.int32, (length, QUERIES), 0)
-    queries = lax.broadcasted_iota(jnp.int32, (length, QUERIES), 1) + start
-    return jnp.log(1.0 + jnp.abs(keys - queries).astype(jnp.float32))
-
-
 def head_lanes(value, head, scale=1.0):
     lane = lax.broadcasted_iota(jnp.int32, value.shape, 1)
     mine = (lane >= 64 * head) & (lane < 64 * head + 64)
@@ -481,9 +475,12 @@
 MESH_ID = pl.DeviceIdType.MESH
 PIECE = 32
 HALO = 16
+TILE, TILES = 128, 8
 UP, DOWN, PROJECT, ATTEND_OUT, POINT_IN, POINT_OUT, REAR_UP, REAR_DOWN = 0, 4, 8, 11, 12, 14, 15, 19
 CHUNKS = 23
-LEAD = 3
+TALL = (False, True, False, False, False, False, False, True)
+LEAD = 12
+VMEM_LIMIT = 63 * 2**20
 STAGE = 1
 STEP = 4 * STAGE
 VECTORS = 48
@@ -522,30 +519,77 @@
     )
 
 
-def attend_block(packed, slopes, seg_cols, seg_rows, row, block, length):
-    distance = log_distance_block(length, block * QUERIES)
-    same = seg_cols == seg_rows
-    q = packed[pl.ds(block * 2, 2), 0, row].reshape(QUERIES, 128)
-    k = packed[:, 1, row].reshape(length, 128)
-    value_t = packed[:, 2, row].reshape(length, 128).T
+def attend_block(e, first_head, row, block):
+    q = e.packed[pl.ds(block * 2, 2), 0, row].reshape(QUERIES, 128)
+    value_t = e.packed[:, 2, row].reshape(TILES * TILE, 128).T
+    first = pl.multiple_of(block * QUERIES, QUERIES)
+    query_seg = e.seg_rows[pl.ds(row, 1), pl.ds(first, QUERIES)]
     outs = []
     for head in range(2):
-        logit = nt(k, head_lanes(q, head, 0.125)) - slopes[head] * distance
-        logit = jnp.where(same, logit, -1e30)
-        top = jnp.max(logit, axis=0, keepdims=True)
-        power = jnp.exp(logit - top)
-        total = jnp.sum(power, axis=0, keepdims=True)
-        out = dot(value_t, low(power))
+        q_head = head_lanes(q, head, 0.125)
+        slope = e.slopes[first_head + head]
+        top = jnp.full((1, QUERIES), -1e30, jnp.float32)
+        for kb in range(TILES):
+            logit = logit_tile(e, q_head, slope, query_seg, row, block, kb)[0]
+            e.logits[kb] = logit
+            top = jnp.maximum(top, jnp.max(logit, axis=0, keepdims=True))
+        total = jnp.zeros((1, QUERIES), jnp.float32)
+        for kb in range(TILES):
+            power = jnp.exp(e.logits[kb] - top)
+            total = total + jnp.sum(power, axis=0, keepdims=True)
+            e.scores[kb * TILE : kb * TILE + TILE, :] = low(power)
+        e.log_sum[row, head, :, pl.ds(first, QUERIES)] = top + jnp.log(total)
+        out = dot(value_t, e.scores[...])
         outs.append(out[64 * head : 64 * head + 64] / total)
-    return low(jnp.concatenate(outs, axis=0).T)
-
-
-def forward_kernel(*refs):
-    shards, vec, seg, frames, slopes = refs[:5]
-    (full, vec_all, seg_all, norm0, pre_f, hid_f, after_front, norm1, packed, attended, after_attend) = refs[5:16]
-    (norm2, conv_pre, gated, mixed, act, after_conv, norm4, pre_r, hid_r, after_rear) = refs[16:26]
-    (wbuf, vectors, pk_out, att_out, att_in, gated_f, seg_plane, seg_cols, seg_rows, acc) = refs[26:36]
-    (gather_sem, own_sem, small_sem, pk_sem, att_sem, halo_sem, load_sem) = refs[36:]
+    return jnp.concatenate(outs, axis=0).T
+
+
+def logit_tile(e, q_head, slope, query_seg, row, block, kb):
+    logit = nt(e.packed[kb, 1, row], q_head)
+    distance = jnp.concatenate(
+        [e.distances[kb - 2 * block + TILES - 1], e.distances[kb - 2 * block + TILES - 2]], axis=1
+    )
+    same = e.seg_cols[row, kb * TILE : kb * TILE + TILE, :] == query_seg
+    return jnp.where(same, logit - slope * distance, -1e30), distance
+
+
+def forward_part(e):
+    sources, gains, biases, depth, segments, frames = (
+        e.sources,
+        e.gains,
+        e.biases,
+        e.depth,
+        e.segments,
+        e.frames,
+    )
+    full, vec_all, seg_all, packed, gated, mixed, act = (
+        e.full,
+        e.vec_all,
+        e.seg_all,
+        e.packed,
+        e.gated,
+        e.mixed,
+        e.act,
+    )
+    norm0, norm1, norm2, norm4, attended, conv_pre = (
+        e.norm0,
+        e.norm1,
+        e.norm2,
+        e.norm4,
+        e.attended,
+        e.conv_pre,
+    )
+    after_front, after_attend, after_conv, after_rear = (
+        e.after_front,
+        e.after_attend,
+        e.after_conv,
+        e.after_rear,
+    )
+    pre, hid, wbuf, vectors, shards, acc = e.pre, e.hid, e.wbuf, e.vectors, e.pool, e.total
+    pk_out, att_out, att_in, gated_f = e.pk_out, e.att_out, e.att_in, e.gated_f
+    seg_plane, seg_cols, seg_rows = e.seg_plane, e.seg_cols, e.seg_rows
+    vec_wide, vec, seg = e.vec_wide, e.vec, e.seg
+    gather_sem, own_sem, small_sem, pk_sem, att_sem, halo_sem, load_sem, keep_sem = e.forward_sems
     y, x, z, core = place()
     dp, seq = y * 2 + x, z * 2 + core
     rows, width = 2, 1024
@@ -558,10 +602,33 @@
     def peer(k):
         return lax.rem(seq + k, 8)
 
+    def read(t):
+        first = 0
+        for source, tall in zip(sources, TALL):
+            count = source.shape[0] // 128 if tall else source.shape[1] // width
+            if t < first + count:
+                at = pl.ds((t - first) * (128 if tall else width), 128 if tall else width)
+                where = source.at[at, :] if tall else source.at[:, at]
+                return pltpu.make_async_copy(where, shards.at[t], own_sem.at[3, t])
+            first += count
+
+    def read_done(t):
+        pltpu.make_async_copy(shards.at[t], shards.at[t], own_sem.at[3, t]).wait()
+
+    for t in range(CHUNKS):
+        read(t).start()
+    vec_wide[...] = jnp.zeros_like(vec_wide)
+    vec_wide[0:6, :] = f32(gains[...])
+    vec_wide[6:12, :] = f32(biases[...])
+    vec_wide[12:43, :] = f32(depth[...])
+    vec[...] = low(vec_wide[...])
+    seg[...] = jnp.zeros_like(seg)
+    seg[0:rows, :] = segments[...]
+
     barrier = pltpu.get_barrier_semaphore()
-    for there in [(dp, peer(k)) for k in range(1, 8)] + [over_x, over_y]:
+    for there in [(dp, peer(k)) for k in range(1, 8)] + [(lax.rem(dp + k, 4), seq) for k in (1, 2, 3)]:
         pl.semaphore_signal(barrier, inc=1, device_id=there, device_id_type=MESH_ID)
-    pl.semaphore_wait(barrier, 9)
+    pl.semaphore_wait(barrier, 10)
 
     q_own, q_x, q_y = PIECE * dp, PIECE * (y * 2 + 1 - x), PIECE * ((1 - y) * 2 + x)
 
@@ -595,11 +662,13 @@
     def to_core(t, k):
         return travel(5, t, k, 0, 4 * PIECE, over_core)
 
-    def own_to_core():
-        return remote_copy(shards, full.at[:, seq], own_sem.at[0], own_sem.at[1], over_core)
-
-    def own_to_full():
-        return pltpu.make_async_copy(shards, full.at[:, seq], own_sem.at[2])
+    def own_to_core(t):
+        return remote_copy(
+            shards.at[t], full.at[t, seq], own_sem.at[0, t], own_sem.at[1, t], over_core
+        )
+
+    def own_to_full(t):
+        return pltpu.make_async_copy(shards.at[t], full.at[t, seq], own_sem.at[2, t])
 
     def small_copies():
         copies = []
@@ -618,8 +687,6 @@
 
     for copy in small_copies():
         copy.start()
-    own_to_core().start()
-    own_to_full().start()
     vec_all[seq] = vec[...]
     seg_all[seq] = seg[...]
     def relay(t):
@@ -641,6 +708,9 @@
     relays = (z == 1) | (z == 2)
 
     def start_line(t):
+        read_done(t)
+        own_to_core(t).start()
+        own_to_full(t).start()
         for k in (1, 2, 3):
 
             @pl.when(direct(k))
@@ -705,13 +775,15 @@
         def _():
             for k in (1, 2, 3):
                 to_core(last, k).wait_recv()
+            own_to_core(last).wait_recv()
+            own_to_full(last).wait()
 
     def load(u):
-        return pltpu.make_async_copy(full.at[u], wbuf.at[lax.rem(u, 2)], load_sem.at[lax.rem(u, 2)])
+        return pltpu.make_async_copy(full.at[u], wbuf.at[lax.rem(u, 3)], load_sem.at[lax.rem(u, 3)])
 
     def weight(u):
         load(u).wait()
-        return wbuf[lax.rem(u, 2)].reshape(width, width)
+        return wbuf[lax.rem(u, 3)].reshape(width, width)
 
     def vector(i):
         return vectors[i : i + 1, :]
@@ -720,8 +792,6 @@
         return low(norm_rows(v, vector(i), vector(6 + i)))
 
     def prepare():
-        own_to_full().wait()
-        own_to_core().wait()
         for copy in small_copies():
             copy.wait()
         for s in range(8):
@@ -740,16 +810,25 @@
                 (HALO + frame_count, after[:HALO, r : r + 1]),
             ):
                 seg_plane[r, first : first + col.shape[0], :] = jnp.broadcast_to(col, (col.shape[0], 128))
-        gated[:, :HALO] = jnp.zeros((rows, HALO, width), jnp.bfloat16)
-        gated[:, HALO + frame_count :] = jnp.zeros((rows, HALO, width), jnp.bfloat16)
+        keys = lax.broadcasted_iota(jnp.int32, (TILE, TILE), 0)
+        queries = lax.broadcasted_iota(jnp.int32, (TILE, TILE), 1)
+        for i in range(2 * TILES - 1):
+            apart = jnp.abs(keys - queries + TILE * (i - TILES + 1))
+            e.distances[i] = jnp.log(1.0 + apart.astype(jnp.float32))
         norm0[...] = norm(f32(frames[...]), 0)
 
-    def up(u, j, source, pre, hid):
+    def up(u, j, source):
         value = dot(source[...], weight(u))
-        pre[j] = low(value)
-        hid[j] = low(value * logistic(value))
-
-    def down(u, j, stream, hid, target):
+        active = low(value * logistic(value))
+        value = low(value)
+        for half in range(2):
+            to = pl.ds(pl.multiple_of((j * 2 + half) * 128, 128), 128)
+            for i in range(4):
+                first = half * 512 + i * 128
+                pre[i, :, to] = value[:, first : first + 128]
+                hid[i, :, to] = active[:, first : first + 128]
+
+    def down(u, j, stream, target):
         value = dot(hid[j], weight(u))
 
         @pl.when(j == 0)
@@ -763,6 +842,12 @@
         @pl.when(j == 3)
         def _():
             target[...] = f32(stream[...]) + 0.5 * acc[...]
+
+    def keep_copies():
+        return [
+            pltpu.make_async_copy(pre, e.pre_keep, keep_sem.at[0]),
+            pltpu.make_async_copy(hid, e.hid_keep, keep_sem.at[1]),
+        ]
 
     def pk_copy(c, k, recv=False):
         there = peer(k)
@@ -793,11 +878,9 @@
 
     def attend_step(i):
         row, block = i // 4, lax.rem(i, 4)
-        cols = seg_cols[row]
-        first = pl.multiple_of(block * QUERIES, QUERIES)
-        out = attend_block(
-            packed, slopes, cols, seg_rows[pl.ds(row, 1), pl.ds(first, QUERIES)], row, block, length
-        )
+        out = attend_block(e, seq * 2, row, block)
+        e.att_keep[row, pl.ds(pl.multiple_of(block * QUERIES, QUERIES), QUERIES), :] = out
+        out = low(out)
         for half in range(2):
             b = block * 2 + half
             att_out[b, row] = out[half * 128 : half * 128 + 128]
@@ -835,11 +918,15 @@
             for r in range(rows):
                 own = seg_plane[r, HALO : HALO + frame_count, :]
                 total = jnp.zeros((frame_count, 128), jnp.float32)
-                for tap in range(31):
-                    first = tap + HALO - 15
-                    same = seg_plane[r, first : first + frame_count, :] == own
-                    term = gated_f[r, first : first + frame_count, at] * vectors[12 + tap : 13 + tap, at]
-                    total = total + jnp.where(same, term, 0.0)
+                for shift in range(8):
+                    near = gated_f[r, shift : shift + frame_count + 24, at]
+                    seg_near = seg_plane[r, shift : shift + frame_count + 24, :]
+                    for first in range(0, 32, 8):
+                        tap = shift + first - 1
+                        if 0 <= tap < 31:
+                            same = seg_near[first : first + frame_count] == own
+                            term = near[first : first + frame_count] * vectors[12 + tap : 13 + tap, at]
+                            total = total + jnp.where(same, term, 0.0)
                 mixed[r * frame_count : (r + 1) * frame_count, at] = total
             return 0
 
@@ -859,17 +946,19 @@
 
         @at(1, 4)
         def _():
-            up(now - 1, now - 1, norm0, pre_f, hid_f)
+            up(now - 1, now - 1, norm0)
 
         @at(5, 4)
         def _():
-            down(now - 1, now - 5, frames, hid_f, after_front)
+            down(now - 1, now - 5, frames, after_front)
 
         @at(9, 3)
         def _():
             @pl.when(now == 9)
             def _():
                 norm1[...] = norm(after_front[...], 1)
+                for copy in keep_copies():
+                    copy.start()
 
             project(now - 1, now - 9)
 
@@ -881,8 +970,11 @@
 
         @at(13, 4)
         def _():
-            attend_step((now - 13) * 2)
-            attend_step((now - 13) * 2 + 1)
+            def one(i, _):
+                attend_step((now - 13) * 2 + i)
+                return 0
+
+            lax.fori_loop(0, 2, one, 0)
 
         @at(17)
         def _():
@@ -898,9 +990,6 @@
         def _():
             acc[...] = dot(norm2[...], weight(POINT_IN))
             conv_pre[0] = low(acc[...])
-
-        @at(19)
-        def _():
             gate = dot(norm2[...], weight(POINT_IN + 1))
             conv_pre[1] = low(gate)
             value = low(acc[...] * logistic(gate))
@@ -914,7 +1003,7 @@
             def _():
                 halo_copy(1).start()
 
-        @at(20)
+        @at(19)
         def _():
             convolve()
             value = norm_rows(mixed[...], vector(3), vector(9))
@@ -922,25 +1011,37 @@
             after_conv[...] = after_attend[...] + dot(act[...], weight(POINT_OUT))
             norm4[...] = norm(after_conv[...], 4)
 
-        @at(21, 4)
-        def _():
-            up(now - 21 + REAR_UP, now - 21, norm4, pre_r, hid_r)
-
-        @at(25, 4)
-        def _():
-            down(now - 25 + REAR_DOWN, now - 25, after_conv, hid_r, after_rear)
-
-        @at(0, 11)
-        def _():
-            load(now - 0).start()
-
-        @at(16, 12)
-        def _():
-            load(now - 5).start()
+        @at(20, 2)
+        def _():
+            @pl.when(now == 20)
+            def _():
+                for copy in keep_copies():
+                    copy.wait()
+
+            for i in range(2):
+                j = (now - 20) * 2 + i
+                up(j + REAR_UP, j, norm4)
+
+        @at(22, 2)
+        def _():
+            for i in range(2):
+                j = (now - 22) * 2 + i
+                down(j + REAR_DOWN, j, after_conv, after_rear)
+
+        @at(0, 14)
+        def _():
+            load(now).start()
+
+        for when, chunks in ((17, (14,)), (18, (15, 16)), (19, (17,)), (20, (18, 19)), (21, (20, 21)), (22, (22,))):
+
+            @at(when)
+            def _(chunks=chunks):
+                for u in chunks:
+                    load(u).start()
 
         return 0
 
-    lax.fori_loop(0, STEP + 29, step_work, 0)
+    lax.fori_loop(0, STEP + 24, step_work, 0)
 
     def drain(t, _):
         for kind in (to_x, to_y, on_x, on_y, to_core):
@@ -956,6 +1057,7 @@
         def _():
             relay(t).wait_send()
 
+        own_to_core(t).wait_send()
         return 0
 
     lax.fori_loop(0, CHUNKS, drain, 0)
@@ -967,72 +1069,9 @@
             att_copy(peer(k), r).wait_send()
 
 
-def forward_layer(shards, vec, seg, frames, slopes):
-    bf16, tokens, width = jnp.bfloat16, frames.shape[0], frames.shape[1]
-    dma = pltpu.SemaphoreType.DMA
-
-    def shape(kind, *sizes):
-        return jax.ShapeDtypeStruct(sizes, kind)
-
-    plain, single = shape(bf16, tokens, width), shape(jnp.float32, tokens, width)
-    four = shape(bf16, 4, tokens, width)
-    outs = [
-        shape(bf16, CHUNKS, 8, 128, width),
-        shape(bf16, 8, VECTORS, 128),
-        shape(jnp.int32, 8, 8, 128),
-        plain,
-        four,
-        four,
-        single,
-        plain,
-        shape(bf16, 8, 3, 2, 128, 128),
-        plain,
-        single,
-        plain,
-        shape(bf16, 2, tokens, width),
-        shape(bf16, 2, 128 + 2 * HALO, width),
-        single,
-        plain,
-        single,
-        plain,
-        four,
-        four,
-        single,
-    ]
-    vmem, hbm = pl.BlockSpec(memory_space=pltpu.VMEM), pl.BlockSpec(memory_space=pltpu.HBM)
-    return pl.pallas_call(
-        forward_kernel,
-        in_specs=[vmem, vmem, vmem, vmem, pl.BlockSpec(memory_space=pltpu.SMEM)],
-        out_specs=[hbm] + [vmem] * (len(outs) - 1),
-        out_shape=outs,
-        scratch_shapes=[
-            pltpu.VMEM((2, 8, 128, width), bf16),
-            pltpu.VMEM((VECTORS, width), jnp.float32),
-            pltpu.VMEM((8, 3, 2, 128, 128), bf16),
-            pltpu.VMEM((8, 2, 128, 128), bf16),
-            pltpu.VMEM((8, 2, 128, 128), bf16),
-            pltpu.VMEM((2, 128 + 2 * HALO, width), jnp.float32),
-            pltpu.VMEM((2, 128 + 2 * HALO, 128), jnp.float32),
-            pltpu.VMEM((2, 1024, 1), jnp.float32),
-            pltpu.VMEM((8, 1024), jnp.float32),
-            pltpu.VMEM((tokens, width), jnp.float32),
-            dma((2, 7, CHUNKS, 3)),
-            dma((3,)),
-            dma((2, 2, 7)),
-            dma((2, 8, 3)),
-            dma((2, 8, 2)),
-            dma((2, 2)),
-            dma((2,)),
-        ],
-        compiler_params=pltpu.CompilerParams(
-            collective_id=0, has_side_effects=True, vmem_limit_bytes=60 * 2**20
-        ),
-        name="forward_layer",
-    )(shards, vec, seg, frames, slopes)
-
-
 JOB_RU, JOB_PO, JOB_PI, JOB_AO, JOB_P, JOB_FD, JOB_FU, JOBS = 4, 8, 9, 11, 12, 15, 19, 23
 RING = 4
+GRADS = ((7, True), (6, False), (5, False), (4, False), (3, False), (2, False), (1, True), (0, False))
 OUT_LAG = 6
 
 
@@ -1045,18 +1084,35 @@
     return lax.dot_general(a, b, (((0,), (0,)), ((), ())), preferred_element_type=jnp.float32)
 
 
-def backward_kernel(*refs):
-    (full, vec_all, seg_all, norm0, pre_f, hid_f, after_front, norm1, packed, attended, after_attend) = refs[:11]
-    (norm2, conv_pre, gated, mixed, act, after_conv, norm4, pre_r, hid_r, after_rear) = refs[11:21]
-    (frames, cotangent, slopes) = refs[21:24]
-    (result, frames_grad, shares, vec_out) = refs[24:28]
-    (wbuf, pre_buf, hid_buf, v_buf, vectors, small, left, right) = refs[28:36]
-    (branch, pre_grads, conv_branch, gate_grads, attend_branch, parts) = refs[36:42]
-    (grad, total, gated_f, mixed_w, mixed_f, seg_plane, seg_cols, seg_rows) = refs[42:50]
-    (g_out, g_in, p_out, p_in, key_sum, value_sum, slope_sum, out_buf) = refs[50:58]
-    (g_buf, h_buf, a_buf, b_buf, q_buf, core_in, a_in, b_in, a2_in, b2_in, z_in, o_buf) = refs[58:70]
-    (vec_send, vec_in, vec_dp) = refs[70:73]
-    (sem, vec_sem, load_sem, pre_sem, hid_sem, v_sem, ga_sem, pk_sem, halo_sem, out_sem) = refs[73:]
+def backward_part(e):
+    full, gated, mixed, act, packed = e.full, e.gated, e.mixed, e.act, e.packed
+    norm0, norm1, norm2, norm4, attended, conv_pre = (
+        e.norm0,
+        e.norm1,
+        e.norm2,
+        e.norm4,
+        e.attended,
+        e.conv_pre,
+    )
+    after_front, after_attend, after_conv, after_rear = (
+        e.after_front,
+        e.after_attend,
+        e.after_conv,
+        e.after_rear,
+    )
+    frames, cotangent, slopes = e.frames, e.cotangent, e.slopes
+    result, frames_grad, vec_out, grads = e.result, e.frames_grad, e.vec_out, e.grads
+    pre_grads, hid, wbuf, vectors, pool = e.pre, e.hid, e.wbuf, e.vectors, e.pool
+    small, left, right, branch, conv_branch = e.small, e.left, e.right, e.branch, e.conv_branch
+    gate_grads, attend_branch, parts = e.gate_grads, e.attend_branch, e.parts
+    grad, total, gated_f, mixed_w, mixed_f = e.grad, e.total, e.gated_f, e.mixed_w, e.mixed_f
+    seg_plane, seg_rows = e.seg_plane, e.seg_rows
+    g_out, g_in, p_out, p_in = e.att_out, e.g_in, e.pk_out, e.p_in
+    key_sum, value_sum, slope_sum, out_buf = e.key_sum, e.value_sum, e.slope_sum, e.out_buf
+    h_buf, a_buf, b_buf, q_buf = e.h_buf, e.a_buf, e.b_buf, e.q_buf
+    a_in, b_in, a2_in, b2_in, z_in, o_buf = e.a_in, e.b_in, e.a2_in, e.b2_in, e.z_in, e.o_buf
+    vec_send, vec_in, vec_dp = e.vec_send, e.vec_in, e.vec_dp
+    sem, vec_sem, load_sem, keep_sem, ga_sem, pk_sem, halo_sem, out_sem, sync = e.backward_sems
     y, x, z, core = place()
     dp, seq = y * 2 + x, z * 2 + core
     rows, width, frame_count = 2, 1024, 128
@@ -1071,12 +1127,9 @@
     def dp_peer(k):
         return (lax.rem(dp + k, 4), seq)
 
-    mixed_w[:, :HALO] = jnp.zeros((rows, HALO, width), jnp.bfloat16)
-    mixed_w[:, HALO + frame_count :] = jnp.zeros((rows, HALO, width), jnp.bfloat16)
-    barrier = pltpu.get_barrier_semaphore()
-    for there in [(dp, peer(k)) for k in range(1, 8)] + [dp_peer(k) for k in range(1, 4)]:
-        pl.semaphore_signal(barrier, inc=1, device_id=there, device_id_type=MESH_ID)
-    pl.semaphore_wait(barrier, 10)
+    pl.semaphore_signal(sync, inc=1, device_id=over_core, device_id_type=MESH_ID)
+    pl.semaphore_wait(sync, 1)
+    mine = 4 * RING
 
     def remote(src, dst, t, slot, there):
         return remote_copy(
@@ -1084,7 +1137,9 @@
         )
 
     def core_copies(t, r):
-        return [remote(g_buf.at[1], core_in.at[r], t, 0, over_core)]
+        return [
+            remote(pool.at[pl.ds(mine + 4, 4)], pool.at[pl.ds(4 * r, 4)], t, 0, over_core)
+        ]
 
     def first_copies(t, r):
         return [
@@ -1114,9 +1169,25 @@
         two = o_buf.at[r, y * 2 + 1 - x, pl.ds(PIECE // 2, PIECE // 2)]
         return [remote(one, one, t, 10, over_x), remote(two, two, t, 11, over_y)]
 
-    def out_copy(t):
+    def out_start(t):
         slot = lax.rem(t, 2)
-        return pltpu.make_async_copy(out_buf.at[slot], shares.at[t], out_sem.at[slot])
+        first = 0
+        for out, tall in GRADS:
+            ref = grads[out]
+            size = 128 if tall else width
+            count = ref.shape[0] // size if tall else ref.shape[1] // size
+
+            @pl.when((t >= first) & (t < first + count))
+            def _(ref=ref, tall=tall, size=size, first=first):
+                at = pl.ds(pl.multiple_of((t - first) * size, size), size)
+                where = ref.at[at, :] if tall else ref.at[:, at]
+                pltpu.make_async_copy(out_buf.at[slot], where, out_sem.at[slot]).start()
+
+            first += count
+
+    def out_done(t):
+        slot = lax.rem(t, 2)
+        pltpu.make_async_copy(out_buf.at[slot], out_buf.at[slot], out_sem.at[slot]).wait()
 
     def finish(copies):
         for copy in copies:
@@ -1131,10 +1202,10 @@
 
         @pl.when(t >= 2)
         def _():
-            out_copy(t - 2).wait()
+            out_done(t - 2)
 
         out_buf[lax.rem(t, 2)] = f32(o_buf[r].reshape(128, width))
-        out_copy(t).start()
+        out_start(t)
 
     def pass_on(t, r):
         finish(share_copies(t, r))
@@ -1161,14 +1232,14 @@
     def total_core(t, r):
         finish(core_copies(t, r))
         for i in range(4):
-            value = low(f32(g_buf[0, i]) + f32(core_in[r, i]))
+            value = low(f32(pool[mine + i]) + f32(pool[4 * r + i]))
             h_buf[i] = value.reshape(2, 2, PIECE, width)
         begin(first_copies(t, r))
 
     def product(t, r):
         for i in range(8):
             part = tn(left[:, 128 * i : 128 * i + 128], right[...])
-            g_buf[lax.rem(core + i, 2), i // 2] = low(part)
+            pool[mine + 4 * lax.rem(core + i, 2) + i // 2] = low(part)
         begin(core_copies(t, r))
 
     sums = [total_core, total_first, total_second, total_line, pass_on, write_out]
@@ -1188,14 +1259,11 @@
         load(i, u).wait()
         return wbuf[i].reshape(width, width)
 
-    def fetch_pre(source, j):
-        return pltpu.make_async_copy(source.at[j], pre_buf, pre_sem.at[0])
-
-    def fetch_hid(source, j):
-        return pltpu.make_async_copy(source.at[j], hid_buf, hid_sem.at[0])
-
-    def fetch(source):
-        return pltpu.make_async_copy(source, v_buf, v_sem.at[0])
+    def keep_copies():
+        return [
+            pltpu.make_async_copy(e.pre_keep, pre_grads, keep_sem.at[0]),
+            pltpu.make_async_copy(e.hid_keep, hid, keep_sem.at[1]),
+        ]
 
     def vector(i):
         return vectors[i : i + 1, :]
@@ -1211,42 +1279,31 @@
         second = jnp.mean(dn * n, axis=-1, keepdims=True)
         return rstd * (dn - first - n * second)
 
-    def half_back(j, pre, up, down):
-        hidden_grad = nt(branch[...], weight(0, down + j))
-        fetch_pre(pre, j).wait()
-        pre_grads[j] = low(silu_slope(f32(pre_buf[...]), hidden_grad))
-        value = nt(pre_grads[j], weight(1, up + j))
-
-        @pl.when(j == 0)
+    def strided(b):
+        blocks = []
+        for half in range(2):
+            at = pl.ds(pl.multiple_of((b * 2 + half) * 128, 128), 128)
+            blocks += [pre_grads[j, :, at] for j in range(4)]
+        return jnp.concatenate(blocks, axis=1)
+
+    def down_back(j, down):
+        hidden_grad = nt(branch[...], weight(lax.rem(j, 2), down + j))
+        pre_grads[j] = low(silu_slope(f32(pre_grads[j]), hidden_grad))
+
+    def up_back(b, up):
+        value = nt(strided(b), weight(lax.rem(b, 2), up + b))
+
+        @pl.when(b == 0)
         def _():
             total[...] = value
 
-        @pl.when(j > 0)
+        @pl.when(b > 0)
         def _():
             total[...] += value
 
     def prepare():
         small[...] = jnp.zeros_like(small)
         slope_sum[...] = jnp.zeros_like(slope_sum)
-        for s in range(8):
-            vectors[:, s * 128 : s * 128 + 128] = f32(vec_all[s])
-            columns = f32(seg_all[s]).T
-            for r in range(rows):
-                seg_cols[r, s * 128 : s * 128 + 128, :] = columns[:, r : r + 1]
-                seg_rows[r : r + 1, s * 128 : s * 128 + 128] = f32(seg_all[s, r : r + 1, :])
-        before = jnp.where(seq > 0, f32(seg_all[lax.max(seq - 1, 0)]), -1.0).T
-        middle = f32(seg_all[seq]).T
-        after = jnp.where(seq < 7, f32(seg_all[lax.min(seq + 1, 7)]), -1.0).T
-        for r in range(rows):
-            for first, col in (
-                (0, before[frame_count - HALO :, r : r + 1]),
-                (HALO, middle[:, r : r + 1]),
-                (HALO + frame_count, after[:HALO, r : r + 1]),
-            ):
-                seg_plane[r, first : first + col.shape[0], :] = jnp.broadcast_to(
-                    col, (col.shape[0], 128)
-                )
-        gated_f[...] = f32(gated[...])
 
     def halo_copy(side):
         if side == 0:
@@ -1269,13 +1326,20 @@
             own = seg_plane[r, HALO : HALO + frame_count, :]
             mine = mixed_f[r, HALO : HALO + frame_count, at]
             value = jnp.zeros((frame_count, 128), jnp.float32)
-            for tap in range(31):
-                first = tap + HALO - 15
-                same = seg_plane[r, first : first + frame_count, :] == own
-                near = jnp.where(same, gated_f[r, first : first + frame_count, at], 0.0)
-                small[12 + tap : 13 + tap, at] += jnp.sum(near * mine, axis=0, keepdims=True)
-                came = jnp.where(same, mixed_f[r, first : first + frame_count, at], 0.0)
-                value = value + came * vectors[12 + 30 - tap : 13 + 30 - tap, at]
+            for shift in range(8):
+                window = slice(shift, shift + frame_count + 24)
+                seg_near = seg_plane[r, window, :]
+                gated_near = gated_f[r, window, at]
+                mixed_near = mixed_f[r, window, at]
+                for first in range(0, 32, 8):
+                    tap = shift + first - 1
+                    if 0 <= tap < 31:
+                        here = slice(first, first + frame_count)
+                        same = seg_near[here] == own
+                        near = jnp.where(same, gated_near[here], 0.0)
+                        small[12 + tap : 13 + tap, at] += jnp.sum(near * mine, axis=0, keepdims=True)
+                        came = jnp.where(same, mixed_near[here], 0.0)
+                        value = value + came * vectors[12 + 30 - tap : 13 + 30 - tap, at]
             total[r * frame_count : (r + 1) * frame_count, at] = value
             return 0
 
@@ -1303,13 +1367,11 @@
     def attend_back_step(i):
         row, block = i // 4, lax.rem(i, 4)
         first = pl.multiple_of(block * QUERIES, QUERIES)
-        distance = log_distance_block(length, block * QUERIES)
-        same = seg_cols[row] == seg_rows[pl.ds(row, 1), pl.ds(first, QUERIES)]
+        query_seg = seg_rows[pl.ds(row, 1), pl.ds(first, QUERIES)]
         q = packed[pl.ds(block * 2, 2), 0, row].reshape(QUERIES, 128)
-        k = packed[:, 1, row].reshape(length, 128)
-        v = packed[:, 2, row].reshape(length, 128)
         g = g_in[pl.ds(block * 2, 2), row].reshape(QUERIES, 128)
-        key_t = k.T
+        key_t = packed[:, 1, row].reshape(length, 128).T
+        deltas = (f32(g) * e.att_keep[row, pl.ds(first, QUERIES), :]).T
 
         @pl.when(block == 0)
         def _():
@@ -1320,20 +1382,25 @@
         for head in range(2):
             q_head = head_lanes(q, head, 0.125)
             g_head = head_lanes(g, head)
-            logit = nt(k, q_head) - slopes[head] * distance
-            logit = jnp.where(same, logit, -1e30)
-            top = jnp.max(logit, axis=0, keepdims=True)
-            power = jnp.exp(logit - top)
-            prob = power * (1.0 / jnp.sum(power, axis=0, keepdims=True))
-            prob_grad = nt(v, g_head)
-            delta = jnp.sum(prob * prob_grad, axis=0, keepdims=True)
-            logit_grad = prob * (prob_grad - delta)
-            slope = jnp.sum(logit_grad * distance, axis=0, keepdims=True)
-            slope_sum[head : head + 1, :] -= slope
-            score = low(logit_grad)
-            key_sum[...] += dot(score, q_head)
-            value_sum[...] += dot(low(prob), g_head)
-            query_t = dot(key_t, score)
+            slope = slopes[seq * 2 + head]
+            log_sum = e.log_sum[row, head, :, pl.ds(first, QUERIES)]
+            delta = jnp.sum(deltas[64 * head : 64 * head + 64], axis=0, keepdims=True)
+            slope_total = jnp.zeros((8, QUERIES), jnp.float32)
+            for kb in range(TILES):
+                at = slice(kb * TILE, kb * TILE + TILE)
+                logit, distance = logit_tile(e, q_head, slope, query_seg, row, block, kb)
+                prob = jnp.exp(logit - log_sum)
+                prob_grad = nt(packed[kb, 2, row], g_head)
+                value_sum[at, :] += dot(low(prob), g_head)
+                logit_grad = prob * (prob_grad - delta)
+                slope_total = slope_total + jnp.sum(
+                    (logit_grad * distance).reshape(TILE // 8, 8, QUERIES), axis=0
+                )
+                score = low(logit_grad)
+                e.scores[at, :] = score
+                key_sum[at, :] += dot(score, q_head)
+            slope_sum[head] -= slope_total
+            query_t = dot(key_t, e.scores[...])
             outs.append(query_t[64 * head : 64 * head + 64] * 0.125)
         query = low(jnp.concatenate(outs, axis=0).T)
 
@@ -1383,7 +1450,7 @@
         lane = lax.broadcasted_iota(jnp.int32, (1, 128), 1)
         mine = jnp.zeros((1, 128), jnp.float32)
         for head in range(2):
-            value = jnp.sum(slope_sum[head : head + 1, :], axis=-1, keepdims=True)
+            value = jnp.sum(jnp.sum(slope_sum[head], axis=0, keepdims=True), axis=-1, keepdims=True)
             mine = mine + jnp.where(lane == seq * 2 + head, value, 0.0)
         for s in range(8):
             vec_send[s] = small[:, s * 128 : s * 128 + 128]
@@ -1407,13 +1474,6 @@
         left[...] = first
         right[...] = second
 
-    def strided(b):
-        blocks = []
-        for e in range(2):
-            at = pl.ds(pl.multiple_of((b * 2 + e) * 128, 128), 128)
-            blocks += [pre_grads[j, :, at] for j in range(4)]
-        return jnp.concatenate(blocks, axis=1)
-
     def step_work(step, _):
         sum_step(step)
 
@@ -1423,42 +1483,30 @@
         @at(0)
         def _():
             load(0, REAR_DOWN).start()
-            load(1, REAR_UP).start()
-            fetch_pre(pre_r, 0).start()
-            fetch(after_rear).start()
+            load(1, REAR_DOWN + 1).start()
             prepare()
-            fetch(after_rear).wait()
-            result[...] = low(norm_rows(v_buf[...], vector(5), vector(11)))
-            grad[...] = norm_back(v_buf[...], 5, f32(cotangent[...]))
+            result[...] = low(norm_rows(after_rear[...], vector(5), vector(11)))
+            grad[...] = norm_back(after_rear[...], 5, f32(cotangent[...]))
             branch[...] = low(0.5 * grad[...])
-            fetch(after_conv).start()
-
-        @at(0, 2)
-        def _():
-            for e in range(2):
-                j = step * 2 + e
-                half_back(j, pre_r, REAR_UP, REAR_DOWN)
-
-                @pl.when(j < 3)
-                def _():
-                    load(0, REAR_DOWN + j + 1).start()
-                    load(1, REAR_UP + j + 1).start()
-                    fetch_pre(pre_r, j + 1).start()
+            for j in range(4):
+                down_back(j, REAR_DOWN)
+                load(j % 2, REAR_DOWN + 2 + j if j < 2 else REAR_UP + j - 2).start()
 
         @at(1)
         def _():
-            fetch(after_conv).wait()
-            grad[...] += norm_back(v_buf[...], 4, total[...])
+            for b in range(4):
+                up_back(b, REAR_UP)
+                if b < 2:
+                    load(b, REAR_UP + 2 + b).start()
+            load(0, POINT_OUT).start()
+            grad[...] += norm_back(after_conv[...], 4, total[...])
             conv_branch[...] = low(grad[...])
-            fetch(mixed).start()
-            load(0, POINT_OUT).start()
 
         @at(2)
         def _():
             act_grad = nt(conv_branch[...], weight(0, POINT_OUT))
-            fetch(mixed).wait()
-            act_grad = silu_slope(norm_rows(v_buf[...], vector(3), vector(9)), act_grad)
-            value = low(norm_back(v_buf[...], 3, act_grad))
+            act_grad = silu_slope(norm_rows(mixed[...], vector(3), vector(9)), act_grad)
+            value = low(norm_back(mixed[...], 3, act_grad))
             mixed_w[:, HALO : HALO + frame_count] = value.reshape(rows, frame_count, width)
 
             @pl.when(seq > 0)
@@ -1469,7 +1517,6 @@
             def _():
                 halo_copy(1).start()
 
-            fetch(after_attend).start()
             load(0, POINT_IN).start()
             load(1, POINT_IN + 1).start()
 
@@ -1500,10 +1547,8 @@
             norm_grad = nt(gate_grads[0], weight(0, POINT_IN))
             load(0, ATTEND_OUT).start()
             norm_grad = norm_grad + nt(gate_grads[1], weight(1, POINT_IN + 1))
-            fetch(after_attend).wait()
-            grad[...] += norm_back(v_buf[...], 2, norm_grad)
+            grad[...] += norm_back(after_attend[...], 2, norm_grad)
             attend_branch[...] = low(grad[...])
-            fetch(after_front).start()
             value = low(nt(attend_branch[...], weight(0, ATTEND_OUT)))
             for s in range(8):
                 g_out[s] = value[:, s * 128 : s * 128 + 128].reshape(rows, frame_count, 128)
@@ -1521,8 +1566,11 @@
 
         @at(7, 4)
         def _():
-            attend_back_step((step - 7) * 2)
-            attend_back_step((step - 7) * 2 + 1)
+            def one(i, _):
+                attend_back_step((step - 7) * 2 + i)
+                return 0
+
+            lax.fori_loop(0, 2, one, 0)
 
         @at(12)
         def _():
@@ -1538,24 +1586,38 @@
             norm_grad = nt(parts[0], weight(0, PROJECT))
             load(0, PROJECT + 2).start()
             norm_grad = norm_grad + nt(parts[1], weight(1, PROJECT + 1))
-            load(1, UP).start()
-            fetch_pre(pre_f, 0).start()
+            load(1, DOWN + 1).start()
             norm_grad = norm_grad + nt(parts[2], weight(0, PROJECT + 2))
             load(0, DOWN).start()
-            fetch(after_front).wait()
-            grad[...] += norm_back(v_buf[...], 1, norm_grad)
+            grad[...] += norm_back(after_front[...], 1, norm_grad)
             branch[...] = low(0.5 * grad[...])
 
-        @at(13, 4)
-        def _():
-            j = step - 13
-            half_back(j, pre_f, UP, DOWN)
-
-            @pl.when(j < 3)
+        @at(8)
+        def _():
+            for copy in keep_copies():
+                copy.start()
+
+        @at(13, 2)
+        def _():
+            @pl.when(step == 13)
             def _():
-                load(0, DOWN + j + 1).start()
-                load(1, UP + j + 1).start()
-                fetch_pre(pre_f, j + 1).start()
+                for copy in keep_copies():
+                    copy.wait()
+
+            for i in range(2):
+                j = (step - 13) * 2 + i
+                down_back(j, DOWN)
+                load(i, lax.rem(DOWN + 2 + j, PROJECT)).start()
+
+        @at(15, 2)
+        def _():
+            for i in range(2):
+                b = (step - 15) * 2 + i
+                up_back(b, UP)
+
+                @pl.when(b < 2)
+                def _(b=b, i=i):
+                    load(i, UP + 2 + b).start()
 
         @at(17)
         def _():
@@ -1572,18 +1634,9 @@
         def _():
             finish_vectors()
 
-        @at(0)
-        def _():
-            fetch_hid(hid_r, 0).start()
-
         @at(0, JOB_RU)
         def _():
-            fetch_hid(hid_r, step).wait()
-            stage(hid_buf[...], branch[...])
-
-            @pl.when(step < 3)
-            def _():
-                fetch_hid(hid_r, step + 1).start()
+            stage(hid[step], branch[...])
 
         @at(JOB_RU, 4)
         def _():
@@ -1605,18 +1658,9 @@
         def _():
             stage(norm1[...], parts[step - JOB_P])
 
-        @at(JOB_FD - 1)
-        def _():
-            fetch_hid(hid_f, 0).start()
-
         @at(JOB_FD, 4)
         def _():
-            fetch_hid(hid_f, step - JOB_FD).wait()
-            stage(hid_buf[...], branch[...])
-
-            @pl.when(step < JOB_FD + 3)
-            def _():
-                fetch_hid(hid_f, step - JOB_FD + 1).start()
+            stage(hid[step - JOB_FD], branch[...])
 
         @at(JOB_FU, 4)
         def _():
@@ -1629,96 +1673,138 @@
         return 0
 
     lax.fori_loop(0, JOBS + OUT_LAG, step_work, 0)
-    out_copy(JOBS - 2).wait()
-    out_copy(JOBS - 1).wait()
-
-
-def backward_layer(saved, frames, cotangent, slopes):
+    out_done(JOBS - 2)
+    out_done(JOBS - 1)
+
+
+class Refs:
+    pass
+
+
+def layer(weights, gains, biases, depth, segments, frames, cotangent, slopes):
     bf16, single = jnp.bfloat16, jnp.float32
     tokens, width = frames.shape
+    tall = 128 + 2 * HALO
     dma = pltpu.SemaphoreType.DMA
     vmem, hbm = pl.BlockSpec(memory_space=pltpu.VMEM), pl.BlockSpec(memory_space=pltpu.HBM)
-    kept = (0, 4, 5, 6, 10, 14, 16, 18, 19, 20)
 
     def buf(kind, *sizes):
         return pltpu.VMEM(sizes, kind)
 
-    low_buf, wide_buf = buf(bf16, tokens, width), buf(single, tokens, width)
-    frame_count = 128
-    tall = frame_count + 2 * HALO
+    plain, wide = buf(bf16, tokens, width), buf(single, tokens, width)
+    four = buf(bf16, 4, tokens, width)
+    quarter = (PIECE, width)
+    scratch = dict(
+        vec_all=buf(bf16, 8, VECTORS, 128),
+        seg_all=buf(jnp.int32, 8, 8, 128),
+        norm0=plain,
+        norm1=plain,
+        norm2=plain,
+        norm4=plain,
+        attended=plain,
+        act=plain,
+        pre=four,
+        hid=four,
+        packed=buf(bf16, 8, 3, 2, 128, 128),
+        conv_pre=buf(bf16, 2, tokens, width),
+        gated=buf(bf16, 2, tall, width),
+        mixed=wide,
+        after_front=wide,
+        after_attend=wide,
+        after_conv=wide,
+        after_rear=wide,
+        wbuf=buf(bf16, 3, 8, 128, width),
+        vectors=buf(single, VECTORS, width),
+        pool=buf(bf16, 4 * RING + 8, 128, width),
+        pk_out=buf(bf16, 8, 3, 2, 128, 128),
+        att_out=buf(bf16, 8, 2, 128, 128),
+        att_in=buf(bf16, 8, 2, 128, 128),
+        att_keep=buf(single, 2, 1024, 128),
+        log_sum=buf(single, 2, 2, 1, 1024),
+        logits=buf(single, TILES, TILE, QUERIES),
+        scores=buf(bf16, TILES * TILE, QUERIES),
+        distances=buf(single, 2 * TILES - 1, TILE, TILE),
+        gated_f=buf(single, 2, tall, width),
+        seg_plane=buf(single, 2, tall, 128),
+        seg_cols=buf(single, 2, 1024, 1),
+        seg_rows=buf(single, 8, 1024),
+        vec_wide=buf(single, VECTORS, 128),
+        vec=buf(bf16, VECTORS, 128),
+        seg=buf(jnp.int32, 8, 128),
+        small=buf(single, VECTORS, width),
+        left=plain,
+        right=plain,
+        branch=plain,
+        conv_branch=plain,
+        gate_grads=buf(bf16, 2, tokens, width),
+        attend_branch=plain,
+        parts=buf(bf16, 3, tokens, width),
+        grad=wide,
+        total=wide,
+        mixed_w=buf(bf16, 2, tall, width),
+        mixed_f=buf(single, 2, tall, width),
+        g_in=buf(bf16, 8, 2, 128, 128),
+        p_in=buf(bf16, 8, 3, 2, 128, 128),
+        key_sum=buf(single, 1024, 128),
+        value_sum=buf(single, 1024, 128),
+        slope_sum=buf(single, 2, 8, QUERIES),
+        out_buf=buf(single, 2, 128, width),
+        h_buf=buf(bf16, 4, 2, 2, *quarter),
+        a_buf=buf(bf16, 2, 2, *quarter),
+        b_buf=buf(bf16, 2, 2, *quarter),
+        q_buf=buf(bf16, 4, *quarter),
+        a_in=buf(bf16, RING, 2, 2, *quarter),
+        b_in=buf(bf16, RING, 2, 2, *quarter),
+        a2_in=buf(bf16, RING, 2, *quarter),
+        b2_in=buf(bf16, RING, 2, *quarter),
+        z_in=buf(bf16, RING, 3, *quarter),
+        o_buf=buf(bf16, RING, 4, *quarter),
+        vec_send=buf(single, 8, VECTORS, 128),
+        vec_in=buf(single, 8, VECTORS, 128),
+        vec_dp=buf(single, 4, VECTORS, 128),
+    )
+    forward_sems = [(2, 7, CHUNKS, 3), (4, CHUNKS), (2, 2, 7), (2, 8, 3), (2, 8, 2), (2, 2), (3,), (2,)]
+    backward_sems = [(2, 12, RING), (2, 10), (2,), (2,), (2, 8), (2, 8, 3, 2), (2, 2), (2,)]
+    count = len(forward_sems)
+
+    def kernel(*refs):
+        e = Refs()
+        e.sources = refs[:8]
+        e.gains, e.biases, e.depth, e.segments, e.frames, e.cotangent, e.slopes = refs[8:15]
+        e.result, e.frames_grad, e.vec_out = refs[15:18]
+        e.grads = refs[18:26]
+        e.full, e.pre_keep, e.hid_keep = refs[26:29]
+        for name, ref in zip(scratch, refs[29:]):
+            setattr(e, name, ref)
+        sems = refs[29 + len(scratch) :]
+        e.forward_sems, e.backward_sems = sems[:count], sems[count:]
+        for wide_ref in (e.gated, e.mixed_w):
+            wide_ref[:, :HALO] = jnp.zeros((2, HALO, width), bf16)
+            wide_ref[:, HALO + 128 :] = jnp.zeros((2, HALO, width), bf16)
+        forward_part(e)
+        backward_part(e)
+
+    shape = jax.ShapeDtypeStruct
     return pl.pallas_call(
-        backward_kernel,
-        in_specs=[hbm if i in kept else vmem for i in range(21)]
-        + [vmem, vmem, pl.BlockSpec(memory_space=pltpu.SMEM)],
-        out_specs=[vmem, vmem, hbm, vmem],
+        kernel,
+        in_specs=[hbm] * 8 + [vmem] * 6 + [pl.BlockSpec(memory_space=pltpu.SMEM)],
+        out_specs=[vmem] * 3 + [hbm] * 11,
         out_shape=[
-            jax.ShapeDtypeStruct((tokens, width), bf16),
-            jax.ShapeDtypeStruct((tokens, width), bf16),
-            jax.ShapeDtypeStruct((JOBS, 128, width), single),
-            jax.ShapeDtypeStruct((VECTORS, 128), single),
-        ],
-        scratch_shapes=[
-            buf(bf16, 2, 8, 128, width),
-            low_buf,
-            low_buf,
-            wide_buf,
-            buf(single, VECTORS, width),
-            buf(single, VECTORS, width),
-            low_buf,
-            low_buf,
-            low_buf,
-            buf(bf16, 4, tokens, width),
-            low_buf,
-            buf(bf16, 2, tokens, width),
-            low_buf,
-            buf(bf16, 3, tokens, width),
-            wide_buf,
-            wide_buf,
-            buf(single, 2, tall, width),
-            buf(bf16, 2, tall, width),
-            buf(single, 2, tall, width),
-            buf(single, 2, tall, 128),
-            buf(single, 2, 1024, 1),
-            buf(single, 8, 1024),
-            buf(bf16, 8, 2, 128, 128),
-            buf(bf16, 8, 2, 128, 128),
-            buf(bf16, 8, 3, 2, 128, 128),
-            buf(bf16, 8, 3, 2, 128, 128),
-            buf(single, 1024, 128),
-            buf(single, 1024, 128),
-            buf(single, 8, QUERIES),
-            buf(single, 2, 128, width),
-            buf(bf16, 2, 4, 128, width),
-            buf(bf16, 4, 2, 2, PIECE, width),
-            buf(bf16, 2, 2, PIECE, width),
-            buf(bf16, 2, 2, PIECE, width),
-            buf(bf16, 4, PIECE, width),
-            buf(bf16, RING, 4, 128, width),
-            buf(bf16, RING, 2, 2, PIECE, width),
-            buf(bf16, RING, 2, 2, PIECE, width),
-            buf(bf16, RING, 2, PIECE, width),
-            buf(bf16, RING, 2, PIECE, width),
-            buf(bf16, RING, 3, PIECE, width),
-            buf(bf16, RING, 4, PIECE, width),
-            buf(single, 8, VECTORS, 128),
-            buf(single, 8, VECTORS, 128),
-            buf(single, 4, VECTORS, 128),
-            dma((2, 12, RING)),
-            dma((2, 10)),
-            dma((2,)),
-            dma((1,)),
-            dma((1,)),
-            dma((1,)),
-            dma((2, 8)),
-            dma((2, 8, 3, 2)),
-            dma((2, 2)),
-            dma((2,)),
-        ],
+            shape((tokens, width), bf16),
+            shape((tokens, width), bf16),
+            shape((VECTORS, 128), single),
+        ]
+        + [shape(weight.shape, single) for weight in weights]
+        + [shape((CHUNKS, 8, 128, width), bf16)]
+        + [shape((4, tokens, width), bf16)] * 2,
+        scratch_shapes=list(scratch.values())
+        + [dma(sizes) for sizes in forward_sems + backward_sems]
+        + [pltpu.SemaphoreType.REGULAR],
         compiler_params=pltpu.CompilerParams(
-            collective_id=1, has_side_effects=True, vmem_limit_bytes=62 * 2**20
+            collective_id=0, has_side_effects=True, vmem_limit_bytes=VMEM_LIMIT
         ),
-        name="backward_layer",
-    )(*saved, frames, cotangent, slopes)
+        name="layer",
+    )(*weights, gains, biases, depth, segments, frames, cotangent, slopes)
 
 
 def body_staged(
@@ -1738,60 +1824,42 @@
     rear_up,
     rear_down,
 ):
-    row_count, frame_count, width = frames.shape
-    token_count = row_count * frame_count
-    seq = lax.axis_index("seq")
+    width = frames.shape[2]
+    token_count = frames.shape[0] * frames.shape[1]
     taps = depthwise.shape[0]
 
-    def wide(shard):
-        return shard.reshape(128, -1, width).transpose(1, 0, 2)
-
-    def dealt(shard):
-        return shard.reshape(128, 8, 4, 128).transpose(2, 0, 1, 3).reshape(4, 128, width)
-
-    shards = jnp.concatenate(
-        [
-            dealt(front_up),
-            front_down.reshape(4, 128, width),
-            wide(attend_in),
-            wide(attend_out),
-            wide(point_in),
-            wide(point_out),
-            dealt(rear_up),
-            rear_down.reshape(4, 128, width),
-        ]
-    )
-    vector_shard = jnp.concatenate([norm_gains, norm_biases, depthwise])
-    vector_shard = jnp.pad(vector_shard, ((0, VECTORS - vector_shard.shape[0]), (0, 0)))
-    segment_shard = jnp.pad(segments, ((0, 8 - row_count), (0, 0)))
-    my_slopes = lax.dynamic_slice_in_dim(slopes, seq * 2, 2, 0)
+    weights = (
+        front_up,
+        front_down,
+        attend_in,
+        attend_out,
+        point_in,
+        point_out,
+        rear_up,
+        rear_down,
+    )
     tokens = frames.reshape(token_count, width)
-    saved = forward_layer(shards, vector_shard, segment_shard, tokens, my_slopes)
-    result, frames_grad, shares, vectors = backward_layer(
-        saved, tokens, cotangent.reshape(token_count, width), my_slopes
-    )
-
-    def beside(first, count):
-        return jnp.concatenate([shares[first + i] for i in range(count)], axis=1)
-
-    def below(first):
-        return shares[first : first + 4].reshape(-1, width)
-
+    result, frames_grad, vectors, *grads = layer(
+        weights,
+        norm_gains,
+        norm_biases,
+        depthwise,
+        segments,
+        tokens,
+        cotangent.reshape(token_count, width),
+        slopes,
+    )
+    grads = grads[:8]
     return (
         result.reshape(frames.shape),
         frames_grad.reshape(frames.shape),
         vectors[:6],
         vectors[6:12],
-        beside(JOB_FU, 4),
-        below(JOB_FD),
-        beside(JOB_P, 3),
-        shares[JOB_AO],
+        *grads[:4],
         vectors[12 + taps, : slopes.shape[0]],
-        beside(JOB_PI, 2),
+        grads[4],
         vectors[12 : 12 + taps],
-        shares[JOB_PO],
-        beside(JOB_RU, 4),
-        below(0),
+        *grads[5:],
     )
 
 

time: 584 us -> 549 us (0.940); the launches traced: 580 us -> 539 us
  Pallas kernels: 540 us -> 518 us
  local copies, waits for them, and re-layouts: 33.2 us -> 19.9 us
  other arithmetic: 5.91 us -> 0 us
    pallas_call x2 -> x1, Pallas kernels: 540 us -> 518 us  [layer(): pl.pallas_call(kernel, in_specs=[hbm] * 8 + [vmem] * 6 + [pl.BlockSpec(me...]
    concatenate x4 -> x0, other arithmetic: 5.91 us -> none  [the longest x3 4.58 us: beside(): return jnp.concatenate([shares[first + i] for i in range(count)], axis=1)]
    unnamed x33 -> x26, local copies, waits for them, and re-layouts: 10.8 us -> 15.9 us
where the time goes in v3:
time: 549 us; the launch traced here: 539 us
  Pallas kernels  518 us (94%)
  local copies, waits for them, and re-layouts  19.9 us (4%)
    pallas_call x1, Pallas kernels, layer(): pl.pallas_call(kernel, in_specs=[hbm] * 8 + [vmem] * 6 + [pl.BlockSpec(me...  518 us
    unnamed x26, local copies, waits for them, and re-layouts  15.9 us

profile of v3, /device:TPU:0, one launch (start us, length us, event | category | flops | bytes accessed | tf_op | source)
XLA Modules:
  0.0 539.3 jit_solution(10055155230544300900)
XLA Ops:
  0.7 518.4 %layer.1 = (bf16[256,1024]{1,0:T(8,128)(2,1)}, bf16[256,1024]{1,0:T(8,128)(2,1)}, f32[48,128]{1,0:T(8,128)}, f32[128,4096]{1,0:T(8,128)}, f32[512,1024]{1,0:T(8,...) custom-call(bf16[128,4096]{1,0:T(8,128)(2,1)} %refs_0_.1, ...), custom_call_target="tpu_custom_call" | custom-call | tf_op jit(solution)/shard_map/layer/pallas_call | solution.py:1788
  519.0 0.0 copy-start.3
  519.1 1.3 slice_bitcast_fusion
  520.4 1.4 fusion
  521.7 1.3 slice.15
  523.1 1.9 copy.39
  525.0 1.9 copy.40
  526.8 0.0 copy-done.3
  526.8 0.0 copy-start.2
  526.8 1.3 copy.41
  528.1 1.0 copy-done.2
  529.2 0.0 copy-start.4
  529.2 1.3 copy.42
  530.5 0.8 copy-done.4
  531.3 0.0 copy-start.7
  531.3 0.0 copy-start.5
  531.3 1.1 copy.43
  532.5 0.2 copy-done.7
  532.7 0.0 copy-start.6
  532.7 0.0 copy-start.1
  532.7 0.8 copy.44
  533.5 0.0 copy-done.5
  533.5 1.0 copy.45
  534.5 0.0 copy-done.6
  534.5 0.8 copy.46
  535.3 0.0 copy-done.1
  535.3 0.0 copy-start
  535.3 1.3 copy.47
  536.6 1.0 copy-done
  537.6 1.3 copy.48
Async XLA Ops:
  519.0 7.8 %copy-start.3 = (f32[128,4096]{1,0:T(8,128)S(1)}, f32[128,4096]{1,0:T(8,128)}, u32[]{:S(2)}) copy-start(f32[128,4096]{1,0:T(8,128)} %get-tuple-element.56) | copy-start | bytes 6291460
  526.8 2.3 copy-start.2
  529.2 2.2 copy-start.4
  531.3 1.4 copy-start.7
  531.3 2.2 copy-start.5
  532.7 1.8 copy-start.6
  532.7 2.6 copy-start.1
  535.3 2.3 copy-start

commit v4 on v3

--- a/solution.py
+++ b/solution.py
@@ -479,7 +479,7 @@
 UP, DOWN, PROJECT, ATTEND_OUT, POINT_IN, POINT_OUT, REAR_UP, REAR_DOWN = 0, 4, 8, 11, 12, 14, 15, 19
 CHUNKS = 23
 TALL = (False, True, False, False, False, False, False, True)
-LEAD = 12
+LEAD = 3
 VMEM_LIMIT = 63 * 2**20
 STAGE = 1
 STEP = 4 * STAGE
@@ -615,6 +615,9 @@
     def read_done(t):
         pltpu.make_async_copy(shards.at[t], shards.at[t], own_sem.at[3, t]).wait()
 
+    barrier = pltpu.get_barrier_semaphore()
+    for there in [(dp, peer(k)) for k in range(1, 8)] + [(lax.rem(dp + k, 4), seq) for k in (1, 2, 3)]:
+        pl.semaphore_signal(barrier, inc=1, device_id=there, device_id_type=MESH_ID)
     for t in range(CHUNKS):
         read(t).start()
     vec_wide[...] = jnp.zeros_like(vec_wide)
@@ -625,9 +628,6 @@
     seg[...] = jnp.zeros_like(seg)
     seg[0:rows, :] = segments[...]
 
-    barrier = pltpu.get_barrier_semaphore()
-    for there in [(dp, peer(k)) for k in range(1, 8)] + [(lax.rem(dp + k, 4), seq) for k in (1, 2, 3)]:
-        pl.semaphore_signal(barrier, inc=1, device_id=there, device_id_type=MESH_ID)
     pl.semaphore_wait(barrier, 10)
 
     q_own, q_x, q_y = PIECE * dp, PIECE * (y * 2 + 1 - x), PIECE * ((1 - y) * 2 + x)
@@ -726,9 +726,12 @@
         start_line(t)
 
     def gather_step(step):
-        @pl.when(step + LEAD < CHUNKS)
-        def _():
-            start_line(step + LEAD)
+        for i in range(2):
+            ahead = LEAD + 2 * step + i
+
+            @pl.when(ahead < CHUNKS)
+            def _(ahead=ahead):
+                start_line(ahead)
 
         @pl.when(step < CHUNKS)
         def _():
@@ -962,21 +965,22 @@
 
             project(now - 1, now - 9)
 
-        @at(13)
+        @at(14)
         def _():
             for c in range(3):
                 for k in range(1, 8):
                     pk_copy(c, k, True).wait_recv()
 
-        @at(13, 4)
+        @at(14, 3)
         def _():
             def one(i, _):
-                attend_step((now - 13) * 2 + i)
+                attend_step(i)
                 return 0
 
-            lax.fori_loop(0, 2, one, 0)
-
-        @at(17)
+            first = (now - 14) * 3
+            lax.fori_loop(first, lax.min(first + 3, 8), one, 0)
+
+        @at(18)
         def _():
             for r in range(rows):
                 for k in range(1, 8):
@@ -984,6 +988,7 @@
             for s in range(8):
                 attended[:, s * 128 : s * 128 + 128] = att_in[s].reshape(rows * frame_count, 128)
             after_attend[...] = after_front[...] + dot(attended[...], weight(ATTEND_OUT))
+            load(14).start()
             norm2[...] = norm(after_attend[...], 2)
 
         @at(18)
@@ -1032,7 +1037,7 @@
         def _():
             load(now).start()
 
-        for when, chunks in ((17, (14,)), (18, (15, 16)), (19, (17,)), (20, (18, 19)), (21, (20, 21)), (22, (22,))):
+        for when, chunks in ((18, (15, 16)), (19, (17,)), (20, (18, 19)), (21, (20, 21)), (22, (22,))):
 
             @at(when)
             def _(chunks=chunks):
@@ -1070,7 +1075,7 @@
 
 
 JOB_RU, JOB_PO, JOB_PI, JOB_AO, JOB_P, JOB_FD, JOB_FU, JOBS = 4, 8, 9, 11, 12, 15, 19, 23
-RING = 4
+RING, SHARES = 4, 5
 GRADS = ((7, True), (6, False), (5, False), (4, False), (3, False), (2, False), (1, True), (0, False))
 OUT_LAG = 6
 
@@ -1103,7 +1108,7 @@
     frames, cotangent, slopes = e.frames, e.cotangent, e.slopes
     result, frames_grad, vec_out, grads = e.result, e.frames_grad, e.vec_out, e.grads
     pre_grads, hid, wbuf, vectors, pool = e.pre, e.hid, e.wbuf, e.vectors, e.pool
-    small, left, right, branch, conv_branch = e.small, e.left, e.right, e.branch, e.conv_branch
+    small, right, branch, conv_branch = e.small, e.right, e.branch, e.conv_branch
     gate_grads, attend_branch, parts = e.gate_grads, e.attend_branch, e.parts
     grad, total, gated_f, mixed_w, mixed_f = e.grad, e.total, e.gated_f, e.mixed_w, e.mixed_f
     seg_plane, seg_rows = e.seg_plane, e.seg_rows
@@ -1136,6 +1141,9 @@
             src, dst, sem.at[0, slot, lax.rem(t, RING)], sem.at[1, slot, lax.rem(t, RING)], there
         )
 
+    def turn(t):
+        return lax.rem(t, 2)
+
     def core_copies(t, r):
         return [
             remote(pool.at[pl.ds(mine + 4, 4)], pool.at[pl.ds(4 * r, 4)], t, 0, over_core)
@@ -1143,30 +1151,30 @@
 
     def first_copies(t, r):
         return [
-            remote(h_buf.at[pl.ds(0, 2), :, 1 - x], a_in.at[r], t, 1, over_x),
-            remote(h_buf.at[pl.ds(2, 2), 1 - y], b_in.at[r], t, 2, over_y),
+            remote(h_buf.at[turn(t), pl.ds(0, 2), :, 1 - x], a_in.at[r], t, 1, over_x),
+            remote(h_buf.at[turn(t), pl.ds(2, 2), 1 - y], b_in.at[r], t, 2, over_y),
         ]
 
     def second_copies(t, r):
         return [
-            remote(a_buf.at[:, 1 - y], a2_in.at[r], t, 3, over_y),
-            remote(b_buf.at[:, 1 - x], b2_in.at[r], t, 4, over_x),
+            remote(a_buf.at[turn(t), :, 1 - y], a2_in.at[r], t, 3, over_y),
+            remote(b_buf.at[turn(t), :, 1 - x], b2_in.at[r], t, 4, over_x),
         ]
 
     def line_copies(t, r):
         copies = []
         for k in (1, 2, 3):
             to = lax.rem(z + k, 4)
-            copies.append(remote(q_buf.at[to], z_in.at[r, k - 1], t, 4 + k, (dp, to * 2 + core)))
+            copies.append(remote(q_buf.at[turn(t), to], z_in.at[r, k - 1], t, 4 + k, (dp, to * 2 + core)))
         return copies
 
     def share_copies(t, r):
-        where = o_buf.at[r, dp]
+        where = o_buf.at[lax.rem(t, SHARES), dp]
         return [remote(where, where, t, 8, over_x), remote(where, where, t, 9, over_y)]
 
     def across_copies(t, r):
-        one = o_buf.at[r, (1 - y) * 2 + x, pl.ds(0, PIECE // 2)]
-        two = o_buf.at[r, y * 2 + 1 - x, pl.ds(PIECE // 2, PIECE // 2)]
+        one = o_buf.at[lax.rem(t, SHARES), (1 - y) * 2 + x, pl.ds(0, PIECE // 2)]
+        two = o_buf.at[lax.rem(t, SHARES), y * 2 + 1 - x, pl.ds(PIECE // 2, PIECE // 2)]
         return [remote(one, one, t, 10, over_x), remote(two, two, t, 11, over_y)]
 
     def out_start(t):
@@ -1204,7 +1212,7 @@
         def _():
             out_done(t - 2)
 
-        out_buf[lax.rem(t, 2)] = f32(o_buf[r].reshape(128, width))
+        out_buf[lax.rem(t, 2)] = f32(o_buf[lax.rem(t, SHARES)].reshape(128, width))
         out_start(t)
 
     def pass_on(t, r):
@@ -1213,39 +1221,39 @@
 
     def total_line(t, r):
         finish(line_copies(t, r))
-        value = f32(q_buf[z]) + f32(z_in[r, 0]) + f32(z_in[r, 1]) + f32(z_in[r, 2])
-        o_buf[r, dp] = low(value)
+        value = f32(q_buf[turn(t), z]) + f32(z_in[r, 0]) + f32(z_in[r, 1]) + f32(z_in[r, 2])
+        o_buf[lax.rem(t, SHARES), dp] = low(value)
         begin(share_copies(t, r))
 
     def total_second(t, r):
         finish(second_copies(t, r))
-        q_buf[0:2] = low(f32(a_buf[:, y]) + f32(a2_in[r]))
-        q_buf[2:4] = low(f32(b_buf[:, x]) + f32(b2_in[r]))
+        q_buf[turn(t), 0:2] = low(f32(a_buf[turn(t), :, y]) + f32(a2_in[r]))
+        q_buf[turn(t), 2:4] = low(f32(b_buf[turn(t), :, x]) + f32(b2_in[r]))
         begin(line_copies(t, r))
 
     def total_first(t, r):
         finish(first_copies(t, r))
-        a_buf[...] = low(f32(h_buf[0:2, :, x]) + f32(a_in[r]))
-        b_buf[...] = low(f32(h_buf[2:4, y]) + f32(b_in[r]))
+        a_buf[turn(t)] = low(f32(h_buf[turn(t), 0:2, :, x]) + f32(a_in[r]))
+        b_buf[turn(t)] = low(f32(h_buf[turn(t), 2:4, y]) + f32(b_in[r]))
         begin(second_copies(t, r))
 
     def total_core(t, r):
         finish(core_copies(t, r))
         for i in range(4):
             value = low(f32(pool[mine + i]) + f32(pool[4 * r + i]))
-            h_buf[i] = value.reshape(2, 2, PIECE, width)
+            h_buf[turn(t), i] = value.reshape(2, 2, PIECE, width)
         begin(first_copies(t, r))
 
-    def product(t, r):
+    def product(t, left, right):
         for i in range(8):
             part = tn(left[:, 128 * i : 128 * i + 128], right[...])
             pool[mine + 4 * lax.rem(core + i, 2) + i // 2] = low(part)
-        begin(core_copies(t, r))
+        begin(core_copies(t, lax.rem(t, RING)))
 
     sums = [total_core, total_first, total_second, total_line, pass_on, write_out]
 
     def sum_step(step):
-        for depth in reversed(range(1, 7)):
+        for depth in range(1, 7):
             t = step - depth
 
             @pl.when((t >= 0) & (t < JOBS))
@@ -1470,10 +1478,6 @@
         finish(vec_dp_copies())
         vec_out[...] = (vec_dp[0] + vec_dp[1]) + (vec_dp[2] + vec_dp[3])
 
-    def stage(first, second):
-        left[...] = first
-        right[...] = second
-
     def step_work(step, _):
         sum_step(step)
 
@@ -1488,6 +1492,53 @@
             result[...] = low(norm_rows(after_rear[...], vector(5), vector(11)))
             grad[...] = norm_back(after_rear[...], 5, f32(cotangent[...]))
             branch[...] = low(0.5 * grad[...])
+
+        @at(12, 3)
+        def _():
+            c = step - 12
+            for r in range(rows):
+                for k in range(1, 8):
+                    pk_copy(peer(k), c, r, True).wait_recv()
+                    pk_copy(peer(k), c, r).wait_send()
+            for s in range(8):
+                parts[c, :, s * 128 : s * 128 + 128] = p_in[s, c].reshape(rows * frame_count, 128)
+
+        @at(0, JOB_RU)
+        def _():
+            product(step, hid.at[step], branch)
+
+        @at(JOB_RU, 4)
+        def _():
+            right[...] = strided(step - JOB_RU)
+            product(step, norm4, right)
+
+        @at(JOB_PO)
+        def _():
+            product(step, act, conv_branch)
+
+        @at(JOB_PI, 2)
+        def _():
+            product(step, norm2, gate_grads.at[step - JOB_PI])
+
+        @at(JOB_AO)
+        def _():
+            product(step, attended, attend_branch)
+
+        @at(JOB_P, 3)
+        def _():
+            product(step, norm1, parts.at[step - JOB_P])
+
+        @at(JOB_FD, 4)
+        def _():
+            product(step, hid.at[step - JOB_FD], branch)
+
+        @at(JOB_FU, 4)
+        def _():
+            right[...] = strided(step - JOB_FU)
+            product(step, norm0, right)
+
+        @at(0)
+        def _():
             for j in range(4):
                 down_back(j, REAR_DOWN)
                 load(j % 2, REAR_DOWN + 2 + j if j < 2 else REAR_UP + j - 2).start()
@@ -1574,20 +1625,19 @@
 
         @at(12)
         def _():
-            for c in range(3):
-                for r in range(rows):
-                    for k in range(1, 8):
-                        pk_copy(peer(k), c, r, True).wait_recv()
-                        pk_copy(peer(k), c, r).wait_send()
-                for s in range(8):
-                    parts[c, :, s * 128 : s * 128 + 128] = p_in[s, c].reshape(
-                        rows * frame_count, 128
-                    )
-            norm_grad = nt(parts[0], weight(0, PROJECT))
+            total[...] = nt(parts[0], weight(0, PROJECT))
             load(0, PROJECT + 2).start()
-            norm_grad = norm_grad + nt(parts[1], weight(1, PROJECT + 1))
+
+        @at(13)
+        def _():
+            total[...] += nt(parts[1], weight(1, PROJECT + 1))
             load(1, DOWN + 1).start()
-            norm_grad = norm_grad + nt(parts[2], weight(0, PROJECT + 2))
+
+        @at(14)
+        def _():
+            for copy in keep_copies():
+                copy.wait()
+            norm_grad = total[...] + nt(parts[2], weight(0, PROJECT + 2))
             load(0, DOWN).start()
             grad[...] += norm_back(after_front[...], 1, norm_grad)
             branch[...] = low(0.5 * grad[...])
@@ -1597,78 +1647,37 @@
             for copy in keep_copies():
                 copy.start()
 
-        @at(13, 2)
-        def _():
-            @pl.when(step == 13)
-            def _():
-                for copy in keep_copies():
-                    copy.wait()
-
+        @at(15, 2)
+        def _():
             for i in range(2):
-                j = (step - 13) * 2 + i
+                j = (step - 15) * 2 + i
                 down_back(j, DOWN)
                 load(i, lax.rem(DOWN + 2 + j, PROJECT)).start()
 
-        @at(15, 2)
+        @at(17, 2)
         def _():
             for i in range(2):
-                b = (step - 15) * 2 + i
+                b = (step - 17) * 2 + i
                 up_back(b, UP)
 
                 @pl.when(b < 2)
                 def _(b=b, i=i):
                     load(i, UP + 2 + b).start()
 
-        @at(17)
+        @at(19)
         def _():
             frames_grad[...] = low(
                 grad[...] + norm_back(f32(frames[...]), 0, total[...])
             )
             send_vectors()
 
-        @at(19)
+        @at(22)
         def _():
             sum_vectors()
 
-        @at(21)
+        @at(24)
         def _():
             finish_vectors()
-
-        @at(0, JOB_RU)
-        def _():
-            stage(hid[step], branch[...])
-
-        @at(JOB_RU, 4)
-        def _():
-            stage(norm4[...], strided(step - JOB_RU))
-
-        @at(JOB_PO)
-        def _():
-            stage(act[...], conv_branch[...])
-
-        @at(JOB_PI, 2)
-        def _():
-            stage(norm2[...], gate_grads[step - JOB_PI])
-
-        @at(JOB_AO)
-        def _():
-            stage(attended[...], attend_branch[...])
-
-        @at(JOB_P, 3)
-        def _():
-            stage(norm1[...], parts[step - JOB_P])
-
-        @at(JOB_FD, 4)
-        def _():
-            stage(hid[step - JOB_FD], branch[...])
-
-        @at(JOB_FU, 4)
-        def _():
-            stage(norm0[...], strided(step - JOB_FU))
-
-        @at(0, JOBS)
-        def _():
-            product(step, lax.rem(step, RING))
 
         return 0
 
@@ -1732,7 +1741,6 @@
         vec=buf(bf16, VECTORS, 128),
         seg=buf(jnp.int32, 8, 128),
         small=buf(single, VECTORS, width),
-        left=plain,
         right=plain,
         branch=plain,
         conv_branch=plain,
@@ -1749,16 +1757,16 @@
         value_sum=buf(single, 1024, 128),
         slope_sum=buf(single, 2, 8, QUERIES),
         out_buf=buf(single, 2, 128, width),
-        h_buf=buf(bf16, 4, 2, 2, *quarter),
-        a_buf=buf(bf16, 2, 2, *quarter),
-        b_buf=buf(bf16, 2, 2, *quarter),
-        q_buf=buf(bf16, 4, *quarter),
+        h_buf=buf(bf16, 2, 4, 2, 2, *quarter),
+        a_buf=buf(bf16, 2, 2, 2, *quarter),
+        b_buf=buf(bf16, 2, 2, 2, *quarter),
+        q_buf=buf(bf16, 2, 4, *quarter),
         a_in=buf(bf16, RING, 2, 2, *quarter),
         b_in=buf(bf16, RING, 2, 2, *quarter),
         a2_in=buf(bf16, RING, 2, *quarter),
         b2_in=buf(bf16, RING, 2, *quarter),
         z_in=buf(bf16, RING, 3, *quarter),
-        o_buf=buf(bf16, RING, 4, *quarter),
+        o_buf=buf(bf16, SHARES, 4, *quarter),
         vec_send=buf(single, 8, VECTORS, 128),
         vec_in=buf(single, 8, VECTORS, 128),
         vec_dp=buf(single, 4, VECTORS, 128),
@@ -1807,6 +1815,59 @@
     )(*weights, gains, biases, depth, segments, frames, cotangent, slopes)
 
 
+def copy_kernel(*refs):
+    count = 10
+    sources, vec, targets = refs[:count], refs[count], refs[count + 1 : 2 * count + 1]
+    gains, biases, depth, slopes = refs[2 * count + 1 : 2 * count + 5]
+    buffers = refs[2 * count + 5 : 3 * count + 5]
+    read_sem, write_sem = refs[3 * count + 5 :]
+    jobs = []
+    for i in range(count):
+        rows = sources[i].shape[0]
+        height = rows // 4
+        for part in range(4):
+            at = pl.ds(part * height, height)
+            jobs.append((i, at, 4 * i + part))
+
+    def read(job):
+        i, at, n = job
+        return pltpu.make_async_copy(sources[i].at[at], buffers[i].at[at], read_sem.at[n])
+
+    def write(job):
+        i, at, n = job
+        return pltpu.make_async_copy(buffers[i].at[at], targets[i].at[at], write_sem.at[n])
+
+    for job in jobs:
+        read(job).start()
+    gains[...] = vec[0:6, :]
+    biases[...] = vec[6:12, :]
+    depth[...] = vec[12:43, :]
+    slopes[...] = vec[43:44, :]
+    for job in jobs:
+        read(job).wait()
+        write(job).start()
+    for job in jobs:
+        write(job).wait()
+
+
+def copy_out(arrays, vec):
+    shape = jax.ShapeDtypeStruct
+    vmem, hbm = pl.BlockSpec(memory_space=pltpu.VMEM), pl.BlockSpec(memory_space=pltpu.HBM)
+    size = sum(array.size * array.dtype.itemsize for array in arrays)
+    return pl.pallas_call(
+        copy_kernel,
+        in_specs=[hbm] * len(arrays) + [vmem],
+        out_specs=[hbm] * len(arrays) + [vmem] * 4,
+        out_shape=[shape(array.shape, array.dtype) for array in arrays]
+        + [shape((height, 128), jnp.float32) for height in (6, 6, 31, 1)],
+        scratch_shapes=[pltpu.VMEM(array.shape, array.dtype) for array in arrays]
+        + [pltpu.SemaphoreType.DMA((4 * len(arrays),))] * 2,
+        compiler_params=pltpu.CompilerParams(vmem_limit_bytes=VMEM_LIMIT),
+        cost_estimate=pl.CostEstimate(flops=0, bytes_accessed=2 * size, transcendentals=0),
+        name="copy_out",
+    )(*arrays, vec)
+
+
 def body_staged(
     frames,
     segments,
@@ -1826,7 +1887,6 @@
 ):
     width = frames.shape[2]
     token_count = frames.shape[0] * frames.shape[1]
-    taps = depthwise.shape[0]
 
     weights = (
         front_up,
@@ -1849,16 +1909,19 @@
         cotangent.reshape(token_count, width),
         slopes,
     )
-    grads = grads[:8]
+    *arrays, gains_grad, biases_grad, depth_grad, slopes_grad = copy_out(
+        [result, frames_grad, *grads[:8]], vectors
+    )
+    result, frames_grad, *grads = arrays
     return (
         result.reshape(frames.shape),
         frames_grad.reshape(frames.shape),
-        vectors[:6],
-        vectors[6:12],
+        gains_grad,
+        biases_grad,
         *grads[:4],
-        vectors[12 + taps, : slopes.shape[0]],
+        slopes_grad[0, : slopes.shape[0]],
         grads[4],
-        vectors[12 : 12 + taps],
+        depth_grad,
         *grads[5:],
     )
 

time: 549 us -> 528 us (0.962)
  local copies, waits for them, and re-layouts: 19.9 us -> 1.08 us
    unnamed x26 -> x0, local copies, waits for them, and re-layouts: 15.9 us -> none
    pallas_call x1, Pallas kernels: 518 us -> 504 us  [layer(): pl.pallas_call(kernel, in_specs=[hbm] * 8 + [vmem] * 6 + [pl.BlockSpec(me...]
    pallas_call x0 -> x1, Pallas kernels: none -> 11.6 us  [copy_out(): pl.pallas_call(copy_kernel, in_specs=[hbm] * len(arrays) + [vmem], out_sp...]
where the time goes in v4:
time: 528 us; the launch traced here: 518 us
  Pallas kernels  516 us (98%)
    pallas_call x1, Pallas kernels, layer(): pl.pallas_call(kernel, in_specs=[hbm] * 8 + [vmem] * 6 + [pl.BlockSpec(me...  504 us
    pallas_call x1, Pallas kernels, copy_out(): pl.pallas_call(copy_kernel, in_specs=[hbm] * len(arrays) + [vmem], out_sp...  11.6 us

profile of v4, /device:TPU:0, one launch (start us, length us, event | category | flops | bytes accessed | tf_op | source)
XLA Modules:
  0.0 518.2 jit_solution(16707866090235327276)
XLA Ops:
  0.7 504.5 %layer.1 = (bf16[256,1024]{1,0:T(8,128)(2,1)}, bf16[256,1024]{1,0:T(8,128)(2,1)}, f32[48,128]{1,0:T(8,128)}, f32[128,4096]{1,0:T(8,128)}, f32[512,1024]{1,0:T(8,...) custom-call(bf16[128,4096]{1,0:T(8,128)(2,1)} %refs_0_.1, ...), custom_call_target="tpu_custom_call" | custom-call | tf_op jit(solution)/shard_map/layer/pallas_call | solution.py:1796
  505.1 11.6 %copy_out.1 = (bf16[256,1024]{1,0:T(8,128)(2,1)}, bf16[256,1024]{1,0:T(8,128)(2,1)}, f32[128,4096]{1,0:T(8,128)}, f32[512,1024]{1,0:T(8,128)}, f32[128,3072]{1,0...) custom-call(bf16[256,1024]{1,0:T(8,128)(2,1)} %get-tuple-element.39., ...), custom_call_target="tpu_custom_call" | custom-call | bytes 26214400 | tf_op jit(solution)/shard_map/copy_out/pallas_call | solution.py:1857
  516.8 1.1 slice_bitcast_fusion

commit v5 on v4

--- a/solution.py
+++ b/solution.py
@@ -1048,6 +1048,11 @@
 
     lax.fori_loop(0, STEP + 24, step_work, 0)
 
+    for i in range(2):
+        pltpu.make_async_copy(
+            full.at[REAR_DOWN + i], wbuf.at[i], e.backward_sems[2].at[i]
+        ).start()
+
     def drain(t, _):
         for kind in (to_x, to_y, on_x, on_y, to_core):
             for k in (1, 2, 3):
@@ -1227,20 +1232,20 @@
 
     def total_second(t, r):
         finish(second_copies(t, r))
-        q_buf[turn(t), 0:2] = low(f32(a_buf[turn(t), :, y]) + f32(a2_in[r]))
-        q_buf[turn(t), 2:4] = low(f32(b_buf[turn(t), :, x]) + f32(b2_in[r]))
+        q_buf[turn(t), 0:2] = a_buf[turn(t), :, y] + a2_in[r]
+        q_buf[turn(t), 2:4] = b_buf[turn(t), :, x] + b2_in[r]
         begin(line_copies(t, r))
 
     def total_first(t, r):
         finish(first_copies(t, r))
-        a_buf[turn(t)] = low(f32(h_buf[turn(t), 0:2, :, x]) + f32(a_in[r]))
-        b_buf[turn(t)] = low(f32(h_buf[turn(t), 2:4, y]) + f32(b_in[r]))
+        a_buf[turn(t)] = h_buf[turn(t), 0:2, :, x] + a_in[r]
+        b_buf[turn(t)] = h_buf[turn(t), 2:4, y] + b_in[r]
         begin(second_copies(t, r))
 
     def total_core(t, r):
         finish(core_copies(t, r))
         for i in range(4):
-            value = low(f32(pool[mine + i]) + f32(pool[4 * r + i]))
+            value = pool[mine + i] + pool[4 * r + i]
             h_buf[turn(t), i] = value.reshape(2, 2, PIECE, width)
         begin(first_copies(t, r))
 
@@ -1486,8 +1491,6 @@
 
         @at(0)
         def _():
-            load(0, REAR_DOWN).start()
-            load(1, REAR_DOWN + 1).start()
             prepare()
             result[...] = low(norm_rows(after_rear[...], vector(5), vector(11)))
             grad[...] = norm_back(after_rear[...], 5, f32(cotangent[...]))

time: 528 us -> 528 us (level)
  no operation moved by 1% of the time
where the time goes in v5:
time: 528 us; the launch traced here: 518 us
  Pallas kernels  516 us (98%)
    pallas_call x1, Pallas kernels, layer(): pl.pallas_call(kernel, in_specs=[hbm] * 8 + [vmem] * 6 + [pl.BlockSpec(me...  504 us
    pallas_call x1, Pallas kernels, copy_out(): pl.pallas_call(copy_kernel, in_specs=[hbm] * len(arrays) + [vmem], out_sp...  11.6 us

profile of v5, /device:TPU:0, one launch (start us, length us, event | category | flops | bytes accessed | tf_op | source)
XLA Modules:
  0.0 518.1 jit_solution(6581749946874016335)
XLA Ops:
  0.7 504.3 %layer.1 = (bf16[256,1024]{1,0:T(8,128)(2,1)}, bf16[256,1024]{1,0:T(8,128)(2,1)}, f32[48,128]{1,0:T(8,128)}, f32[128,4096]{1,0:T(8,128)}, f32[512,1024]{1,0:T(8,...) custom-call(bf16[128,4096]{1,0:T(8,128)(2,1)} %refs_0_.1, ...), custom_call_target="tpu_custom_call" | custom-call | tf_op jit(solution)/shard_map/layer/pallas_call | solution.py:1799
  505.0 11.6 %copy_out.1 = (bf16[256,1024]{1,0:T(8,128)(2,1)}, bf16[256,1024]{1,0:T(8,128)(2,1)}, f32[128,4096]{1,0:T(8,128)}, f32[512,1024]{1,0:T(8,128)}, f32[128,3072]{1,0...) custom-call(bf16[256,1024]{1,0:T(8,128)(2,1)} %get-tuple-element.39., ...), custom_call_target="tpu_custom_call" | custom-call | bytes 26214400 | tf_op jit(solution)/shard_map/copy_out/pallas_call | solution.py:1860
  516.6 1.1 slice_bitcast_fusion
